TPU v7x, 256 devices: a whole 4x4x8 slice. The times are simulated.
256 devices in a mesh: dom: 64 (over x, z, core), col: 4 (over y).
Axes of the slice: x: 4, y: 4, z: 8, core: 2. Of those that a mesh axis runs over, the one named last changes fastest.
Arguments:
- embeddings: float32 [262144, 512], P('dom', 'col'), may hold values from -1.3 to 1.3
- adagrad_state: float32 [262144], P('dom'), may hold values from 1e-05 to 0.01
- relations: float32 [1345, 512], P(None, 'col'), may hold values from 0.1 to 1.9
- src_rows: int32 [262144], P('dom'), may hold values from 0 to 4095
- dst_rows: int32 [262144], P('dom'), may hold values from 0 to 4095
- rel_ids: int32 [262144], P('dom'), may hold values from 0 to 1344
- bucket_counts: int32 [64, 64], P('dom'), may hold values from 1 to 64, as said below
- neg_rows: int32 [64000], P('dom'), may hold values from 0 to 4095
Outputs:
- new_embeddings: float32 [262144, 512], P('dom', 'col')
- new_state: float32 [262144], P('dom')
Inputs may be any that keep to these rules, and one draw needn't show every extreme that they name: `bucket_counts`: edge slot j of a partition lies in the bucket of destination partition j // 64; in every draw some destination partition has all 64 slots live from every source partition.
All inputs are finite; a program needn't handle non-finite values.
Results may differ from a plain program's by a relative error of at most 0.0025.
Values may be sent and summed in bfloat16 or wider, within the bound.
No kernel may reach another device: no remote copies, remote signals or barrier semaphores. Data moves between devices by JAX's collectives and lax.ppermute only.
A program may use at most 128 MiB of HBM per device.

v0:
```python
import jax
import jax.numpy as jnp
from jax import lax
from jax.sharding import PartitionSpec as P

learning_rate = 0.3


def shards(
    embeddings, adagrad_state, relations, src_rows, dst_rows, rel_ids, bucket_counts, neg_rows
):
    owners = lax.axis_size("dom")
    slot_total = src_rows.shape[0]
    per_owner = slot_total // owners
    col_width = embeddings.shape[1]
    full_width = col_width * lax.axis_size("col")
    negatives = neg_rows.shape[0]
    counts = bucket_counts[0]
    live_mask = (
        (lax.broadcasted_iota(jnp.int32, (owners, per_owner), 1) < counts[:, None])
        .astype(jnp.float32)
        .reshape(slot_total)
    )
    requests = dst_rows.reshape(owners, per_owner)
    wanted = lax.all_to_all(requests, "dom", split_axis=0, concat_axis=0, tiled=True)
    gathered_rows = (
        embeddings[wanted.reshape(-1)]
        .astype(jnp.bfloat16)
        .reshape(wanted.shape[0], wanted.shape[1], col_width)
    )
    returned_rows = lax.all_to_all(gathered_rows, "dom", split_axis=0, concat_axis=0, tiled=True)
    tail_rows = returned_rows.reshape(slot_total, col_width)
    head_rows = embeddings[src_rows].astype(jnp.bfloat16)
    corrupt_rows = embeddings[neg_rows].astype(jnp.bfloat16)
    relation = relations[rel_ids]
    weighted = (relation * tail_rows.astype(jnp.float32)).astype(jnp.bfloat16)
    pos_partial = jnp.sum(head_rows.astype(jnp.float32) * weighted.astype(jnp.float32), axis=1)
    positive = lax.psum(pos_partial, "col")
    scores = lax.dot_general(
        lax.all_gather(corrupt_rows, "col", axis=1, tiled=True),
        lax.all_gather(weighted, "col", axis=1, tiled=True),
        (((1,), (1,)), ((), ())),
        preferred_element_type=jnp.float32,
    )
    grad_positive = -live_mask * jax.nn.sigmoid(-positive)
    grad_scores = (live_mask[None, :] * jax.nn.sigmoid(scores) / negatives).astype(jnp.bfloat16)
    grad_head = grad_positive[:, None] * weighted.astype(jnp.float32)
    pulled = lax.dot_general(
        grad_scores, corrupt_rows, (((0,), (0,)), ((), ())), preferred_element_type=jnp.float32
    )
    grad_tail = (
        grad_positive[:, None] * head_rows.astype(jnp.float32) * relation + relation * pulled
    )
    grad_corrupt = jnp.dot(grad_scores, weighted, preferred_element_type=jnp.float32)
    returned = lax.all_to_all(
        grad_tail.reshape(owners, per_owner, col_width),
        "dom",
        split_axis=0,
        concat_axis=0,
        tiled=True,
    )
    gradient = jnp.zeros(embeddings.shape, jnp.float32)
    gradient = gradient.at[wanted.reshape(-1)].add(returned.reshape(slot_total, col_width))
    gradient = gradient.at[src_rows].add(grad_head).at[neg_rows].add(grad_corrupt)
    square_sum = lax.psum(jnp.sum(gradient * gradient, axis=1), "col")
    new_state = adagrad_state + square_sum / full_width
    new_embeddings = embeddings - learning_rate * gradient / jnp.sqrt(new_state)[:, None]
    return (new_embeddings, new_state)


def solution(mesh):
    placed = (
        P("dom", "col"),
        P("dom"),
        P(None, "col"),
        P("dom"),
        P("dom"),
        P("dom"),
        P("dom", None),
        P("dom"),
    )
    return jax.shard_map(
        shards, mesh=mesh, in_specs=placed, out_specs=(P("dom", "col"), P("dom")), check_vma=False
    )
```

profile of v0, /device:TPU:8, one launch (start us, length us, event | category | flops | bytes accessed | tf_op | source)
XLA Modules:
  0.0 313.2 jit_solution(9937594585295506261)
XLA Ops:
  7.2 0.0 copy-start
  7.2 0.9 all_to_all.12
  8.1 21.2 %all_to_all.19 = s32[64,1,64]{2,1,0:T(1,128)S(1)} all-to-all(s32[64,1,64]{2,1,0:T(1,128)S(1)} %all_to_all.12), channel_id=1, replica_groups=mesh['dom'=64,'col'=4] {'dom'}, dimensions={0} | all-to-all | bytes 32768 | tf_op jit(solution)/shard_map/all_to_all | solution.py:25
  29.3 0.5 broadcast.88
  29.8 0.7 reduce.4
  30.5 0.1 reshape.82
  30.7 15.8 %gather_fusion.2 = bf16[4096,128]{1,0:T(8,128)(2,1)} fusion(f32[4096,128]{1,0:T(8,128)} %param.8, s32[4096]{0:T(1024)S(1)} %broadcast_clamp_fusion), kind=kCustom, calls=%fused_computation.2 | custom fusion | bytes 2113536 | tf_op jit(solution)/shard_map/gather | solution.py:27
  46.5 5.6 %all-to-all-start.1 = ((bf16[64,64,128]{2,1,0:T(8,128)(2,1)}), bf16[64,64,128]{2,1,0:T(8,128)(2,1)}, u32[]{:S(2)}, u32[]{:S(2)}) async-start(bf16[64,64,128]{2,1,0:T(8,128)(2,1)} %bitcast.4), calls=%async_computation.1 | async-start | bytes 2097152 | tf_op jit(solution)/shard_map/all_to_all | solution.py:31
  52.2 0.0 all-gather.2.cloned.1.call-start
  52.2 0.0 copy-done.7
  52.2 0.0 copy-done
  52.2 14.2 %gather_fusion.1 = f32[4096,128]{1,0:T(8,128)} fusion(f32[1345,128]{1,0:T(8,128)S(1)} %copy-done, s32[4096]{0:T(1024)S(1)} %fusion.9), kind=kCustom, calls=%fused_computation.1 | custom fusion | bytes 4210688 | tf_op jit(solution)/shard_map/gather | solution.py:35
  66.5 13.7 %all-to-all-done.1 = bf16[64,64,128]{2,1,0:T(8,128)(2,1)} async-done(((bf16[64,64,128]{2,1,0:T(8,128)(2,1)}), bf16[64,64,128]{2,1,0:T(8,128)(2,1)}, u32[]{:S(2)}, u32[]{:S(2)}) %all-to-all-start.1) | async-done | bytes 1048608 | tf_op jit(solution)/shard_map/all_to_all | solution.py:31
  80.2 3.0 fusion.1
  83.2 0.0 all-gather.2.cloned.1.call-update
  83.2 0.0 copy-done.9
  83.3 0.0 copy-done.1
  83.3 3.0 gather_fusion.3
  86.3 0.0 copy-done.10
  86.3 0.1 fusion.8
  86.4 0.1 reshape.85
  86.5 0.0 copy-done.6
  86.5 14.3 %gather_fusion = bf16[4096,128]{1,0:T(8,128)(2,1)} fusion(f32[4096,128]{1,0:T(8,128)S(1)} %copy-done.1, s32[4096]{0:T(1024)S(1)} %get-tuple-element.5), kind=kCustom, calls=%fused_computation | custom fusion | bytes 2113536 | tf_op jit(solution)/shard_map/gather | solution.py:33
  100.8 1.5 convert_element_type.100
  102.3 32.8 %all_gather.6 = bf16[1000,512]{1,0:T(8,128)(2,1)} all-gather(bf16[1000,128]{1,0:T(8,128)(2,1)S(1)} %gather_fusion.3), channel_id=1, replica_groups=mesh['dom'=64,'col'=4] {'col'}, dimensions={1}, use_global_device_ids=true | all-gather | bytes 1280000 | tf_op jit(solution)/shard_map/all_gather | solution.py:40
  135.1 0.0 copy-done.2
  135.1 2.0 multiply_reduce_fusion.1
  137.0 0.1 reduce_sum.21
  137.1 16.2 %psum.14 = f32[4096]{0:T(1024)S(1)} all-reduce(f32[4096]{0:T(1024)S(1)} %reduce_sum.21), channel_id=1, replica_groups=mesh['dom'=64,'col'=4] {'col'}, use_global_device_ids=true, to_apply=%region_1.0 | all-reduce | flops 4096 | bytes 32768 | tf_op jit(solution)/shard_map/psum | solution.py:38
  153.3 0.0 all-gather.2.cloned.1.call-done
  153.4 0.0 copy-start.3
  153.4 0.0 copy-start.4
  153.4 8.1 %multiply_convert_fusion = bf16[1000,4096]{1,0:T(8,128)(2,1)S(1)} fusion(bf16[1000,512]{1,0:T(8,128)(2,1)} %all_gather.6, bf16[4096,512]{1,0:T(8,128)(2,1)} %all-gather.2.cloned.1.call-done, f32[4096]{0:T(1024)S(1)} %reshape.85), kind=kOutput, calls=%fused_computation.7 | convolution fusion | flops 4218880000 | bytes 13426688 | tf_op jit(solution)/shard_map/dot_general | solution.py:39
  161.5 0.0 copy-done.3
  161.5 0.0 copy-done.4
  161.5 0.0 copy-start.5
  161.5 4.7 %fusion = f32[4096,128]{1,0:T(8,128)} fusion(f32[4096,128]{1,0:T(8,128)S(1)} %copy-done.3, bf16[1000,4096]{1,0:T(8,128)(2,1)S(1)} %multiply_convert_fusion, bf16[1000,128]{1,0:T(8,128)(2,1)S(1)} %gather_fusion.3, f32[4096]{0:T(1024)S(1)} %divide_multiply_fusion, bf16[4096,128]{1,0:T(8,128)(2,1)S(1)} %copy-done.4), kind=kOutput, calls=%fused_computation.9 | convolution fusion | flops 1050673152 | bytes 13707264 | tf_op jit(solution)/shard_map/dot_general | solution.py:48
  166.2 0.0 copy-done.5
  166.2 8.2 %all-to-all-start.2 = ((f32[64,64,128]{2,1,0:T(8,128)}), f32[64,64,128]{2,1,0:T(8,128)}, u32[]{:S(2)}, u32[]{:S(2)}) async-start(f32[64,64,128]{2,1,0:T(8,128)} %bitcast.18), calls=%async_computation.2 | async-start | bytes 4194304 | tf_op jit(solution)/shard_map/all_to_all | solution.py:55
  174.4 5.8 %fusion.11 = f32[1000,128]{1,0:T(8,128)S(1)} fusion(bf16[1000,4096]{1,0:T(8,128)(2,1)} %copy-done.5, bf16[4096,128]{1,0:T(8,128)(2,1)} %fusion.1), kind=kOutput, calls=%fused_computation.36 | convolution fusion | flops 1048576000 | bytes 9752576 | tf_op jit(solution)/shard_map/dot_general | solution.py:54
  180.3 45.0 %all-to-all-done.2 = f32[64,64,128]{2,1,0:T(8,128)} async-done(((f32[64,64,128]{2,1,0:T(8,128)}), f32[64,64,128]{2,1,0:T(8,128)}, u32[]{:S(2)}, u32[]{:S(2)}) %all-to-all-start.2) | async-done | bytes 2097184 | tf_op jit(solution)/shard_map/all_to_all | solution.py:55
  225.3 24.1 %scatter_custom_fusion = f32[4096,128]{1,0:T(8,128)} fusion(s32[4096]{0:T(1024)S(1)} %bitcast.21, f32[4096,128]{1,0:T(8,128)} %bitcast.7, f32[]{:T(128)} %constant.8.clone.1), kind=kCustom, calls=%fused_computation.21 | custom fusion | flops 524288 | bytes 2097664 | tf_op jit(solution)/shard_map/scatter-add | solution.py:63
  249.3 27.5 %scatter_custom_fusion.1 = f32[4096,128]{1,0:T(8,128)} fusion(f32[4096,128]{1,0:T(8,128)} %scatter_custom_fusion, s32[4096]{0:T(1024)S(1)} %get-tuple-element.4, bf16[4096,128]{1,0:T(8,128)(2,1)} %fusion.1, f32[4096]{0:T(1024)S(1)} %divide_multiply_fusion), kind=kCustom, calls=%fused_computation.14 | custom fusion | flops 1572864 | bytes 3162112 | tf_op jit(solution)/shard_map/scatter-add | solution.py:64
  276.9 8.3 %scatter_fusion = f32[4096,128]{1,0:T(8,128)} fusion(f32[4096,128]{1,0:T(8,128)} %scatter_custom_fusion.1, s32[1000]{0:T(1024)S(1)} %compare_select_fusion.3, f32[1000,128]{1,0:T(8,128)S(1)} %fusion.11), kind=kCustom, calls=%fused_computation.6 | custom fusion | flops 128000 | bytes 1540000 | tf_op jit(solution)/shard_map/scatter-add | solution.py:64
  285.2 2.2 multiply_reduce_fusion
  287.4 15.4 %psum.15 = f32[4096]{0:T(1024)S(1)} all-reduce(f32[4096]{0:T(1024)S(1)} %multiply_reduce_fusion), channel_id=1, replica_groups=mesh['dom'=64,'col'=4] {'col'}, use_global_device_ids=true, to_apply=%region_6.0 | all-reduce | flops 4096 | bytes 32768 | tf_op jit(solution)/shard_map/psum | solution.py:65
  302.9 0.6 fusion.10
  303.5 2.9 divide_subtract_fusion
  (15 shorter events, 0.1 us)
Async XLA Ops:
  7.2 45.1 %copy-start = (f32[1345,128]{1,0:T(8,128)S(1)}, f32[1345,128]{1,0:T(8,128)}, u32[]{:S(2)}) copy-start(f32[1345,128]{1,0:T(8,128)} %param.10) | copy-start | bytes 2065924
  46.5 5.7 %copy-start.7 = (s32[4096]{0:T(1024)S(1)}, s32[4096]{0:T(1024)}, u32[]{:S(2)}) copy-start(s32[4096]{0:T(1024)} %param.13) | copy-start | bytes 49156
  46.5 33.7 %all-to-all-start.1 = ((bf16[64,64,128]{2,1,0:T(8,128)(2,1)}), bf16[64,64,128]{2,1,0:T(8,128)(2,1)}, u32[]{:S(2)}, u32[]{:S(2)}) async-start(bf16[64,64,128]{2,1,0:T(8,128)(2,1)} %bitcast.4), calls=%async_computation.1 | async-start | bytes 2097152 | tf_op jit(solution)/shard_map/all_to_all | solution.py:31
  52.2 101.2 %all-gather.2.cloned.1.call-start = ((), (), s32[]{:S(2)}) async-start(), calls=%async_computation.3 | async-start | bytes 5242880 | tf_op jit(solution)/shard_map/all_gather | solution.py:41
  66.4 16.8 %copy-start.9 = (s32[1000]{0:T(1024)S(1)}, s32[1000]{0:T(1024)}, u32[]{:S(2)}) copy-start(s32[1000]{0:T(1024)} %param.15) | copy-start | bytes 12004
  66.5 16.8 %copy-start.1 = (f32[4096,128]{1,0:T(8,128)S(1)}, f32[4096,128]{1,0:T(8,128)}, u32[]{:S(2)}) copy-start(f32[4096,128]{1,0:T(8,128)} %param.8) | copy-start | bytes 6291460
  83.2 3.1 copy-start.10
  83.2 3.3 %copy-start.6 = (s32[4096]{0:T(1024)S(1)}, s32[4096]{0:T(1024)}, u32[]{:S(2)}) copy-start(s32[4096]{0:T(1024)} %param.11) | copy-start | bytes 49156
  100.8 34.3 %copy-start.2 = (f32[4096,128]{1,0:T(8,128)S(1)}, f32[4096,128]{1,0:T(8,128)}, u32[]{:S(2)}) copy-start(f32[4096,128]{1,0:T(8,128)} %gather_fusion.1) | copy-start | bytes 6291460
  153.4 8.1 %copy-start.3 = (f32[4096,128]{1,0:T(8,128)S(1)}, f32[4096,128]{1,0:T(8,128)}, u32[]{:S(2)}) copy-start(f32[4096,128]{1,0:T(8,128)} %gather_fusion.1) | copy-start | bytes 6291460
  153.4 8.1 %copy-start.4 = (bf16[4096,128]{1,0:T(8,128)(2,1)S(1)}, bf16[4096,128]{1,0:T(8,128)(2,1)}, u32[]{:S(2)}) copy-start(bf16[4096,128]{1,0:T(8,128)(2,1)} %gather_fusion) | copy-start | bytes 3145732
  161.5 4.7 %copy-start.5 = (bf16[1000,4096]{1,0:T(8,128)(2,1)}, bf16[1000,4096]{1,0:T(8,128)(2,1)S(1)}, u32[]{:S(2)}) copy-start(bf16[1000,4096]{1,0:T(8,128)(2,1)S(1)} %multiply_convert_fusion) | copy-start | bytes 24576004
  166.2 59.1 %all-to-all-start.2 = ((f32[64,64,128]{2,1,0:T(8,128)}), f32[64,64,128]{2,1,0:T(8,128)}, u32[]{:S(2)}, u32[]{:S(2)}) async-start(f32[64,64,128]{2,1,0:T(8,128)} %bitcast.18), calls=%async_computation.2 | async-start | bytes 4194304 | tf_op jit(solution)/shard_map/all_to_all | solution.py:55
  285.2 17.7 %copy-start.8 = (f32[4096]{0:T(1024)S(1)}, f32[4096]{0:T(1024)}, u32[]{:S(2)}) copy-start(f32[4096]{0:T(1024)} %param.9) | copy-start | bytes 49156
Sparse Core Ops, SparseCore 0:
  83.4 63.6 all-gather.1
where the time goes:
time: 314 us; the launch traced here: 313 us
  blocking collectives  85.7 us (27%)
  other arithmetic  73 us (23%)
  waiting for transfers between devices  58.8 us (19%)
  local copies, waits for them, and re-layouts  49 us (16%)
  matrix products  18.6 us (6%)
  between operations  14.3 us (5%)
  starting transfers between devices  13.9 us (4%)
    all_to_all x1, waiting for transfers between devices, shards(): lax.all_to_all(grad_tail.reshape(owners, per_owner, col_width), 'dom', sp...  45 us
    scatter-add x2, other arithmetic, shards(): gradient.at[src_rows].add(grad_head).at[neg_rows].add(grad_corrupt)  35.9 us
    all_gather x1, blocking collectives, shards(): lax.all_gather(corrupt_rows, 'col', axis=1, tiled=True)  32.8 us
    scatter-add x1, other arithmetic, shards(): gradient.at[wanted.reshape(-1)].add(returned.reshape(slot_total, col_width))  24.1 us
    all_to_all x1, blocking collectives, shards(): lax.all_to_all(requests, 'dom', split_axis=0, concat_axis=0, tiled=True)  21.2 us
    psum x1, blocking collectives, shards(): positive = lax.psum(pos_partial, 'col')  16.2 us
    gather x1, local copies, waits for them, and re-layouts, shards(): embeddings[wanted.reshape(-1)].astype(jnp.bfloat16)  15.8 us
    psum x1, blocking collectives, shards(): square_sum = lax.psum(jnp.sum(gradient * gradient, axis=1), 'col')  15.4 us
  transfers between devices with their start and end apart: 3, of which 2 were waited for; matrix products, arithmetic and copies ran while one was open for 13% of the time, Pallas kernels for 0%

commit v1 on v0

v1 whole, which is shorter than its diff:
```python
import functools
import jax
import jax.numpy as jnp
from jax import lax
from jax.experimental import pallas as pl
from jax.experimental.pallas import tpu as pltpu
from jax.sharding import PartitionSpec as P

learning_rate = 0.3
OWNERS = 64
COLS = 4
PART = 16
SLOTS = OWNERS * COLS * PART
EDGES = OWNERS * PART
WIDTH = 128
NEG = 1000
NEG_PAD = 1008
PIECE = EDGES + NEG_PAD
ROW_BITS = 12
CHAINS = 4

F32, BF16 = jnp.float32, jnp.bfloat16
SMEM = pl.BlockSpec(memory_space=pltpu.SMEM)
VMEM = pl.BlockSpec(memory_space=pltpu.VMEM)


def call(body, name, out, ins, scratch, flops=0, moved=0):
    return pl.pallas_call(
        body,
        out_shape=out,
        in_specs=ins,
        out_specs=jax.tree.map(lambda _: VMEM, out),
        scratch_shapes=scratch,
        compiler_params=pltpu.CompilerParams(vmem_limit_bytes=40 * 1024 * 1024),
        cost_estimate=pl.CostEstimate(flops=flops, bytes_accessed=moved, transcendentals=0),
        name=name,
    )


def shape(rows, dtype):
    return jax.ShapeDtypeStruct((rows, WIDTH), dtype)


def gather_heads_body(col, src, neg, table, *rest):
    outs, (rows, corrupt) = rest[:COLS], rest[COLS:]
    for s in range(COLS):
        quarter = (col[0] + s) & (COLS - 1)

        @pl.loop(0, OWNERS)
        def _(b):
            base = (b * COLS + quarter) * PART
            for i in range(PART):
                rows[pl.ds(s * EDGES + b * PART + i, 1), :] = table[pl.ds(src[base + i], 1), :]

    @pl.loop(0, NEG // 8)
    def _(g):
        for i in range(8):
            corrupt[pl.ds(g * 8 + i, 1), :] = table[pl.ds(neg[g * 8 + i], 1), :]

    corrupt[NEG:NEG_PAD, :] = jnp.zeros((NEG_PAD - NEG, WIDTH), F32)
    rounded = corrupt[...].astype(BF16)
    for s in range(COLS):
        outs[s][0:EDGES, :] = rows[s * EDGES : (s + 1) * EDGES, :].astype(BF16)
        outs[s][EDGES:PIECE, :] = rounded


def gather_heads(col, src, neg, table):
    return call(
        gather_heads_body,
        "gather_heads",
        [shape(PIECE, BF16)] * COLS,
        [SMEM, SMEM, SMEM, VMEM],
        [pltpu.VMEM((SLOTS, WIDTH), F32), pltpu.VMEM((NEG_PAD, WIDTH), F32)],
        moved=20_000_000,
    )(col, src, neg, table)


def gather_tails_body(wanted, table, relations, weighted, factors, rows):
    @pl.loop(0, SLOTS // 16)
    def _(g):
        for i in range(16):
            j = g * 16 + i
            word = wanted[j]
            rows[pl.ds(j, 1), :] = table[pl.ds(word & ((1 << ROW_BITS) - 1), 1), :]
            factors[pl.ds(j, 1), :] = relations[pl.ds(word >> ROW_BITS, 1), :]

    weighted[...] = (factors[...] * rows[...].astype(BF16).astype(F32)).astype(BF16)


def gather_tails(wanted, table, relations):
    return call(
        gather_tails_body,
        "gather_tails",
        [shape(SLOTS, BF16), shape(SLOTS, F32)],
        [SMEM, VMEM, VMEM],
        [pltpu.VMEM((SLOTS, WIDTH), F32)],
        moved=20_000_000,
    )(wanted, table, relations)


def edge_scores_body(col, weighted, live, p0, p1, p2, p3, pulled_out, o0, o1, o2, o3, w, heads, corrupt):
    outs = (o0, o1, o2, o3)
    owner = [(col[0] + COLS - s) & (COLS - 1) for s in range(COLS)]
    span = [slice(s * WIDTH, (s + 1) * WIDTH) for s in range(COLS)]
    for s, piece in enumerate((p0, p1, p2, p3)):
        w[:, span[s]] = weighted[:, owner[s]].reshape(EDGES, WIDTH)
        heads[:, span[s]] = piece[0:EDGES, :]
        corrupt[0:NEG_PAD, span[s]] = piece[EDGES:PIECE, :]
        corrupt[NEG_PAD:1024, span[s]] = jnp.zeros((1024 - NEG_PAD, WIDTH), BF16)
    grad_corrupt = jnp.zeros((1024, COLS * WIDTH), F32)
    negatives = corrupt[...]
    block = 256
    for k in range(EDGES // block):
        rows = slice(k * block, (k + 1) * block)
        wk = w[rows, :]
        wf = wk.astype(F32)
        hf = heads[rows, :].astype(F32)
        mask = live[rows, :]
        positive = jnp.sum(hf * wf, axis=1, keepdims=True)
        grad_positive = -mask * jax.nn.sigmoid(-positive)
        scores = lax.dot_general(wk, negatives, (((1,), (1,)), ((), ())), preferred_element_type=F32)
        grad_scores = (mask * jax.nn.sigmoid(scores) * (1.0 / NEG)).astype(BF16)
        pulled = jnp.dot(grad_scores, negatives, preferred_element_type=F32)
        pulled = (grad_positive * hf + pulled).astype(BF16)
        grad_head = (grad_positive * wf).astype(BF16)
        grad_corrupt += lax.dot_general(
            grad_scores, wk, (((0,), (0,)), ((), ())), preferred_element_type=F32
        )
        for s in range(COLS):
            buckets = block // PART
            pulled_out[pl.ds(k * buckets, buckets), owner[s]] = pulled[:, span[s]].reshape(
                buckets, PART, WIDTH
            )
            outs[s][rows, :] = grad_head[:, span[s]]
    for s in range(COLS):
        outs[s][EDGES:PIECE, :] = grad_corrupt[0:NEG_PAD, span[s]].astype(BF16)


def edge_scores(col, weighted, live, pieces):
    return call(
        edge_scores_body,
        "edge_scores",
        [jax.ShapeDtypeStruct((OWNERS, COLS, PART, WIDTH), BF16)] + [shape(PIECE, BF16)] * COLS,
        [SMEM] + [VMEM] * 6,
        [pltpu.VMEM((EDGES, COLS * WIDTH), BF16)] * 2 + [pltpu.VMEM((1024, COLS * WIDTH), BF16)],
        flops=3_200_000_000,
        moved=5_000_000,
    )(col, weighted, live, *pieces)


def total_of(tables):
    total = tables[0][...]
    for table in tables[1:]:
        total += table[...]
    return total


def scatter_heads_body(col, src, neg, g0, g1, g2, g3, out, rows, corrupt, *tables):
    tables = (out,) + tables
    for table in tables:
        table[...] = jnp.zeros((SLOTS, WIDTH), F32)
    grad_corrupt = jnp.zeros((NEG_PAD, WIDTH), F32)
    for s, piece in enumerate((g0, g1, g2, g3)):
        rows[s * EDGES : (s + 1) * EDGES, :] = piece[0:EDGES, :].astype(F32)
        grad_corrupt += piece[EDGES:PIECE, :].astype(F32)
    corrupt[...] = grad_corrupt
    for s in range(COLS):
        quarter = (col[0] + s) & (COLS - 1)

        @pl.loop(0, OWNERS)
        def _(b):
            base = (b * COLS + quarter) * PART
            for i in range(PART):
                into = tables[i % CHAINS]
                into[pl.ds(src[base + i], 1), :] += rows[pl.ds(s * EDGES + b * PART + i, 1), :]

    @pl.loop(0, NEG // 8)
    def _(g):
        for i in range(8):
            into = tables[i % CHAINS]
            into[pl.ds(neg[g * 8 + i], 1), :] += corrupt[pl.ds(g * 8 + i, 1), :]

    out[...] = total_of(tables)


def scatter_heads(col, src, neg, pieces):
    return call(
        scatter_heads_body,
        "scatter_heads",
        shape(SLOTS, F32),
        [SMEM] * 3 + [VMEM] * 4,
        [pltpu.VMEM((SLOTS, WIDTH), F32), pltpu.VMEM((NEG_PAD, WIDTH), F32)]
        + [pltpu.VMEM((SLOTS, WIDTH), F32)] * (CHAINS - 1),
        moved=30_000_000,
    )(col, src, neg, *pieces)


def scatter_tails_body(wanted, start, factors, pulled, out, rows, *tables):
    tables = (out,) + tables
    out[...] = start[...]
    for table in tables[1:]:
        table[...] = jnp.zeros((SLOTS, WIDTH), F32)
    rows[...] = factors[...] * pulled[...].astype(F32)

    @pl.loop(0, SLOTS // 16)
    def _(g):
        for i in range(16):
            j = g * 16 + i
            into = tables[i % CHAINS]
            into[pl.ds(wanted[j] & ((1 << ROW_BITS) - 1), 1), :] += rows[pl.ds(j, 1), :]

    out[...] = total_of(tables)


def scatter_tails(wanted, start, factors, pulled):
    return call(
        scatter_tails_body,
        "scatter_tails",
        shape(SLOTS, F32),
        [SMEM] + [VMEM] * 3,
        [pltpu.VMEM((SLOTS, WIDTH), F32)] * CHAINS,
        moved=30_000_000,
    )(wanted, start, factors, pulled)


def shifted(x, s):
    return lax.ppermute(x, "col", [(i, (i + s) % COLS) for i in range(COLS)])


def shards(
    embeddings, adagrad_state, relations, src_rows, dst_rows, rel_ids, bucket_counts, neg_rows
):
    axes = ("dom", "col")
    me = lax.axis_index("col")
    col = me.astype(jnp.int32).reshape(1)
    first = lax.broadcasted_iota(jnp.int32, (OWNERS, PART), 1) + me * PART
    live = (first < bucket_counts[0][:, None]).astype(F32).reshape(EDGES, 1)

    words = dst_rows | (rel_ids << ROW_BITS)
    wanted = lax.all_to_all(
        words.reshape(OWNERS, SLOTS // OWNERS), "dom", split_axis=0, concat_axis=0, tiled=True
    ).reshape(SLOTS)
    pieces = gather_heads(col, src_rows, neg_rows, embeddings)
    pieces = [pieces[0]] + [shifted(pieces[s], s) for s in range(1, COLS)]

    weighted, factors = gather_tails(wanted, embeddings, relations)
    weighted = lax.all_to_all(
        weighted.reshape(OWNERS * COLS, PART, WIDTH), axes, split_axis=0, concat_axis=0, tiled=True
    ).reshape(OWNERS, COLS, PART, WIDTH)
    pulled, *grads = edge_scores(col, weighted, live, pieces)
    pulled = lax.all_to_all(
        pulled.reshape(OWNERS * COLS, PART, WIDTH), axes, split_axis=0, concat_axis=0, tiled=True
    ).reshape(SLOTS, WIDTH)
    grads = [grads[0]] + [shifted(grads[s], -s) for s in range(1, COLS)]
    gradient = scatter_heads(col, src_rows, neg_rows, grads)
    gradient = scatter_tails(wanted, gradient, factors, pulled)

    squares = jnp.sum(gradient * gradient, axis=1).reshape(-1, WIDTH)
    squares = (squares + shifted(squares, 2)) + (shifted(squares, 1) + shifted(squares, 3))
    new_state = adagrad_state + squares.reshape(-1) / (COLS * WIDTH)
    new_embeddings = embeddings - learning_rate * gradient / jnp.sqrt(new_state)[:, None]
    return (new_embeddings, new_state)


def solution(mesh):
    placed = (
        P("dom", "col"),
        P("dom"),
        P(None, "col"),
        P("dom"),
        P("dom"),
        P("dom"),
        P("dom", None),
        P("dom"),
    )
    return jax.shard_map(
        shards, mesh=mesh, in_specs=placed, out_specs=(P("dom", "col"), P("dom")), check_vma=False
    )
```

time: 314 us -> 185 us (0.59)
  other arithmetic: 73 us -> 4.44 us
  blocking collectives: 85.7 us -> 21.2 us
  Pallas kernels: 0 us -> 40.7 us
  local copies, waits for them, and re-layouts: 49 us -> 19.4 us
  matrix products: 18.6 us -> 0 us
  starting transfers between devices: 13.9 us -> 32.4 us
  between operations: 14.3 us -> 0.78 us
  waiting for transfers between devices: 58.8 us -> 62.8 us
    ppermute x0 -> x9, waiting for transfers between devices: none -> 62.8 us  [shifted(): return lax.ppermute(x, 'col', [(i, (i + s) % COLS) for i in range(COLS)])]
    scatter-add x3 -> x0, other arithmetic: 59.9 us -> none  [the longest x2 35.9 us: shards(): gradient.at[src_rows].add(grad_head).at[neg_rows].add(grad_corrupt)]
    all_to_all x2, waiting for transfers between devices: 58.7 us -> 0.01 us  [the longest x1 0.01 us: shards(): lax.all_to_all(pulled.reshape(OWNERS * COLS, PART, WIDTH), axes, split_ax...]
    gather x4 -> x0, local copies, waits for them, and re-layouts: 47.3 us -> none  [the longest x1 15.8 us: shards(): embeddings[wanted.reshape(-1)].astype(jnp.bfloat16)]
    pallas_call x0 -> x5, Pallas kernels: none -> 40.7 us  [the longest x1 9.99 us: scatter_heads(): call(scatter_heads_body, 'scatter_heads', shape(SLOTS, F32), [SMEM] * 3 +...]
    all_gather x1 -> x0, blocking collectives: 32.8 us -> none  [shards(): lax.all_gather(corrupt_rows, 'col', axis=1, tiled=True)]
    psum x2 -> x0, blocking collectives: 31.7 us -> none  [the longest x1 16.2 us: shards(): positive = lax.psum(pos_partial, 'col')]
    dot_general x3 -> x0, matrix products: 18.6 us -> none  [the longest x1 8.09 us: shards(): lax.dot_general(lax.all_gather(corrupt_rows, 'col', axis=1, tiled=True),...]
  transfers between devices with their start and end apart: 3 -> 11, of which waited for: 2 -> 7; matrix products, arithmetic and copies ran while one was open for 13% -> 1% of each run, Pallas kernels for 0% -> 10%
where the time goes in v1:
time: 185 us; the launch traced here: 182 us
  waiting for transfers between devices  62.8 us (34%)
  Pallas kernels  40.7 us (22%)
  starting transfers between devices  32.4 us (18%)
  blocking collectives  21.2 us (11%)
  local copies, waits for them, and re-layouts  19.4 us (10%)
  other arithmetic  4.44 us (2%)
    ppermute x9, waiting for transfers between devices, shifted(): return lax.ppermute(x, 'col', [(i, (i + s) % COLS) for i in range(COLS)])  62.8 us
    all_to_all x1, blocking collectives, shards(): lax.all_to_all(words.reshape(OWNERS, SLOTS // OWNERS), 'dom', split_axis=...  21.2 us
    unnamed x42, local copies, waits for them, and re-layouts  17.6 us
    ppermute x9, starting transfers between devices, shifted(): return lax.ppermute(x, 'col', [(i, (i + s) % COLS) for i in range(COLS)])  14.4 us
    all_to_all x1, starting transfers between devices, shards(): lax.all_to_all(pulled.reshape(OWNERS * COLS, PART, WIDTH), axes, split_ax...  11.5 us
    pallas_call x1, Pallas kernels, scatter_heads(): call(scatter_heads_body, 'scatter_heads', shape(SLOTS, F32), [SMEM] * 3 +...  9.99 us
    pallas_call x1, Pallas kernels, gather_tails(): call(gather_tails_body, 'gather_tails', [shape(SLOTS, BF16), shape(SLOTS,...  8.92 us
    pallas_call x1, Pallas kernels, scatter_tails(): call(scatter_tails_body, 'scatter_tails', shape(SLOTS, F32), [SMEM] + [VM...  8.2 us
  transfers between devices with their start and end apart: 11, of which 7 were waited for; matrix products, arithmetic and copies ran while one was open for 1% of the time, Pallas kernels for 10%

profile of v1, /device:TPU:8, one launch (start us, length us, event | category | flops | bytes accessed | tf_op | source)
XLA Modules:
  0.0 181.7 jit_solution(15718139350650528187)
XLA Ops:
  0.6 0.7 shift-left_or_fusion
  1.4 0.1 all_to_all.12
  1.5 21.2 %all_to_all.19 = s32[64,1,64]{2,1,0:T(1,128)S(1)} all-to-all(s32[64,1,64]{2,1,0:T(1,128)S(1)} %all_to_all.12), channel_id=1, replica_groups=mesh['dom'=64,'col'=4] {'dom'}, dimensions={0} | all-to-all | bytes 32768 | tf_op jit(solution)/shard_map/all_to_all | solution.py:240
  22.7 0.5 broadcast.13
  23.2 0.7 reduce.3
  24.0 1.6 copy-done
  25.6 1.1 copy-done.8
  26.7 8.9 %gather_tails.1 = (bf16[4096,128]{1,0:T(8,128)(2,1)S(1)}, f32[4096,128]{1,0:T(8,128)S(1)}) custom-call(s32[4096]{0:T(1024)S(1)} %reshape.63.wanted, f32[4096,128]{1,0:T(8,128)S(1)} %copy-done, f32[1345,128]{1,0:T(8,128)S(1)} %copy-done.8), custom_call_target="tpu_custom_call" | custom-call | bytes 20000000 | tf_op jit(solution)/shard_map/gather_tails/pallas_call | solution.py:91
  35.7 1.4 copy-done.4
  37.0 1.0 copy-done.6
  38.0 6.5 %all-to-all-start.1 = ((bf16[256,16,128]{2,1,0:T(8,128)(2,1)}), bf16[256,16,128]{2,1,0:T(8,128)(2,1)S(1)}, u32[]{:S(2)}, u32[]{:S(2)}) async-start(bf16[256,16,128]{2,1,0:T(8,128)(2,1)} %bitcast.14), calls=%async_computation.1 | async-start | bytes 2097152 | tf_op jit(solution)/shard_map/all_to_all | solution.py:247
  44.5 8.1 %gather_heads.1 = (bf16[2032,128]{1,0:T(8,128)(2,1)S(1)}, bf16[2032,128]{1,0:T(8,128)(2,1)}, bf16[2032,128]{1,0:T(8,128)(2,1)}, bf16[2032,128]{1,0:T(8,128)(2,1)}) custom-call(s32[1]{0:T(128)} %bitcast.col, s32[4096]{0:T(1024)S(1)} %copy-done.12, s32[1000]{0:T(1024)S(1)} %copy-done.13, f32[4096,128]{1,0:T(8,128)S(1)} %copy-done.1), custom_call_target="tpu_custom_call" | custom-call | bytes 20000000 | tf_op jit(solution)/shard_map/gather_heads/pallas_call | solution.py:68
  52.6 0.8 copy-done.14
  53.4 1.5 collective-permute-start
  54.9 2.7 %collective-permute-start.1 = (bf16[2032,128]{1,0:T(8,128)(2,1)}, bf16[2032,128]{1,0:T(8,128)(2,1)}, u32[]{:S(2)}, u32[]{:S(2)}) collective-permute-start(bf16[2032,128]{1,0:T(8,128)(2,1)} %get-tuple-element.16), channel_id=1, source_target_pairs={{0,2},{1,3},{2,0},{3,1},{4,6},{5,7},{6,4},{7,5},{8,10},{9,11},{10,... | collective-permute-start | bytes 1560584 | tf_op jit(solution)/shard_map/ppermute | solution.py:227
  57.6 0.5 collective-permute-start.2
  58.2 1.1 reshape.71.live
  59.4 15.5 %collective-permute-done.p1 = bf16[2032,128]{1,0:T(8,128)(2,1)} collective-permute-done((bf16[2032,128]{1,0:T(8,128)(2,1)}, bf16[2032,128]{1,0:T(8,128)(2,1)}, u32[]{:S(2)}, u32[]{:S(2)}) %collective-permute-start) | collective-permute-done | bytes 520224 | tf_op jit(solution)/shard_map/ppermute | solution.py:227
  74.8 2.2 %collective-permute-done.1.p2 = bf16[2032,128]{1,0:T(8,128)(2,1)} collective-permute-done((bf16[2032,128]{1,0:T(8,128)(2,1)}, bf16[2032,128]{1,0:T(8,128)(2,1)}, u32[]{:S(2)}, u32[]{:S(2)}) %collective-permute-start.1) | collective-permute-done | bytes 520224 | tf_op jit(solution)/shard_map/ppermute | solution.py:227
  77.0 9.9 %collective-permute-done.2.p3 = bf16[2032,128]{1,0:T(8,128)(2,1)} collective-permute-done((bf16[2032,128]{1,0:T(8,128)(2,1)}, bf16[2032,128]{1,0:T(8,128)(2,1)}, u32[]{:S(2)}, u32[]{:S(2)}) %collective-permute-start.2) | collective-permute-done | bytes 520224 | tf_op jit(solution)/shard_map/ppermute | solution.py:227
  86.9 1.0 copy-done.9
  88.0 1.0 copy-done.15
  89.0 5.5 %edge_scores.1 = (bf16[64,4,16,128]{3,2,1,0:T(8,128)(2,1)S(1)}, bf16[2032,128]{1,0:T(8,128)(2,1)S(1)}, bf16[2032,128]{1,0:T(8,128)(2,1)S(1)}, bf16[2032,128]{1,0:T(8,128)(2,1)S(1)}, bf16[2032,128]{1,0:T(8,128)(2,1)S(1)}) custom-call(s32[1]{0:T(128)} %bitcast.col, bf16[64,4,16,128]{3,2,1,0:T(8,128)(2,1)S(1)} %bitcast.13, f32[1024,1]{1,0:T(8,128)S(1)} %copy-done.9, ...), custom_call_target="tpu_custom_call" | custom-call | flops 3200000000 | bytes 5000000 | tf_op jit(solution)/shard_map/edge_scores/pallas_call | solution.py:140
  94.5 1.0 copy-done.7
  95.5 0.8 copy-done.10
  96.3 0.8 copy-done.16
  97.1 0.8 copy-done.17
  97.9 0.8 copy-done.18
  98.7 11.5 %all-to-all-start.2 = ((bf16[256,16,128]{2,1,0:T(8,128)(2,1)}), bf16[256,16,128]{2,1,0:T(8,128)(2,1)S(1)}, u32[]{:S(2)}, u32[]{:S(2)}) async-start(bf16[256,16,128]{2,1,0:T(8,128)(2,1)} %bitcast.15), calls=%async_computation.2 | async-start | bytes 2097152 | tf_op jit(solution)/shard_map/all_to_all | solution.py:251
  110.2 2.2 %collective-permute-start.3 = (bf16[2032,128]{1,0:T(8,128)(2,1)}, bf16[2032,128]{1,0:T(8,128)(2,1)S(1)}, u32[]{:S(2)}, u32[]{:S(2)}) collective-permute-start(bf16[2032,128]{1,0:T(8,128)(2,1)} %copy-done.18), channel_id=1, source_target_pairs={{0,3},{1,0},{2,1},{3,2},{4,7},{5,4},{6,5},{7,6},{8,11},{9,8},{10,9... | collective-permute-start | bytes 1560584 | tf_op jit(solution)/shard_map/ppermute | solution.py:227
  112.4 0.8 collective-permute-start.4
  113.2 1.8 %collective-permute-start.5 = (bf16[2032,128]{1,0:T(8,128)(2,1)}, bf16[2032,128]{1,0:T(8,128)(2,1)S(1)}, u32[]{:S(2)}, u32[]{:S(2)}) collective-permute-start(bf16[2032,128]{1,0:T(8,128)(2,1)} %copy-done.16), channel_id=1, source_target_pairs={{0,1},{1,2},{2,3},{3,0},{4,5},{5,6},{6,7},{7,4},{8,9},{9,10},{10,1... | collective-permute-start | bytes 1560584 | tf_op jit(solution)/shard_map/ppermute | solution.py:227
  115.1 17.9 %collective-permute-done.3.g1 = bf16[2032,128]{1,0:T(8,128)(2,1)S(1)} collective-permute-done((bf16[2032,128]{1,0:T(8,128)(2,1)}, bf16[2032,128]{1,0:T(8,128)(2,1)S(1)}, u32[]{:S(2)}, u32[]{:S(2)}) %collective-permute-start.3) | collective-permute-done | bytes 520224 | tf_op jit(solution)/shard_map/ppermute | solution.py:227
  132.9 14.0 %collective-permute-done.4.g2 = bf16[2032,128]{1,0:T(8,128)(2,1)S(1)} collective-permute-done((bf16[2032,128]{1,0:T(8,128)(2,1)}, bf16[2032,128]{1,0:T(8,128)(2,1)S(1)}, u32[]{:S(2)}, u32[]{:S(2)}) %collective-permute-start.4) | collective-permute-done | bytes 520224 | tf_op jit(solution)/shard_map/ppermute | solution.py:227
  147.0 1.0 copy-done.11
  148.0 10.0 %scatter_heads.1.start = f32[4096,128]{1,0:T(8,128)S(1)} custom-call(s32[1]{0:T(128)} %bitcast.col, s32[4096]{0:T(1024)S(1)} %copy-done.12, s32[1000]{0:T(1024)S(1)} %copy-done.13, bf16[2032,128]{1,0:T(8,128)(2,1)S(1)} %copy-done.11, bf16[2032,128]{1,0:T(8,128)(2,1)S(1)} %collective-permute-done.3.g1, bf16[2032,128]{1,0:T(8,128)(2,1)S(1)} %collective-permute-done.4.g2, ...), custom_call_target="tpu_custom_call" | custom-call | bytes 30000000 | tf_op jit(solution)/shard_map/scatter_heads/pallas_call | solution.py:187
  158.0 1.3 copy-done.2
  159.3 1.6 copy-done.3
  160.9 1.6 copy-done.5
  162.5 8.2 %scatter_tails.1 = f32[4096,128]{1,0:T(8,128)S(1)} custom-call(s32[4096]{0:T(1024)S(1)} %reshape.63.wanted, f32[4096,128]{1,0:T(8,128)S(1)} %copy-done.3, f32[4096,128]{1,0:T(8,128)S(1)} %copy-done.5, bf16[4096,128]{1,0:T(8,128)(2,1)S(1)} %bitcast.12), custom_call_target="tpu_custom_call" | custom-call | bytes 30000000 | tf_op jit(solution)/shard_map/scatter_tails/pallas_call | solution.py:216
  170.7 0.6 multiply_reduce_fusion
  171.4 1.3 collective-permute-start.7
  172.7 1.5 collective-permute-start.8
  174.2 2.0 %collective-permute-start.6 = (f32[32,128]{1,0:T(8,128)S(1)}, f32[32,128]{1,0:T(8,128)S(1)}, u32[]{:S(2)}, u32[]{:S(2)}) collective-permute-start(f32[32,128]{1,0:T(8,128)S(1)} %bitcast.18), channel_id=1, source_target_pairs={{0,2},{1,3},{2,0},{3,1},{4,6},{5,7},{6,4},{7,5},{8,10},{9,11},{10,... | collective-permute-start | bytes 49160 | tf_op jit(solution)/shard_map/ppermute | solution.py:227
  176.2 0.3 collective-permute-done.8
  176.4 3.0 %collective-permute-done.6 = f32[32,128]{1,0:T(8,128)S(1)} collective-permute-done((f32[32,128]{1,0:T(8,128)S(1)}, f32[32,128]{1,0:T(8,128)S(1)}, u32[]{:S(2)}, u32[]{:S(2)}) %collective-permute-start.6) | collective-permute-done | bytes 16416 | tf_op jit(solution)/shard_map/ppermute | solution.py:227
  179.4 0.6 fusion
  180.0 1.7 divide_subtract_fusion
  (33 shorter events, 0.2 us)
Async XLA Ops:
  24.0 1.6 copy-start
  25.6 1.1 copy-start.8
  26.7 17.8 %copy-start.1 = (f32[4096,128]{1,0:T(8,128)S(1)}, f32[4096,128]{1,0:T(8,128)}, u32[]{:S(2)}) copy-start(f32[4096,128]{1,0:T(8,128)} %table.3) | copy-start | bytes 6291460
  26.7 17.8 %copy-start.12 = (s32[4096]{0:T(1024)S(1)}, s32[4096]{0:T(1024)}, u32[]{:S(2)}) copy-start(s32[4096]{0:T(1024)} %src.3) | copy-start | bytes 49156
  26.7 17.8 %copy-start.13 = (s32[1000]{0:T(1024)S(1)}, s32[1000]{0:T(1024)}, u32[]{:S(2)}) copy-start(s32[1000]{0:T(1024)} %neg.3) | copy-start | bytes 12004
  35.6 1.4 copy-start.4
  37.0 1.0 copy-start.6
  38.0 20.2 %copy-start.20 = (s32[1,64]{1,0:T(1,128)S(1)}, s32[1,64]{1,0:T(1,128)}, u32[]{:S(2)}) copy-start(s32[1,64]{1,0:T(1,128)} %param.14) | copy-start | bytes 772
  38.0 49.0 %all-to-all-start.1 = ((bf16[256,16,128]{2,1,0:T(8,128)(2,1)}), bf16[256,16,128]{2,1,0:T(8,128)(2,1)S(1)}, u32[]{:S(2)}, u32[]{:S(2)}) async-start(bf16[256,16,128]{2,1,0:T(8,128)(2,1)} %bitcast.14), calls=%async_computation.1 | async-start | bytes 2097152 | tf_op jit(solution)/shard_map/all_to_all | solution.py:247
  52.6 0.8 copy-start.14
  53.4 21.4 %collective-permute-start = (bf16[2032,128]{1,0:T(8,128)(2,1)}, bf16[2032,128]{1,0:T(8,128)(2,1)}, u32[]{:S(2)}, u32[]{:S(2)}) collective-permute-start(bf16[2032,128]{1,0:T(8,128)(2,1)} %get-tuple-element.15), channel_id=1, source_target_pairs={{0,1},{1,2},{2,3},{3,0},{4,5},{5,6},{6,7},{7,4},{8,9},{9,10},{10,1... | collective-permute-start | bytes 1560584 | tf_op jit(solution)/shard_map/ppermute | solution.py:227
  54.9 22.2 %collective-permute-start.1 = (bf16[2032,128]{1,0:T(8,128)(2,1)}, bf16[2032,128]{1,0:T(8,128)(2,1)}, u32[]{:S(2)}, u32[]{:S(2)}) collective-permute-start(bf16[2032,128]{1,0:T(8,128)(2,1)} %get-tuple-element.16), channel_id=1, source_target_pairs={{0,2},{1,3},{2,0},{3,1},{4,6},{5,7},{6,4},{7,5},{8,10},{9,11},{10,... | collective-permute-start | bytes 1560584 | tf_op jit(solution)/shard_map/ppermute | solution.py:227
  57.6 29.3 %collective-permute-start.2 = (bf16[2032,128]{1,0:T(8,128)(2,1)}, bf16[2032,128]{1,0:T(8,128)(2,1)}, u32[]{:S(2)}, u32[]{:S(2)}) collective-permute-start(bf16[2032,128]{1,0:T(8,128)(2,1)} %get-tuple-element.17), channel_id=1, source_target_pairs={{0,3},{1,0},{2,1},{3,2},{4,7},{5,4},{6,5},{7,6},{8,11},{9,8},{10,9... | collective-permute-start | bytes 1560584 | tf_op jit(solution)/shard_map/ppermute | solution.py:227
  86.9 1.0 copy-start.9
  88.0 1.0 copy-start.15
  94.5 1.0 copy-start.7
  95.5 0.8 copy-start.10
  96.3 0.8 copy-start.16
  97.1 0.8 copy-start.17
  97.9 0.8 copy-start.18
  98.7 60.6 %all-to-all-start.2 = ((bf16[256,16,128]{2,1,0:T(8,128)(2,1)}), bf16[256,16,128]{2,1,0:T(8,128)(2,1)S(1)}, u32[]{:S(2)}, u32[]{:S(2)}) async-start(bf16[256,16,128]{2,1,0:T(8,128)(2,1)} %bitcast.15), calls=%async_computation.2 | async-start | bytes 2097152 | tf_op jit(solution)/shard_map/all_to_all | solution.py:251
  110.2 22.7 %collective-permute-start.3 = (bf16[2032,128]{1,0:T(8,128)(2,1)}, bf16[2032,128]{1,0:T(8,128)(2,1)S(1)}, u32[]{:S(2)}, u32[]{:S(2)}) collective-permute-start(bf16[2032,128]{1,0:T(8,128)(2,1)} %copy-done.18), channel_id=1, source_target_pairs={{0,3},{1,0},{2,1},{3,2},{4,7},{5,4},{6,5},{7,6},{8,11},{9,8},{10,9... | collective-permute-start | bytes 1560584 | tf_op jit(solution)/shard_map/ppermute | solution.py:227
  112.4 34.5 %collective-permute-start.4 = (bf16[2032,128]{1,0:T(8,128)(2,1)}, bf16[2032,128]{1,0:T(8,128)(2,1)S(1)}, u32[]{:S(2)}, u32[]{:S(2)}) collective-permute-start(bf16[2032,128]{1,0:T(8,128)(2,1)} %copy-done.17), channel_id=1, source_target_pairs={{0,2},{1,3},{2,0},{3,1},{4,6},{5,7},{6,4},{7,5},{8,10},{9,11},{10,... | collective-permute-start | bytes 1560584 | tf_op jit(solution)/shard_map/ppermute | solution.py:227
  113.2 33.7 %collective-permute-start.5 = (bf16[2032,128]{1,0:T(8,128)(2,1)}, bf16[2032,128]{1,0:T(8,128)(2,1)S(1)}, u32[]{:S(2)}, u32[]{:S(2)}) collective-permute-start(bf16[2032,128]{1,0:T(8,128)(2,1)} %copy-done.16), channel_id=1, source_target_pairs={{0,1},{1,2},{2,3},{3,0},{4,5},{5,6},{6,7},{7,4},{8,9},{9,10},{10,1... | collective-permute-start | bytes 1560584 | tf_op jit(solution)/shard_map/ppermute | solution.py:227
  147.0 1.0 copy-start.11
  158.0 1.3 copy-start.2
  159.3 1.6 copy-start.3
  160.9 1.6 copy-start.5
  170.7 8.7 %copy-start.19 = (f32[4096]{0:T(1024)S(1)}, f32[4096]{0:T(1024)}, u32[]{:S(2)}) copy-start(f32[4096]{0:T(1024)} %param.9) | copy-start | bytes 49156
  171.4 4.8 %collective-permute-start.7 = (f32[32,128]{1,0:T(8,128)S(1)}, f32[32,128]{1,0:T(8,128)S(1)}, u32[]{:S(2)}, u32[]{:S(2)}) collective-permute-start(f32[32,128]{1,0:T(8,128)S(1)} %bitcast.16), channel_id=1, source_target_pairs={{0,1},{1,2},{2,3},{3,0},{4,5},{5,6},{6,7},{7,4},{8,9},{9,10},{10,1... | collective-permute-start | bytes 49160 | tf_op jit(solution)/shard_map/ppermute | solution.py:227
  172.7 3.7 %collective-permute-start.8 = (f32[32,128]{1,0:T(8,128)S(1)}, f32[32,128]{1,0:T(8,128)S(1)}, u32[]{:S(2)}, u32[]{:S(2)}) collective-permute-start(f32[32,128]{1,0:T(8,128)S(1)} %bitcast.17), channel_id=1, source_target_pairs={{0,3},{1,0},{2,1},{3,2},{4,7},{5,4},{6,5},{7,6},{8,11},{9,8},{10,9... | collective-permute-start | bytes 49160 | tf_op jit(solution)/shard_map/ppermute | solution.py:227
  174.2 5.2 %collective-permute-start.6 = (f32[32,128]{1,0:T(8,128)S(1)}, f32[32,128]{1,0:T(8,128)S(1)}, u32[]{:S(2)}, u32[]{:S(2)}) collective-permute-start(f32[32,128]{1,0:T(8,128)S(1)} %bitcast.18), channel_id=1, source_target_pairs={{0,2},{1,3},{2,0},{3,1},{4,6},{5,7},{6,4},{7,5},{8,10},{9,11},{10,... | collective-permute-start | bytes 49160 | tf_op jit(solution)/shard_map/ppermute | solution.py:227

commit v2 on v0

v2 whole, which is shorter than its diff:
```python
import jax
import jax.numpy as jnp
from jax import lax
from jax.experimental import pallas as pl
from jax.experimental.pallas import tpu as pltpu
from jax.sharding import PartitionSpec as P

learning_rate = 0.3
OWNERS = 64
COLS = 4
PART = 16
BUCKET = COLS * PART
SLOTS = OWNERS * BUCKET
EDGES = OWNERS * PART
WIDTH = 128
FULL = COLS * WIDTH
NEG = 1000
NEG_PAD = 1024
HALF = 512
BLOCK = 256
CHAINS = 4

F32, BF16, I32 = jnp.float32, jnp.bfloat16, jnp.int32
SMEM = pl.BlockSpec(memory_space=pltpu.SMEM)
VMEM = pl.BlockSpec(memory_space=pltpu.VMEM)
HBM = pl.BlockSpec(memory_space=pltpu.HBM)
TABLE = pltpu.VMEM((SLOTS, WIDTH), F32)


def call(body, name, outs, ins, scratch, mib, flops=0, moved=0):
    return pl.pallas_call(
        body,
        out_shape=[shape for shape, _ in outs],
        in_specs=ins,
        out_specs=[spec for _, spec in outs],
        scratch_shapes=scratch,
        compiler_params=pltpu.CompilerParams(vmem_limit_bytes=mib * 1024 * 1024),
        cost_estimate=pl.CostEstimate(flops=flops, bytes_accessed=moved, transcendentals=0),
        name=name,
    )


def shape(rows, dtype, width=WIDTH):
    return jax.ShapeDtypeStruct((rows, width), dtype)


def rows_at(start, count):
    return pl.ds(start, count)


class Copies:
    def __init__(self, sems):
        self.sems, self.all = sems, []

    def start(self, source, target):
        self.all.append(pltpu.make_async_copy(source, target, self.sems.at[len(self.all)]))
        self.all[-1].start()

    def wait(self):
        for copy in self.all:
            copy.wait()


def gather_heads_body(col, src, neg, table, rounded, own, right, left, via_r, via_l, rows, corrupt, o, r, l, vr, vl, sems):
    copies = Copies(sems)
    rounded[...] = table[...].astype(BF16).astype(F32)

    @pl.loop(0, NEG // 40)
    def _(g):
        for i in range(40):
            corrupt[pl.ds(g * 40 + i, 1), :] = table[pl.ds(neg[g * 40 + i], 1), :]

    corrupt[NEG:NEG_PAD, :] = jnp.zeros((NEG_PAD - NEG, WIDTH), F32)
    first, second = corrupt[0:HALF, :].astype(BF16), corrupt[HALF:NEG_PAD, :].astype(BF16)

    @pl.loop(0, OWNERS)
    def _(b):
        for s in (2, 1, 3, 0):
            base = b * BUCKET + ((col[0] + s) & (COLS - 1)) * PART
            for i in range(PART):
                rows[pl.ds(s * EDGES + b * PART + i, 1), :] = table[pl.ds(src[base + i], 1), :]

    vr[0:HALF, :] = rows[2 * EDGES : 2 * EDGES + HALF, :].astype(BF16)
    vr[HALF:, :] = first
    copies.start(vr, via_r)
    vl[0:HALF, :] = rows[2 * EDGES + HALF : 3 * EDGES, :].astype(BF16)
    vl[HALF:, :] = second
    copies.start(vl, via_l)
    r[0:EDGES, :] = rows[EDGES : 2 * EDGES, :].astype(BF16)
    r[EDGES:, :] = second
    copies.start(r, right)
    l[0:EDGES, :] = rows[3 * EDGES :, :].astype(BF16)
    l[EDGES:, :] = first
    copies.start(l, left)
    o[0:EDGES, :] = rows[0:EDGES, :].astype(BF16)
    o[EDGES : EDGES + HALF, :] = first
    o[EDGES + HALF :, :] = second
    copies.start(o, own)
    copies.wait()


def gather_heads(col, src, neg, table):
    sizes = (EDGES + NEG_PAD, EDGES + HALF, EDGES + HALF, 2 * HALF, 2 * HALF)
    return call(
        gather_heads_body,
        "gather_heads",
        [(shape(SLOTS, F32), VMEM)] + [(shape(n, BF16), HBM) for n in sizes],
        [SMEM, SMEM, SMEM, VMEM],
        [TABLE, pltpu.VMEM((NEG_PAD, WIDTH), F32)]
        + [pltpu.VMEM((n, WIDTH), BF16) for n in sizes]
        + [pltpu.SemaphoreType.DMA((5,))],
        60,
        moved=20_000_000,
    )(col, src, neg, table)


def gather_tails_body(wanted, table, relations, out, rows, weighted, sems):
    copies = Copies(sems)
    for k in range(4):

        @pl.loop(k * OWNERS // 4, (k + 1) * OWNERS // 4)
        def _(b):
            for i in range(BUCKET):
                rows[pl.ds(b * BUCKET + i, 1), :] = (
                    table[pl.ds(wanted[b * 2 * BUCKET + i], 1), :]
                    * relations[pl.ds(wanted[b * 2 * BUCKET + BUCKET + i], 1), :]
                )

        part = pl.ds(k * SLOTS // 4, SLOTS // 4)
        weighted[part, :] = rows[part, :].astype(BF16)
        copies.start(weighted.at[part], out.at[part])
    copies.wait()


def gather_tails(wanted, table, relations):
    return call(
        gather_tails_body,
        "gather_tails",
        [(shape(SLOTS, BF16), HBM)],
        [SMEM, VMEM, VMEM],
        [TABLE, pltpu.VMEM((SLOTS, WIDTH), BF16), pltpu.SemaphoreType.DMA((4,))],
        60,
        flops=10_000_000_000,
        moved=20_000_000,
    )(wanted, table, relations)[0]


def gather_factors_body(wanted, relations, out):
    @pl.loop(0, OWNERS)
    def _(b):
        for i in range(BUCKET):
            row = wanted[b * 2 * BUCKET + BUCKET + i]
            out[pl.ds(b * BUCKET + i, 1), :] = relations[pl.ds(row, 1), :]


def gather_factors(wanted, relations):
    return call(
        gather_factors_body,
        "gather_factors",
        [(shape(SLOTS, F32), VMEM)],
        [SMEM, VMEM],
        [],
        60,
        moved=10_000_000,
    )(wanted, relations)[0]


def collect_body(own, dr, vr, dl, vl, wr, wl, heads, corrupt, *rest):
    held, sems = rest[:-1], rest[-1]
    copies = Copies(sems)
    for source, target in zip((own, dr, vr, dl, vl, wr, wl), held):
        copies.start(source, target)
    copies.wait()
    own, dr, vr, dl, vl, wr, wl = held
    span = [slice(s * WIDTH, (s + 1) * WIDTH) for s in range(COLS)]
    heads[:, span[0]] = own[0:EDGES, :]
    heads[:, span[1]] = dr[0:EDGES, :]
    heads[0:HALF, span[2]] = wr[0:HALF, :]
    heads[HALF:, span[2]] = wl[0:HALF, :]
    heads[:, span[3]] = dl[0:EDGES, :]
    corrupt[:, span[0]] = own[EDGES:, :]
    corrupt[0:HALF, span[1]] = vr[HALF:, :]
    corrupt[HALF:, span[1]] = dr[EDGES:, :]
    corrupt[0:HALF, span[2]] = wr[HALF:, :]
    corrupt[HALF:, span[2]] = wl[HALF:, :]
    corrupt[0:HALF, span[3]] = dl[EDGES:, :]
    corrupt[HALF:, span[3]] = vl[HALF:, :]


def collect(pieces):
    return call(
        collect_body,
        "collect",
        [(shape(EDGES, BF16, FULL), VMEM), (shape(NEG_PAD, BF16, FULL), VMEM)],
        [HBM] * 7,
        [pltpu.VMEM(p.shape, BF16) for p in pieces] + [pltpu.SemaphoreType.DMA((7,))],
        60,
        flops=19_000_000_000,
        moved=6_000_000,
    )(*pieces)


def edge_scores_body(col, counts, weighted, heads, corrupt, pulled_out, own, right, left, via_r, via_l, *rest):
    w, grad_scores, pulled, o, r, l, vr, vl, in_sems, out_sems = rest
    owner = [(col[0] + COLS - s) & (COLS - 1) for s in range(COLS)]
    span = [slice(s * WIDTH, (s + 1) * WIDTH) for s in range(COLS)]
    arrivals, copies = Copies(in_sems), Copies(out_sems)
    for s in range(COLS):
        arrivals.start(weighted.at[:, owner[s]], w.at[s])
    arrivals.wait()

    def send(values, at, second, where):
        n = values.shape[0]
        via, via_out = (vl, via_l) if second else (vr, via_r)
        for s, held, out, place in (
            (2, via, via_out, where),
            (1, l, left, at),
            (3, r, right, at),
            (0, o, own, at),
        ):
            held[place : place + n, :] = values[:, span[s]]
            copies.start(held.at[pl.ds(place, n)], out.at[pl.ds(place, n)])

    negatives = corrupt[...]
    slot = lax.broadcasted_iota(I32, (PART, 1), 0) + col[0] * PART
    buckets = BLOCK // PART
    whole = []
    for k in range(EDGES // BLOCK):
        rows = slice(k * BLOCK, (k + 1) * BLOCK)
        live = jnp.concatenate(
            [(slot < counts[0, b]).astype(F32) for b in range(k * buckets, (k + 1) * buckets)], axis=0
        )
        wk = jnp.concatenate(
            [w[s, k * buckets : (k + 1) * buckets].reshape(BLOCK, WIDTH) for s in range(COLS)], axis=1
        )
        whole.append(wk)
        wf, hf = wk.astype(F32), heads[rows, :].astype(F32)
        positive = jnp.sum(hf * wf, axis=1, keepdims=True)
        grad_positive = -live * jax.nn.sigmoid(-positive)
        scores = lax.dot_general(wk, negatives, (((1,), (1,)), ((), ())), preferred_element_type=F32)
        grad = (live * jax.nn.sigmoid(scores) * (1.0 / NEG)).astype(BF16)
        grad_scores[rows, :] = grad
        total = jnp.dot(grad, negatives, preferred_element_type=F32) + grad_positive * hf
        total = total.astype(BF16)
        place = pl.ds(k * buckets, buckets)
        for s in range(COLS):
            pulled[place, owner[s]] = total[:, span[s]].reshape(buckets, PART, WIDTH)
        copies.start(pulled.at[place], pulled_out.at[place])
        send((grad_positive * wf).astype(BF16), k * BLOCK, k * BLOCK >= HALF, k * BLOCK % HALF)
    weights = jnp.concatenate(whole, axis=0)
    for k in range(NEG_PAD // BLOCK):
        total = lax.dot_general(
            grad_scores[:, k * BLOCK : (k + 1) * BLOCK],
            weights,
            (((0,), (0,)), ((), ())),
            preferred_element_type=F32,
        )
        send(total.astype(BF16), EDGES + k * BLOCK, k * BLOCK >= HALF, HALF + k * BLOCK % HALF)
    copies.wait()


def edge_scores(col, counts, weighted, heads, corrupt):
    whole = (OWNERS, COLS, PART, WIDTH)
    sizes = (EDGES + NEG_PAD,) * 3 + (2 * HALF,) * 2
    return call(
        edge_scores_body,
        "edge_scores",
        [(jax.ShapeDtypeStruct(whole, BF16), HBM)] + [(shape(n, BF16), HBM) for n in sizes],
        [SMEM, SMEM, HBM, VMEM, VMEM],
        [
            pltpu.VMEM((COLS, OWNERS, PART, WIDTH), BF16),
            pltpu.VMEM((EDGES, NEG_PAD), BF16),
            pltpu.VMEM(whole, BF16),
        ]
        + [pltpu.VMEM((n, WIDTH), BF16) for n in sizes]
        + [pltpu.SemaphoreType.DMA((COLS,)), pltpu.SemaphoreType.DMA((36,))],
        60,
        flops=3_200_000_000,
        moved=8_000_000,
    )(col, counts, weighted, heads, corrupt)


def begin(tables, start=None):
    for n, table in enumerate(tables):
        if n > 0 or start is None:
            table[...] = jnp.zeros((SLOTS, WIDTH), F32)
        else:
            table[...] = start[...]


def finish(tables):
    total = tables[0][...]
    for table in tables[1:]:
        total += table[...]
    tables[0][...] = total


def scatter_near_body(col, src, g0, g1, g3, out, b0, b1, b3, r0, r1, r3, sems, *tables):
    tables = (out,) + tables
    copies = Copies(sems)
    for source, target in ((g0, b0), (g1, b1), (g3, b3)):
        copies.start(source.at[pl.ds(0, EDGES)], target)
    begin(tables)
    copies.wait()
    for source, target in ((b0, r0), (b1, r1), (b3, r3)):
        target[...] = source[...].astype(F32)

    @pl.loop(0, OWNERS)
    def _(b):
        for i in range(PART):
            for s, rows in ((0, r0), (1, r1), (3, r3)):
                base = b * BUCKET + ((col[0] + s) & (COLS - 1)) * PART
                into = tables[(i * 3 + s) % CHAINS]
                into[pl.ds(src[base + i], 1), :] += rows[pl.ds(b * PART + i, 1), :]

    finish(tables)


def scatter_near(col, src, g0, g1, g3):
    return call(
        scatter_near_body,
        "scatter_near",
        [(shape(SLOTS, F32), VMEM)],
        [SMEM] * 2 + [HBM] * 3,
        [pltpu.VMEM((EDGES, WIDTH), BF16)] * 3
        + [pltpu.VMEM((EDGES, WIDTH), F32)] * 3
        + [pltpu.SemaphoreType.DMA((3,))]
        + [TABLE] * (CHAINS - 1),
        60,
        flops=10_000_000_000,
        moved=20_000_000,
    )(col, src, g0, g1, g3)[0]


def scatter_far_body(col, src, neg, start, g0, g1, g3, wr, wl, out, b0, b1, b3, br, bl, rr, rl, corrupt, sems, *tables):
    tables = (out,) + tables
    copies = Copies(sems)
    copies.start(wr, br)
    copies.start(wl, bl)
    for source, target in ((g0, b0), (g1, b1), (g3, b3)):
        copies.start(source.at[pl.ds(EDGES, NEG_PAD)], target)
    begin(tables, start)
    copies.wait()
    rr[...] = br[0:HALF, :].astype(F32)
    rl[...] = bl[0:HALF, :].astype(F32)
    near = b0[...].astype(F32) + b1[...].astype(F32) + b3[...].astype(F32)
    corrupt[0:HALF, :] = near[0:HALF, :] + br[HALF:, :].astype(F32)
    corrupt[HALF:, :] = near[HALF:, :] + bl[HALF:, :].astype(F32)

    @pl.loop(0, OWNERS // 2)
    def _(b):
        for i in range(PART):
            for n, rows in enumerate((rr, rl)):
                base = (b + n * OWNERS // 2) * BUCKET + ((col[0] + 2) & (COLS - 1)) * PART
                into = tables[(i * 2 + n) % CHAINS]
                into[pl.ds(src[base + i], 1), :] += rows[pl.ds(b * PART + i, 1), :]

    @pl.loop(0, NEG // 40)
    def _(g):
        for i in range(40):
            into = tables[i % CHAINS]
            into[pl.ds(neg[g * 40 + i], 1), :] += corrupt[pl.ds(g * 40 + i, 1), :]

    finish(tables)


def scatter_far(col, src, neg, start, g0, g1, g3, wr, wl):
    return call(
        scatter_far_body,
        "scatter_far",
        [(shape(SLOTS, F32), VMEM)],
        [SMEM] * 3 + [VMEM] + [HBM] * 5,
        [pltpu.VMEM((NEG_PAD, WIDTH), BF16)] * 5
        + [pltpu.VMEM((HALF, WIDTH), F32)] * 2
        + [pltpu.VMEM((NEG_PAD, WIDTH), F32), pltpu.SemaphoreType.DMA((5,))]
        + [TABLE] * (CHAINS - 1),
        60,
        flops=10_000_000_000,
        moved=20_000_000,
    )(col, src, neg, start, g0, g1, g3, wr, wl)[0]


def scatter_tails_body(wanted, start, factors, pulled, out, held, rows, sems, *tables):
    tables = (out,) + tables
    copies = Copies(sems)
    copies.start(pulled, held)
    begin(tables, start)
    copies.wait()
    rows[...] = factors[...] * held[...].astype(F32)

    @pl.loop(0, OWNERS)
    def _(b):
        for i in range(BUCKET):
            into = tables[i % CHAINS]
            into[pl.ds(wanted[b * 2 * BUCKET + i], 1), :] += rows[pl.ds(b * BUCKET + i, 1), :]

    finish(tables)


def scatter_tails(wanted, start, factors, pulled):
    return call(
        scatter_tails_body,
        "scatter_tails",
        [(shape(SLOTS, F32), VMEM)],
        [SMEM] + [VMEM] * 2 + [HBM],
        [pltpu.VMEM((SLOTS, WIDTH), BF16), TABLE, pltpu.SemaphoreType.DMA((1,))] + [TABLE] * (CHAINS - 1),
        60,
        moved=30_000_000,
    )(wanted, start, factors, pulled)[0]


def shifted(x, s):
    return lax.ppermute(x, "col", [(i, (i + s) % COLS) for i in range(COLS)])


def exchanged(right, left, via_r, via_l):
    vr, vl = shifted(via_r, 1), shifted(via_l, -1)
    dr, dl = shifted(right, 1), shifted(left, -1)
    return dr, vr, dl, vl, shifted(vr, 1), shifted(vl, -1)


def shards(
    embeddings, adagrad_state, relations, src_rows, dst_rows, rel_ids, bucket_counts, neg_rows
):
    axes = ("dom", "col")
    col = lax.axis_index("col").astype(I32).reshape(1)

    def sent(x):
        return lax.all_to_all(
            x.reshape(OWNERS * COLS, PART, WIDTH), axes, split_axis=0, concat_axis=0, tiled=True
        )

    words = jnp.concatenate([dst_rows.reshape(OWNERS, BUCKET), rel_ids.reshape(OWNERS, BUCKET)], axis=1)
    wanted = lax.all_to_all(words, "dom", split_axis=0, concat_axis=0, tiled=True).reshape(2 * SLOTS)
    rounded, own, *outgoing = gather_heads(col, src_rows, neg_rows, embeddings)
    weighted = sent(gather_tails(wanted, rounded, relations))
    heads, corrupt = collect([own, *exchanged(*outgoing)])
    pulled, own, *outgoing = edge_scores(
        col, bucket_counts, weighted.reshape(OWNERS, COLS, PART, WIDTH), heads, corrupt
    )
    pulled = sent(pulled).reshape(SLOTS, WIDTH)
    from_left, _, from_right, _, far_a, far_b = exchanged(*outgoing)
    gradient = scatter_near(col, src_rows, own, from_right, from_left)
    gradient = scatter_far(col, src_rows, neg_rows, gradient, own, from_right, from_left, far_a, far_b)
    gradient = scatter_tails(wanted, gradient, gather_factors(wanted, relations), pulled)

    squares = jnp.sum(gradient * gradient, axis=1).reshape(-1, WIDTH)
    squares = (squares + shifted(squares, 2)) + (shifted(squares, 1) + shifted(squares, 3))
    new_state = adagrad_state + squares.reshape(-1) / FULL
    new_embeddings = embeddings - learning_rate * gradient / jnp.sqrt(new_state)[:, None]
    return (new_embeddings, new_state)


def solution(mesh):
    placed = (
        P("dom", "col"),
        P("dom"),
        P(None, "col"),
        P("dom"),
        P("dom"),
        P("dom"),
        P("dom", None),
        P("dom"),
    )
    return jax.shard_map(
        shards, mesh=mesh, in_specs=placed, out_specs=(P("dom", "col"), P("dom")), check_vma=False
    )
```

time: 314 us -> 161 us (0.51)
  blocking collectives: 85.7 us -> 0 us
  other arithmetic: 73 us -> 5.35 us
  Pallas kernels: 0 us -> 62.6 us
  local copies, waits for them, and re-layouts: 49 us -> 6.59 us
  starting transfers between devices: 13.9 us -> 50.1 us
  waiting for transfers between devices: 58.8 us -> 35.1 us
  matrix products: 18.6 us -> 0 us
  between operations: 14.3 us -> 0.86 us
    pallas_call x0 -> x8, Pallas kernels: none -> 62.6 us  [the longest x1 10.9 us: scatter_tails(): call(scatter_tails_body, 'scatter_tails', [(shape(SLOTS, F32), VMEM)], [S...]
    scatter-add x3 -> x0, other arithmetic: 59.9 us -> none  [the longest x2 35.9 us: shards(): gradient.at[src_rows].add(grad_head).at[neg_rows].add(grad_corrupt)]
    gather x4 -> x0, local copies, waits for them, and re-layouts: 47.3 us -> none  [the longest x1 15.8 us: shards(): embeddings[wanted.reshape(-1)].astype(jnp.bfloat16)]
    all_to_all x2 -> x3, waiting for transfers between devices: 58.7 us -> 14.3 us  [the longest x2 14.3 us: sent(): lax.all_to_all(x.reshape(OWNERS * COLS, PART, WIDTH), axes, split_axis=0,...]
    all_gather x1 -> x0, blocking collectives: 32.8 us -> none  [shards(): lax.all_gather(corrupt_rows, 'col', axis=1, tiled=True)]
    psum x2 -> x0, blocking collectives: 31.7 us -> none  [the longest x1 16.2 us: shards(): positive = lax.psum(pos_partial, 'col')]
    all_to_all x1 -> x0, blocking collectives: 21.2 us -> none  [shards(): lax.all_to_all(requests, 'dom', split_axis=0, concat_axis=0, tiled=True)]
    ppermute x0 -> x15, waiting for transfers between devices: none -> 20.8 us  [shifted(): return lax.ppermute(x, 'col', [(i, (i + s) % COLS) for i in range(COLS)])]
  transfers between devices with their start and end apart: 3 -> 18, of which waited for: 2 -> 9; matrix products, arithmetic and copies ran while one was open for 13% -> 0% of each run, Pallas kernels for 0% -> 27%
where the time goes in v2:
time: 161 us
  Pallas kernels  62.6 us (39%)
  starting transfers between devices  50.1 us (31%)
  waiting for transfers between devices  35.1 us (22%)
  local copies, waits for them, and re-layouts  6.59 us (4%)
  other arithmetic  5.35 us (3%)
    ppermute x15, waiting for transfers between devices, shifted(): return lax.ppermute(x, 'col', [(i, (i + s) % COLS) for i in range(COLS)])  20.8 us
    all_to_all x2, starting transfers between devices, sent(): lax.all_to_all(x.reshape(OWNERS * COLS, PART, WIDTH), axes, split_axis=0,...  20.7 us
    ppermute x15, starting transfers between devices, shifted(): return lax.ppermute(x, 'col', [(i, (i + s) % COLS) for i in range(COLS)])  17.4 us
    all_to_all x2, waiting for transfers between devices, sent(): lax.all_to_all(x.reshape(OWNERS * COLS, PART, WIDTH), axes, split_axis=0,...  14.3 us
    all_to_all x1, starting transfers between devices, shards(): lax.all_to_all(words, 'dom', split_axis=0, concat_axis=0, tiled=True)  11.9 us
    pallas_call x1, Pallas kernels, scatter_tails(): call(scatter_tails_body, 'scatter_tails', [(shape(SLOTS, F32), VMEM)], [S...  10.9 us
    pallas_call x1, Pallas kernels, gather_tails(): call(gather_tails_body, 'gather_tails', [(shape(SLOTS, BF16), HBM)], [SME...  9.41 us
    pallas_call x1, Pallas kernels, gather_heads(): call(gather_heads_body, 'gather_heads', [(shape(SLOTS, F32), VMEM)] + [(s...  9.16 us
  transfers between devices with their start and end apart: 18, of which 9 were waited for; matrix products, arithmetic and copies ran while one was open for 0% of the time, Pallas kernels for 27%

profile of v2, /device:TPU:8, one launch (start us, length us, event | category | flops | bytes accessed | tf_op | source)
XLA Modules:
  0.0 160.6 jit_solution(5889229352375281723)
XLA Ops:
  0.6 0.8 reshape.38
  1.4 0.8 reshape.39
  2.2 0.7 pad_add_fusion
  2.9 11.9 %all-to-all-start = ((s32[64,1,128]{2,1,0:T(1,128)}), s32[64,1,128]{2,1,0:T(1,128)S(1)}, u32[]{:S(2)}, u32[]{:S(2)}) async-start(s32[64,1,128]{2,1,0:T(1,128)} %bitcast), calls=%async_computation | async-start | bytes 65536 | tf_op jit(solution)/shard_map/all_to_all | solution.py:434
  14.8 9.2 %gather_heads.1 = (f32[4096,128]{1,0:T(8,128)}, bf16[2048,128]{1,0:T(8,128)(2,1)}, bf16[1536,128]{1,0:T(8,128)(2,1)}, bf16[1536,128]{1,0:T(8,128)(2,1)}, bf16[10...) custom-call(s32[1]{0:T(128)} %bitcast.2.col, s32[4096]{0:T(1024)} %src.5, s32[1000]{0:T(1024)} %neg.3, f32[4096,128]{1,0:T(8,128)} %table.1), custom_call_target="tpu_custom_call" | custom-call | bytes 20000000 | tf_op jit(solution)/shard_map/gather_heads/pallas_call | solution.py:104
  24.0 1.7 %collective-permute-start.1 = (bf16[1024,128]{1,0:T(8,128)(2,1)}, bf16[1024,128]{1,0:T(8,128)(2,1)S(1)}, u32[]{:S(2)}, u32[]{:S(2)}) collective-permute-start(bf16[1024,128]{1,0:T(8,128)(2,1)} %get-tuple-element.19), channel_id=1, source_target_pairs={{0,1},{1,2},{2,3},{3,0},{4,5},{5,6},{6,7},{7,4},{8,9},{9,10},{10,1... | collective-permute-start | bytes 786440 | tf_op jit(solution)/shard_map/ppermute | solution.py:413
  25.7 0.4 collective-permute-start.3
  26.1 1.6 collective-permute-start
  27.7 0.4 collective-permute-start.2
  28.1 0.6 copy-done.4
  28.8 9.4 %gather_tails.1 = bf16[4096,128]{1,0:T(8,128)(2,1)} custom-call(s32[8192]{0:T(1024)} %bitcast.17, f32[4096,128]{1,0:T(8,128)} %get-tuple-element.16.table, f32[1345,128]{1,0:T(8,128)} %relations.3), custom_call_target="tpu_custom_call" | custom-call | flops 10000000000 | bytes 20000000 | tf_op jit(solution)/shard_map/gather_tails/pallas_call | solution.py:136
  38.2 13.0 %all-to-all-start.1 = ((bf16[256,16,128]{2,1,0:T(8,128)(2,1)}), bf16[256,16,128]{2,1,0:T(8,128)(2,1)S(1)}, u32[]{:S(2)}, u32[]{:S(2)}) async-start(bf16[256,16,128]{2,1,0:T(8,128)(2,1)} %bitcast.16), calls=%async_computation.1 | async-start | bytes 2097152 | tf_op jit(solution)/shard_map/all_to_all | solution.py:429
  51.2 1.5 collective-permute-start.4
  52.8 0.8 collective-permute-start.5
  53.6 10.0 %collective-permute-done.4.wr = bf16[1024,128]{1,0:T(8,128)(2,1)S(1)} collective-permute-done((bf16[1024,128]{1,0:T(8,128)(2,1)S(1)}, bf16[1024,128]{1,0:T(8,128)(2,1)S(1)}, u32[]{:S(2)}, u32[]{:S(2)}) %collective-permute-start.4) | collective-permute-done | bytes 262176 | tf_op jit(solution)/shard_map/ppermute | solution.py:413
  63.6 1.1 collective-permute-done.5.wl
  64.8 0.7 copy-done.14
  65.5 3.3 %collect.1 = (bf16[1024,512]{1,0:T(8,128)(2,1)}, bf16[1024,512]{1,0:T(8,128)(2,1)}) custom-call(bf16[2048,128]{1,0:T(8,128)(2,1)} %get-tuple-element.17.own, bf16[1536,128]{1,0:T(8,128)(2,1)} %copy-done.8, bf16[1024,128]{1,0:T(8,128)(2,1)} %copy-done.10, bf16[1536,128]{1,0:T(8,128)(2,1)} %copy-done.9, bf16[1024,128]{1,0:T(8,128)(2,1)} %copy-done.11, ...), custom_call_target="tpu_custom_call" | custom-call | flops 19000000512 | bytes 6000000 | tf_op jit(solution)/shard_map/collect/pallas_call | solution.py:191
  68.8 14.3 %all-to-all-done.1 = bf16[256,16,128]{2,1,0:T(8,128)(2,1)S(1)} async-done(((bf16[256,16,128]{2,1,0:T(8,128)(2,1)}), bf16[256,16,128]{2,1,0:T(8,128)(2,1)S(1)}, u32[]{:S(2)}, u32[]{:S(2)}) %all-to-all-start.1) | async-done | bytes 1048608 | tf_op jit(solution)/shard_map/all_to_all | solution.py:429
  83.0 1.0 copy-done.3
  84.0 7.6 %edge_scores.1 = (bf16[64,4,16,128]{3,2,1,0:T(8,128)(2,1)}, bf16[2048,128]{1,0:T(8,128)(2,1)}, bf16[2048,128]{1,0:T(8,128)(2,1)}, bf16[2048,128]{1,0:T(8,128)(2,...) custom-call(s32[1]{0:T(128)} %bitcast.2.col, s32[1,64]{1,0:T(1,128)} %counts.1, ...), custom_call_target="tpu_custom_call" | custom-call | flops 3200000000 | bytes 8000000 | tf_op jit(solution)/shard_map/edge_scores/pallas_call | solution.py:265
  91.7 1.6 %collective-permute-start.6 = (bf16[2048,128]{1,0:T(8,128)(2,1)}, bf16[2048,128]{1,0:T(8,128)(2,1)S(1)}, u32[]{:S(2)}, u32[]{:S(2)}) collective-permute-start(bf16[2048,128]{1,0:T(8,128)(2,1)} %get-tuple-element.25), channel_id=1, source_target_pairs={{0,3},{1,0},{2,1},{3,2},{4,7},{5,4},{6,5},{7,6},{8,11},{9,8},{10,9... | collective-permute-start | bytes 1572872 | tf_op jit(solution)/shard_map/ppermute | solution.py:413
  93.3 0.7 collective-permute-start.7
  93.9 1.4 collective-permute-start.10
  95.3 0.7 collective-permute-start.8
  96.0 7.7 %all-to-all-start.2 = ((bf16[256,16,128]{2,1,0:T(8,128)(2,1)}), bf16[256,16,128]{2,1,0:T(8,128)(2,1)S(1)}, u32[]{:S(2)}, u32[]{:S(2)}) async-start(bf16[256,16,128]{2,1,0:T(8,128)(2,1)} %bitcast.14), calls=%async_computation.2 | async-start | bytes 2097152 | tf_op jit(solution)/shard_map/all_to_all | solution.py:429
  103.7 6.1 %gather_factors.1.factors = f32[4096,128]{1,0:T(8,128)} custom-call(s32[8192]{0:T(1024)} %bitcast.18, f32[1345,128]{1,0:T(8,128)} %relations.3), custom_call_target="tpu_custom_call" | custom-call | bytes 10000000 | tf_op jit(solution)/shard_map/gather_factors/pallas_call | solution.py:157
  109.8 5.4 %collective-permute-done.10 = bf16[1024,128]{1,0:T(8,128)(2,1)S(1)} collective-permute-done((bf16[1024,128]{1,0:T(8,128)(2,1)}, bf16[1024,128]{1,0:T(8,128)(2,1)S(1)}, u32[]{:S(2)}, u32[]{:S(2)}) %collective-permute-start.10) | collective-permute-done | bytes 262176 | tf_op jit(solution)/shard_map/ppermute | solution.py:413
  115.2 2.0 %collective-permute-start.11 = (bf16[1024,128]{1,0:T(8,128)(2,1)S(1)}, bf16[1024,128]{1,0:T(8,128)(2,1)S(1)}, u32[]{:S(2)}, u32[]{:S(2)}) collective-permute-start(bf16[1024,128]{1,0:T(8,128)(2,1)S(1)} %collective-permute-done.10), channel_id=1, source_target_pairs={{0,3},{1,0},{2,1},{3,2},{4,7},{5,4},{6,5},{7,6},{8,11},{9,8},{10,9... | collective-permute-start | bytes 786440 | tf_op jit(solution)/shard_map/ppermute | solution.py:413
  117.3 0.8 collective-permute-done.8
  118.2 0.8 copy-done.6
  119.0 0.2 copy-done.7
  119.1 8.4 %scatter_near.1.start = f32[4096,128]{1,0:T(8,128)} custom-call(s32[1]{0:T(128)} %bitcast.2.col, s32[4096]{0:T(1024)} %src.5, bf16[2048,128]{1,0:T(8,128)(2,1)} %get-tuple-element.24.g0, bf16[2048,128]{1,0:T(8,128)(2,1)} %copy-done.6, bf16[2048,128]{1,0:T(8,128)(2,1)} %copy-done.7), custom_call_target="tpu_custom_call" | custom-call | flops 10000000000 | bytes 20000000 | tf_op jit(solution)/shard_map/scatter_near/pallas_call | solution.py:320
  127.6 0.7 collective-permute-done.9.wr
  128.3 0.0 copy-done.13
  128.3 0.7 copy-done.15
  129.0 7.6 %scatter_far.1.start = f32[4096,128]{1,0:T(8,128)} custom-call(s32[1]{0:T(128)} %bitcast.2.col, s32[4096]{0:T(1024)} %src.5, s32[1000]{0:T(1024)} %neg.3, f32[4096,128]{1,0:T(8,128)} %scatter_near.1.start, bf16[2048,128]{1,0:T(8,128)(2,1)} %get-tuple-element.24.g0, bf16[2048,128]{1,0:T(8,128)(2,1)} %copy-done.6, bf16[2048,128]{1,0:T(8,128)(2,1)} %copy-done.7, ...), custom_call_target="tpu_custom_call" | custom-call | flops 10000000000 | bytes 20000000 | tf_op jit(solution)/shard_map/scatter_far/pallas_call | solution.py:368
  136.6 1.0 copy-done.2
  137.6 10.9 %scatter_tails.1 = f32[4096,128]{1,0:T(8,128)} custom-call(s32[8192]{0:T(1024)} %bitcast.19, f32[4096,128]{1,0:T(8,128)} %scatter_far.1.start, f32[4096,128]{1,0:T(8,128)} %gather_factors.1.factors, bf16[4096,128]{1,0:T(8,128)(2,1)} %bitcast.13), custom_call_target="tpu_custom_call" | custom-call | bytes 30000000 | tf_op jit(solution)/shard_map/scatter_tails/pallas_call | solution.py:401
  148.6 2.4 %multiply_reduce_fusion = f32[4096]{0:T(1024)S(1)} fusion(f32[4096,128]{1,0:T(8,128)} %scatter_tails.1), kind=kLoop, calls=%fused_computation.1 | loop fusion | flops 1044480 | bytes 2113536 | tf_op jit(solution)/shard_map/reduce_sum | solution.py:447
  150.9 2.6 %collective-permute-start.12 = (f32[32,128]{1,0:T(8,128)S(1)}, f32[32,128]{1,0:T(8,128)S(1)}, u32[]{:S(2)}, u32[]{:S(2)}) collective-permute-start(f32[32,128]{1,0:T(8,128)S(1)} %bitcast.20), channel_id=1, source_target_pairs={{0,2},{1,3},{2,0},{3,1},{4,6},{5,7},{6,4},{7,5},{8,10},{9,11},{10,... | collective-permute-start | bytes 49160 | tf_op jit(solution)/shard_map/ppermute | solution.py:413
  153.5 1.0 collective-permute-start.13
  154.5 1.0 collective-permute-start.14
  155.5 0.7 collective-permute-done.12
  156.3 1.0 collective-permute-done.13
  157.3 1.0 collective-permute-done.14
  158.3 0.6 fusion
  158.9 1.7 %divide_subtract_fusion = f32[4096,128]{1,0:T(8,128)} fusion(f32[4096,128]{1,0:T(8,128)S(1)} %copy-done.1, f32[4096,128]{1,0:T(8,128)S(1)} %copy-done, f32[4096]{0:T(1024)S(1)} %get-tuple-element.30), kind=kLoop, calls=%fused_computation | loop fusion | flops 1572864 | bytes 6307840 | tf_op jit(solution)/shard_map/sub | solution.py:450
  (34 shorter events, 0.1 us)
Async XLA Ops:
  2.9 25.2 %all-to-all-start = ((s32[64,1,128]{2,1,0:T(1,128)}), s32[64,1,128]{2,1,0:T(1,128)S(1)}, u32[]{:S(2)}, u32[]{:S(2)}) async-start(s32[64,1,128]{2,1,0:T(1,128)} %bitcast), calls=%async_computation | async-start | bytes 65536 | tf_op jit(solution)/shard_map/all_to_all | solution.py:434
  24.0 27.2 %collective-permute-start.1 = (bf16[1024,128]{1,0:T(8,128)(2,1)}, bf16[1024,128]{1,0:T(8,128)(2,1)S(1)}, u32[]{:S(2)}, u32[]{:S(2)}) collective-permute-start(bf16[1024,128]{1,0:T(8,128)(2,1)} %get-tuple-element.19), channel_id=1, source_target_pairs={{0,1},{1,2},{2,3},{3,0},{4,5},{5,6},{6,7},{7,4},{8,9},{9,10},{10,1... | collective-permute-start | bytes 786440 | tf_op jit(solution)/shard_map/ppermute | solution.py:413
  25.7 27.1 %collective-permute-start.3 = (bf16[1024,128]{1,0:T(8,128)(2,1)}, bf16[1024,128]{1,0:T(8,128)(2,1)S(1)}, u32[]{:S(2)}, u32[]{:S(2)}) collective-permute-start(bf16[1024,128]{1,0:T(8,128)(2,1)} %get-tuple-element.21), channel_id=1, source_target_pairs={{0,3},{1,0},{2,1},{3,2},{4,7},{5,4},{6,5},{7,6},{8,11},{9,8},{10,9... | collective-permute-start | bytes 786440 | tf_op jit(solution)/shard_map/ppermute | solution.py:413
  26.1 27.4 %collective-permute-start = (bf16[1536,128]{1,0:T(8,128)(2,1)}, bf16[1536,128]{1,0:T(8,128)(2,1)S(1)}, u32[]{:S(2)}, u32[]{:S(2)}) collective-permute-start(bf16[1536,128]{1,0:T(8,128)(2,1)} %get-tuple-element.18), channel_id=1, source_target_pairs={{0,1},{1,2},{2,3},{3,0},{4,5},{5,6},{6,7},{7,4},{8,9},{9,10},{10,1... | collective-permute-start | bytes 1179656 | tf_op jit(solution)/shard_map/ppermute | solution.py:413
  27.7 25.9 %collective-permute-start.2 = (bf16[1536,128]{1,0:T(8,128)(2,1)}, bf16[1536,128]{1,0:T(8,128)(2,1)S(1)}, u32[]{:S(2)}, u32[]{:S(2)}) collective-permute-start(bf16[1536,128]{1,0:T(8,128)(2,1)} %get-tuple-element.20), channel_id=1, source_target_pairs={{0,3},{1,0},{2,1},{3,2},{4,7},{5,4},{6,5},{7,6},{8,11},{9,8},{10,9... | collective-permute-start | bytes 1179656 | tf_op jit(solution)/shard_map/ppermute | solution.py:413
  28.1 0.6 copy-start.4
  38.2 44.9 %all-to-all-start.1 = ((bf16[256,16,128]{2,1,0:T(8,128)(2,1)}), bf16[256,16,128]{2,1,0:T(8,128)(2,1)S(1)}, u32[]{:S(2)}, u32[]{:S(2)}) async-start(bf16[256,16,128]{2,1,0:T(8,128)(2,1)} %bitcast.16), calls=%async_computation.1 | async-start | bytes 2097152 | tf_op jit(solution)/shard_map/all_to_all | solution.py:429
  51.2 13.5 %copy-start.10 = (bf16[1024,128]{1,0:T(8,128)(2,1)}, bf16[1024,128]{1,0:T(8,128)(2,1)S(1)}, u32[]{:S(2)}) copy-start(bf16[1024,128]{1,0:T(8,128)(2,1)S(1)} %collective-permute-done.1.vr) | copy-start | bytes 786436
  51.2 12.4 %collective-permute-start.4 = (bf16[1024,128]{1,0:T(8,128)(2,1)S(1)}, bf16[1024,128]{1,0:T(8,128)(2,1)S(1)}, u32[]{:S(2)}, u32[]{:S(2)}) collective-permute-start(bf16[1024,128]{1,0:T(8,128)(2,1)S(1)} %collective-permute-done.1.vr), channel_id=1, source_target_pairs={{0,1},{1,2},{2,3},{3,0},{4,5},{5,6},{6,7},{7,4},{8,9},{9,10},{10,1... | collective-permute-start | bytes 786440 | tf_op jit(solution)/shard_map/ppermute | solution.py:413
  52.8 12.0 %copy-start.11 = (bf16[1024,128]{1,0:T(8,128)(2,1)}, bf16[1024,128]{1,0:T(8,128)(2,1)S(1)}, u32[]{:S(2)}) copy-start(bf16[1024,128]{1,0:T(8,128)(2,1)S(1)} %collective-permute-done.3.vl) | copy-start | bytes 786436
  52.8 12.0 %collective-permute-start.5 = (bf16[1024,128]{1,0:T(8,128)(2,1)S(1)}, bf16[1024,128]{1,0:T(8,128)(2,1)S(1)}, u32[]{:S(2)}, u32[]{:S(2)}) collective-permute-start(bf16[1024,128]{1,0:T(8,128)(2,1)S(1)} %collective-permute-done.3.vl), channel_id=1, source_target_pairs={{0,3},{1,0},{2,1},{3,2},{4,7},{5,4},{6,5},{7,6},{8,11},{9,8},{10,9... | collective-permute-start | bytes 786440 | tf_op jit(solution)/shard_map/ppermute | solution.py:413
  53.5 11.2 %copy-start.8 = (bf16[1536,128]{1,0:T(8,128)(2,1)}, bf16[1536,128]{1,0:T(8,128)(2,1)S(1)}, u32[]{:S(2)}) copy-start(bf16[1536,128]{1,0:T(8,128)(2,1)S(1)} %collective-permute-done.dr) | copy-start | bytes 1179652
  53.6 11.2 %copy-start.9 = (bf16[1536,128]{1,0:T(8,128)(2,1)}, bf16[1536,128]{1,0:T(8,128)(2,1)S(1)}, u32[]{:S(2)}) copy-start(bf16[1536,128]{1,0:T(8,128)(2,1)S(1)} %collective-permute-done.2.dl) | copy-start | bytes 1179652
  63.6 1.2 copy-start.12
  64.7 0.7 copy-start.14
  83.0 1.0 copy-start.3
  91.7 26.5 %collective-permute-start.6 = (bf16[2048,128]{1,0:T(8,128)(2,1)}, bf16[2048,128]{1,0:T(8,128)(2,1)S(1)}, u32[]{:S(2)}, u32[]{:S(2)}) collective-permute-start(bf16[2048,128]{1,0:T(8,128)(2,1)} %get-tuple-element.25), channel_id=1, source_target_pairs={{0,3},{1,0},{2,1},{3,2},{4,7},{5,4},{6,5},{7,6},{8,11},{9,8},{10,9... | collective-permute-start | bytes 1572872 | tf_op jit(solution)/shard_map/ppermute | solution.py:413
  93.3 24.9 %collective-permute-start.7 = (bf16[2048,128]{1,0:T(8,128)(2,1)}, bf16[2048,128]{1,0:T(8,128)(2,1)S(1)}, u32[]{:S(2)}, u32[]{:S(2)}) collective-permute-start(bf16[2048,128]{1,0:T(8,128)(2,1)} %get-tuple-element.26), channel_id=1, source_target_pairs={{0,1},{1,2},{2,3},{3,0},{4,5},{5,6},{6,7},{7,4},{8,9},{9,10},{10,1... | collective-permute-start | bytes 1572872 | tf_op jit(solution)/shard_map/ppermute | solution.py:413
  93.9 21.3 %collective-permute-start.10 = (bf16[1024,128]{1,0:T(8,128)(2,1)}, bf16[1024,128]{1,0:T(8,128)(2,1)S(1)}, u32[]{:S(2)}, u32[]{:S(2)}) collective-permute-start(bf16[1024,128]{1,0:T(8,128)(2,1)} %get-tuple-element.28), channel_id=1, source_target_pairs={{0,3},{1,0},{2,1},{3,2},{4,7},{5,4},{6,5},{7,6},{8,11},{9,8},{10,9... | collective-permute-start | bytes 786440 | tf_op jit(solution)/shard_map/ppermute | solution.py:413
  95.3 22.8 %collective-permute-start.8 = (bf16[1024,128]{1,0:T(8,128)(2,1)}, bf16[1024,128]{1,0:T(8,128)(2,1)S(1)}, u32[]{:S(2)}, u32[]{:S(2)}) collective-permute-start(bf16[1024,128]{1,0:T(8,128)(2,1)} %get-tuple-element.27), channel_id=1, source_target_pairs={{0,1},{1,2},{2,3},{3,0},{4,5},{5,6},{6,7},{7,4},{8,9},{9,10},{10,1... | collective-permute-start | bytes 786440 | tf_op jit(solution)/shard_map/ppermute | solution.py:413
  96.0 40.6 %all-to-all-start.2 = ((bf16[256,16,128]{2,1,0:T(8,128)(2,1)}), bf16[256,16,128]{2,1,0:T(8,128)(2,1)S(1)}, u32[]{:S(2)}, u32[]{:S(2)}) async-start(bf16[256,16,128]{2,1,0:T(8,128)(2,1)} %bitcast.14), calls=%async_computation.2 | async-start | bytes 2097152 | tf_op jit(solution)/shard_map/all_to_all | solution.py:429
  115.2 12.3 %collective-permute-start.11 = (bf16[1024,128]{1,0:T(8,128)(2,1)S(1)}, bf16[1024,128]{1,0:T(8,128)(2,1)S(1)}, u32[]{:S(2)}, u32[]{:S(2)}) collective-permute-start(bf16[1024,128]{1,0:T(8,128)(2,1)S(1)} %collective-permute-done.10), channel_id=1, source_target_pairs={{0,3},{1,0},{2,1},{3,2},{4,7},{5,4},{6,5},{7,6},{8,11},{9,8},{10,9... | collective-permute-start | bytes 786440 | tf_op jit(solution)/shard_map/ppermute | solution.py:413
  118.1 10.1 %collective-permute-start.9 = (bf16[1024,128]{1,0:T(8,128)(2,1)S(1)}, bf16[1024,128]{1,0:T(8,128)(2,1)S(1)}, u32[]{:S(2)}, u32[]{:S(2)}) collective-permute-start(bf16[1024,128]{1,0:T(8,128)(2,1)S(1)} %collective-permute-done.8), channel_id=1, source_target_pairs={{0,1},{1,2},{2,3},{3,0},{4,5},{5,6},{6,7},{7,4},{8,9},{9,10},{10,1... | collective-permute-start | bytes 786440 | tf_op jit(solution)/shard_map/ppermute | solution.py:413
  118.1 0.8 copy-start.6
  118.2 1.0 copy-start.7
  127.6 0.7 copy-start.13
  128.3 0.7 copy-start.15
  136.6 1.0 copy-start.2
  137.6 21.3 %copy-start.1 = (f32[4096,128]{1,0:T(8,128)S(1)}, f32[4096,128]{1,0:T(8,128)}, u32[]{:S(2)}) copy-start(f32[4096,128]{1,0:T(8,128)} %table.1) | copy-start | bytes 6291460
  148.6 9.7 %copy-start.5 = (f32[4096]{0:T(1024)S(1)}, f32[4096]{0:T(1024)}, u32[]{:S(2)}) copy-start(f32[4096]{0:T(1024)} %param.9) | copy-start | bytes 49156
  148.6 10.3 %copy-start = (f32[4096,128]{1,0:T(8,128)S(1)}, f32[4096,128]{1,0:T(8,128)}, u32[]{:S(2)}) copy-start(f32[4096,128]{1,0:T(8,128)} %scatter_tails.1) | copy-start | bytes 6291460
  150.9 5.3 %collective-permute-start.12 = (f32[32,128]{1,0:T(8,128)S(1)}, f32[32,128]{1,0:T(8,128)S(1)}, u32[]{:S(2)}, u32[]{:S(2)}) collective-permute-start(f32[32,128]{1,0:T(8,128)S(1)} %bitcast.20), channel_id=1, source_target_pairs={{0,2},{1,3},{2,0},{3,1},{4,6},{5,7},{6,4},{7,5},{8,10},{9,11},{10,... | collective-permute-start | bytes 49160 | tf_op jit(solution)/shard_map/ppermute | solution.py:413
  153.5 3.7 %collective-permute-start.13 = (f32[32,128]{1,0:T(8,128)S(1)}, f32[32,128]{1,0:T(8,128)S(1)}, u32[]{:S(2)}, u32[]{:S(2)}) collective-permute-start(f32[32,128]{1,0:T(8,128)S(1)} %bitcast.21), channel_id=1, source_target_pairs={{0,1},{1,2},{2,3},{3,0},{4,5},{5,6},{6,7},{7,4},{8,9},{9,10},{10,1... | collective-permute-start | bytes 49160 | tf_op jit(solution)/shard_map/ppermute | solution.py:413
  154.5 3.7 %collective-permute-start.14 = (f32[32,128]{1,0:T(8,128)S(1)}, f32[32,128]{1,0:T(8,128)S(1)}, u32[]{:S(2)}, u32[]{:S(2)}) collective-permute-start(f32[32,128]{1,0:T(8,128)S(1)} %bitcast.22), channel_id=1, source_target_pairs={{0,3},{1,0},{2,1},{3,2},{4,7},{5,4},{6,5},{7,6},{8,11},{9,8},{10,9... | collective-permute-start | bytes 49160 | tf_op jit(solution)/shard_map/ppermute | solution.py:413

commit v3 on v2

v3 whole, which is shorter than its diff:
```python
import jax
import jax.numpy as jnp
from jax import lax
from jax.experimental import pallas as pl
from jax.experimental.pallas import tpu as pltpu
from jax.sharding import PartitionSpec as P

learning_rate = 0.3
OWNERS = 64
COLS = 4
PART = 16
BUCKET = COLS * PART
SLOTS = OWNERS * BUCKET
EDGES = OWNERS * PART
WIDTH = 128
FULL = COLS * WIDTH
NEG = 1000
NEG_PAD = 1024
DIRECT = EDGES + NEG_PAD
HALF = 512
BLOCK = 256
CHAINS = 4
WHOLE = 65_300

F32, BF16, I32 = jnp.float32, jnp.bfloat16, jnp.int32
SMEM = pl.BlockSpec(memory_space=pltpu.SMEM)
VMEM = pl.BlockSpec(memory_space=pltpu.VMEM)
HBM = pl.BlockSpec(memory_space=pltpu.HBM)
TABLE = pltpu.VMEM((SLOTS, WIDTH), F32)


def call(body, name, outs, ins, scratch, kib=WHOLE, flops=0, moved=0):
    return pl.pallas_call(
        body,
        out_shape=[shape for shape, _ in outs],
        in_specs=ins,
        out_specs=[spec for _, spec in outs],
        scratch_shapes=scratch,
        compiler_params=pltpu.CompilerParams(vmem_limit_bytes=kib * 1024),
        cost_estimate=pl.CostEstimate(flops=flops, bytes_accessed=moved, transcendentals=0),
        name=name,
    )


def shape(rows, dtype, width=WIDTH):
    return jax.ShapeDtypeStruct((rows, width), dtype)


def rows_at(start, count):
    return pl.ds(start, count)


class Copies:
    def __init__(self, sems):
        self.sems, self.all = sems, []

    def start(self, source, target):
        self.all.append(pltpu.make_async_copy(source, target, self.sems.at[len(self.all)]))
        self.all[-1].start()

    def wait(self):
        for copy in self.all:
            copy.wait()


def head_rows(place, src, table, rows, pieces):
    @pl.loop(0, OWNERS)
    def _(b):
        for n, s in enumerate(pieces):
            base = b * BUCKET + ((place[0] + s) & (COLS - 1)) * PART
            for i in range(PART):
                rows[pl.ds(n * EDGES + b * PART + i, 1), :] = table[pl.ds(src[base + i], 1), :]


def gather_far_body(place, src, neg, table, via_r, via_l, corrupt_out, rows, corrupt, rounded, vr, vl, sems):
    copies = Copies(sems)

    @pl.loop(0, NEG // 40)
    def _(g):
        for i in range(40):
            corrupt[pl.ds(g * 40 + i, 1), :] = table[pl.ds(neg[g * 40 + i], 1), :]

    corrupt[NEG:NEG_PAD, :] = jnp.zeros((NEG_PAD - NEG, WIDTH), F32)
    rounded[...] = corrupt[...].astype(BF16)
    copies.start(rounded, corrupt_out)
    head_rows(place, src, table, rows, (2,))
    for held, out, part in ((vr, via_r, slice(0, HALF)), (vl, via_l, slice(HALF, 2 * HALF))):
        held[0:HALF, :] = rows[part, :].astype(BF16)
        held[HALF:, :] = rounded[part, :]
        copies.start(held, out)
    copies.wait()


def gather_far(place, src, neg, table):
    return call(
        gather_far_body,
        "gather_far",
        [(shape(2 * HALF, BF16), HBM)] * 3,
        [SMEM, SMEM, SMEM, VMEM],
        [pltpu.VMEM((EDGES, WIDTH), F32), pltpu.VMEM((NEG_PAD, WIDTH), F32)]
        + [pltpu.VMEM((2 * HALF, WIDTH), BF16)] * 3
        + [pltpu.SemaphoreType.DMA((3,))],
        WHOLE,
        moved=10_000_000,
    )(place, src, neg, table)


def gather_near_body(place, src, table, corrupt, right, left, rows, halves, r, l, in_sems, sems):
    arrivals, copies = Copies(in_sems), Copies(sems)
    arrivals.start(corrupt, halves)
    head_rows(place, src, table, rows, (1, 3))
    arrivals.wait()
    r[0:EDGES, :] = rows[0:EDGES, :].astype(BF16)
    r[EDGES:, :] = halves[HALF:, :]
    copies.start(r, right)
    l[0:EDGES, :] = rows[EDGES : 2 * EDGES, :].astype(BF16)
    l[EDGES:, :] = halves[0:HALF, :]
    copies.start(l, left)
    copies.wait()


def gather_near(place, src, table, corrupt):
    sizes = (EDGES + HALF, EDGES + HALF)
    return call(
        gather_near_body,
        "gather_near",
        [(shape(n, BF16), HBM) for n in sizes],
        [SMEM, SMEM, VMEM, HBM],
        [pltpu.VMEM((2 * EDGES, WIDTH), F32), pltpu.VMEM((NEG_PAD, WIDTH), BF16)]
        + [pltpu.VMEM((n, WIDTH), BF16) for n in sizes]
        + [pltpu.SemaphoreType.DMA((1,)), pltpu.SemaphoreType.DMA((2,))],
        WHOLE,
        flops=17_000_000_000,
        moved=20_000_000,
    )(place, src, table, corrupt)


LINES = 4 * BUCKET


def gather_tails_body(place, wanted, table, relations, out, factors_out, words, rows, factors, weighted, sems):
    copies = Copies(sems)
    copies.start(wanted, words)
    for k in range(4):

        @pl.loop(k * OWNERS // 4, (k + 1) * OWNERS // 4)
        def _(b):
            base = b * LINES + place[1] * BUCKET
            for i in range(BUCKET):
                rows[pl.ds(b * BUCKET + i, 1), :] = table[pl.ds(wanted[base + i], 1), :]
                row = wanted[base + 2 * BUCKET + i]
                factors[pl.ds(b * BUCKET + i, 1), :] = relations[pl.ds(row, 1), :]

        part = pl.ds(k * SLOTS // 4, SLOTS // 4)
        weighted[part, :] = (factors[part, :] * rows[part, :].astype(BF16).astype(F32)).astype(BF16)
        copies.start(weighted.at[part], out.at[part])
        copies.start(factors.at[part], factors_out.at[part])
    copies.wait()


def gather_tails(place, wanted, table, relations):
    return call(
        gather_tails_body,
        "gather_tails",
        [
            (shape(SLOTS, BF16), HBM),
            (shape(SLOTS, F32), HBM),
            (jax.ShapeDtypeStruct((OWNERS * LINES,), I32), HBM),
        ],
        [SMEM, SMEM, VMEM, VMEM],
        [TABLE, TABLE, pltpu.VMEM((SLOTS, WIDTH), BF16), pltpu.SemaphoreType.DMA((9,))],
        WHOLE,
        flops=10_000_000_000,
        moved=20_000_000,
    )(place, wanted, table, relations)


def gather_own_body(place, src, table, out, rows, held, sems):
    copies = Copies(sems)
    head_rows(place, src, table, rows, (0,))
    held[...] = rows[...].astype(BF16)
    copies.start(held, out)
    copies.wait()


def gather_own(place, src, table):
    return call(
        gather_own_body,
        "gather_own",
        [(shape(EDGES, BF16), HBM)],
        [SMEM, SMEM, VMEM],
        [
            pltpu.VMEM((EDGES, WIDTH), F32),
            pltpu.VMEM((EDGES, WIDTH), BF16),
            pltpu.SemaphoreType.DMA((1,)),
        ],
        WHOLE,
        moved=3_000_000,
    )(place, src, table)[0]


def edge_scores_body(
    place, counts, weighted_in, h0, n0, dr, vr, dl, vl, wr, wl, pulled_out, own, right, left, *rest
):
    weighted, heads, corrupt, grad_scores, pulled, o, r, l, in_sems, sems = rest
    owner = [(place[0] + COLS - s) & (COLS - 1) for s in range(COLS)]
    span = [slice(s * WIDTH, (s + 1) * WIDTH) for s in range(COLS)]
    arrivals, copies = Copies(in_sems), Copies(sems)

    def fetch(source, begin, target, row, s, n):
        arrivals.start(source.at[pl.ds(begin, n)], target.at[pl.ds(row, n), pl.ds(s * WIDTH, WIDTH)])

    fetch(n0, 0, corrupt, 0, 0, NEG_PAD)
    fetch(vr, HALF, corrupt, 0, 1, HALF)
    fetch(dr, EDGES, corrupt, HALF, 1, HALF)
    fetch(wr, HALF, corrupt, 0, 2, HALF)
    fetch(wl, HALF, corrupt, HALF, 2, HALF)
    fetch(dl, EDGES, corrupt, 0, 3, HALF)
    fetch(vl, HALF, corrupt, HALF, 3, HALF)
    arrivals.start(weighted_in, weighted)
    fetch(h0, 0, heads, 0, 0, EDGES)
    fetch(dr, 0, heads, 0, 1, EDGES)
    fetch(wr, 0, heads, 0, 2, HALF)
    fetch(wl, 0, heads, HALF, 2, HALF)
    fetch(dl, 0, heads, 0, 3, EDGES)
    arrivals.wait()

    def send(values, at, where, second):
        n = values.shape[0]
        via, via_out = (l, left) if second else (r, right)
        for s, held, out, begins in ((2, via, via_out, where), (1, l, left, at), (3, r, right, at), (0, o, own, at)):
            held[begins : begins + n, :] = values[:, span[s]]
            copies.start(held.at[pl.ds(begins, n)], out.at[pl.ds(begins, n)])

    negatives = corrupt[...]
    slot = lax.broadcasted_iota(I32, (PART, 1), 0) + place[0] * PART
    buckets = BLOCK // PART
    whole = []
    for k in range(EDGES // BLOCK):
        rows = slice(k * BLOCK, (k + 1) * BLOCK)
        live = jnp.concatenate(
            [(slot < counts[0, b]).astype(F32) for b in range(k * buckets, (k + 1) * buckets)], axis=0
        )
        wk = jnp.concatenate(
            [weighted[k * buckets : (k + 1) * buckets, owner[s]].reshape(BLOCK, WIDTH) for s in range(COLS)],
            axis=1,
        )
        whole.append(wk)
        wf, hf = wk.astype(F32), heads[rows, :].astype(F32)
        positive = jnp.sum(hf * wf, axis=1, keepdims=True)
        grad_positive = -live * jax.nn.sigmoid(-positive)
        scores = lax.dot_general(wk, negatives, (((1,), (1,)), ((), ())), preferred_element_type=F32)
        grad = (live * jax.nn.sigmoid(scores) * (1.0 / NEG)).astype(BF16)
        grad_scores[rows, :] = grad
        total = jnp.dot(grad, negatives, preferred_element_type=F32) + grad_positive * hf
        total = total.astype(BF16)
        at = pl.ds(k * buckets, buckets)
        for s in range(COLS):
            pulled[at, owner[s]] = total[:, span[s]].reshape(buckets, PART, WIDTH)
        copies.start(pulled.at[at], pulled_out.at[at])
        send((grad_positive * wf).astype(BF16), k * BLOCK, DIRECT + k * BLOCK % HALF, k * BLOCK >= HALF)
    weights = jnp.concatenate(whole, axis=0)
    for k in range(NEG_PAD // BLOCK):
        total = lax.dot_general(
            grad_scores[:, k * BLOCK : (k + 1) * BLOCK],
            weights,
            (((0,), (0,)), ((), ())),
            preferred_element_type=F32,
        )
        send(
            total.astype(BF16),
            EDGES + k * BLOCK,
            DIRECT + HALF + k * BLOCK % HALF,
            k * BLOCK >= HALF,
        )
    copies.wait()


def edge_scores(place, counts, weighted, pieces):
    whole = (OWNERS, COLS, PART, WIDTH)
    sizes = (DIRECT, DIRECT + 2 * HALF, DIRECT + 2 * HALF)
    return call(
        edge_scores_body,
        "edge_scores",
        [(jax.ShapeDtypeStruct(whole, BF16), HBM)] + [(shape(n, BF16), HBM) for n in sizes],
        [SMEM, SMEM] + [HBM] * 9,
        [
            pltpu.VMEM(whole, BF16),
            pltpu.VMEM((EDGES, FULL), BF16),
            pltpu.VMEM((NEG_PAD, FULL), BF16),
            pltpu.VMEM((EDGES, NEG_PAD), BF16),
            pltpu.VMEM(whole, BF16),
        ]
        + [pltpu.VMEM((n, WIDTH), BF16) for n in sizes]
        + [pltpu.SemaphoreType.DMA((13,)), pltpu.SemaphoreType.DMA((36,))],
        WHOLE,
        flops=3_200_000_000,
        moved=8_000_000,
    )(place, counts, weighted, *pieces)


def begin(tables, start=None):
    for n, table in enumerate(tables):
        if n > 0 or start is None:
            table[...] = jnp.zeros((SLOTS, WIDTH), F32)
        else:
            table[...] = start[...]


def finish(tables):
    total = tables[0][...]
    for table in tables[1:]:
        total += table[...]
    tables[0][...] = total


def scatter_near_body(col, src, g0, g1, g3, out, b0, b1, b3, r0, r1, r3, sems, *tables):
    tables = (out,) + tables
    copies = Copies(sems)
    for source, target in ((g0, b0), (g1, b1), (g3, b3)):
        copies.start(source.at[pl.ds(0, EDGES)], target)
    begin(tables)
    copies.wait()
    for source, target in ((b0, r0), (b1, r1), (b3, r3)):
        target[...] = source[...].astype(F32)

    @pl.loop(0, OWNERS)
    def _(b):
        for i in range(PART):
            for s, rows in ((0, r0), (1, r1), (3, r3)):
                base = b * BUCKET + ((col[0] + s) & (COLS - 1)) * PART
                into = tables[(i * 3 + s) % CHAINS]
                into[pl.ds(src[base + i], 1), :] += rows[pl.ds(b * PART + i, 1), :]

    finish(tables)


def scatter_near(col, src, g0, g1, g3):
    return call(
        scatter_near_body,
        "scatter_near",
        [(shape(SLOTS, F32), VMEM)],
        [SMEM] * 2 + [HBM] * 3,
        [pltpu.VMEM((EDGES, WIDTH), BF16)] * 3
        + [pltpu.VMEM((EDGES, WIDTH), F32)] * 3
        + [pltpu.SemaphoreType.DMA((3,))]
        + [TABLE] * (CHAINS - 1),
        WHOLE,
        flops=10_000_000_000,
        moved=20_000_000,
    )(col, src, g0, g1, g3)[0]


def scatter_far_body(col, src, neg, start, g0, g1, g3, wr, wl, out, b0, b1, b3, br, bl, rr, rl, corrupt, sems, *tables):
    tables = (out,) + tables
    copies = Copies(sems)
    copies.start(wr, br)
    copies.start(wl, bl)
    for source, target in ((g0, b0), (g1, b1), (g3, b3)):
        copies.start(source.at[pl.ds(EDGES, NEG_PAD)], target)
    begin(tables, start)
    copies.wait()
    rr[...] = br[0:HALF, :].astype(F32)
    rl[...] = bl[0:HALF, :].astype(F32)
    near = b0[...].astype(F32) + b1[...].astype(F32) + b3[...].astype(F32)
    corrupt[0:HALF, :] = near[0:HALF, :] + br[HALF:, :].astype(F32)
    corrupt[HALF:, :] = near[HALF:, :] + bl[HALF:, :].astype(F32)

    @pl.loop(0, OWNERS // 2)
    def _(b):
        for i in range(PART):
            for n, rows in enumerate((rr, rl)):
                base = (b + n * OWNERS // 2) * BUCKET + ((col[0] + 2) & (COLS - 1)) * PART
                into = tables[(i * 2 + n) % CHAINS]
                into[pl.ds(src[base + i], 1), :] += rows[pl.ds(b * PART + i, 1), :]

    @pl.loop(0, NEG // 40)
    def _(g):
        for i in range(40):
            into = tables[i % CHAINS]
            into[pl.ds(neg[g * 40 + i], 1), :] += corrupt[pl.ds(g * 40 + i, 1), :]

    finish(tables)


def scatter_far(col, src, neg, start, g0, g1, g3, wr, wl):
    return call(
        scatter_far_body,
        "scatter_far",
        [(shape(SLOTS, F32), VMEM)],
        [SMEM] * 3 + [VMEM] + [HBM] * 5,
        [pltpu.VMEM((NEG_PAD, WIDTH), BF16)] * 5
        + [pltpu.VMEM((HALF, WIDTH), F32)] * 2
        + [pltpu.VMEM((NEG_PAD, WIDTH), F32), pltpu.SemaphoreType.DMA((5,))]
        + [TABLE] * (CHAINS - 1),
        WHOLE,
        flops=10_000_000_000,
        moved=20_000_000,
    )(col, src, neg, start, g0, g1, g3, wr, wl)[0]


def scatter_tails_body(place, wanted, start, factors, pulled, out, squares, held, scale, rows, first, in_sems, *tables):
    arrivals = []
    parts = [pl.ds(k * SLOTS // 4, SLOTS // 4) for k in range(4)]
    for k, part in enumerate(parts):
        for n, (source, target) in enumerate(((pulled, held), (factors, scale))):
            arrivals.append(pltpu.make_async_copy(source.at[part], target.at[part], in_sems.at[2 * k + n]))
            arrivals[-1].start()
    arrivals.append(pltpu.make_async_copy(start, first, in_sems.at[8]))
    arrivals[-1].start()
    begin(tables)
    for k, part in enumerate(parts):
        arrivals[2 * k].wait()
        arrivals[2 * k + 1].wait()
        rows[part, :] = scale[part, :] * held[part, :].astype(F32)

        @pl.loop(k * OWNERS // 4, (k + 1) * OWNERS // 4)
        def _(b):
            base = b * LINES + place[1] * BUCKET
            for i in range(BUCKET):
                into = tables[i % CHAINS]
                into[pl.ds(wanted[base + i], 1), :] += rows[pl.ds(b * BUCKET + i, 1), :]

    arrivals[-1].wait()
    ones = jnp.ones((16, 2 * WIDTH), BF16)
    for k, part in enumerate(parts):
        total = first[part, :]
        for table in tables:
            total += table[part, :]
        out[part, :] = total
        square = total * total
        high = square.astype(BF16)
        low = (square - high.astype(F32)).astype(BF16)
        sums = lax.dot_general(
            ones, jnp.concatenate([high, low], axis=1), (((1,), (1,)), ((), ())), preferred_element_type=F32
        )
        for n in range(SLOTS // 4 // WIDTH):
            line = k * SLOTS // 4 // WIDTH + n
            squares[line : line + 1, :] = sums[0:1, n * WIDTH : (n + 1) * WIDTH]


def scatter_tails(place, wanted, start, factors, pulled):
    return call(
        scatter_tails_body,
        "scatter_tails",
        [(shape(SLOTS, F32), VMEM), (shape(SLOTS // WIDTH, F32), VMEM)],
        [SMEM] * 2 + [HBM] * 3,
        [pltpu.VMEM((SLOTS, WIDTH), BF16), TABLE, TABLE, TABLE]
        + [pltpu.SemaphoreType.DMA((9,))]
        + [TABLE] * CHAINS,
        WHOLE,
        moved=30_000_000,
    )(place, wanted, start, factors, pulled)


def stage_body(table, gradient, table_out, step_out):
    table_out[...] = table[...]
    step_out[...] = gradient[...] * learning_rate


def stage(table, gradient):
    return call(
        stage_body,
        "stage",
        [(shape(SLOTS, F32), VMEM)] * 2,
        [VMEM] * 2,
        [],
        12 * 1024,
        moved=8_000_000,
    )(table, gradient)


def shifted(x, s):
    return lax.ppermute(x, "col", [(i, (i + s) % COLS) for i in range(COLS)])


def shards(
    embeddings, adagrad_state, relations, src_rows, dst_rows, rel_ids, bucket_counts, neg_rows
):
    axes = ("dom", "col")
    place = jnp.stack([lax.axis_index("col"), lax.axis_index("dom") & 1]).astype(I32)

    def sent(x):
        return lax.all_to_all(
            x.reshape(OWNERS * COLS, PART, WIDTH), axes, split_axis=0, concat_axis=0, tiled=True
        )

    pairs = (OWNERS // 2, 2, 2, WIDTH)
    rows, kinds = (lax.broadcast_in_dim(x.reshape(-1, WIDTH), pairs, (0, 3)) for x in (dst_rows, rel_ids))
    words = jnp.where(lax.broadcasted_iota(I32, pairs, 2) == 0, rows, kinds).reshape(OWNERS, 2, WIDTH)
    wanted = lax.all_to_all(words, "dom", split_axis=0, concat_axis=0, tiled=True).reshape(-1)

    via_r, via_l, negatives = gather_far(place, src_rows, neg_rows, embeddings)
    vr, vl = shifted(via_r, 1), shifted(via_l, -1)
    weighted, factors, wanted = gather_tails(place, wanted, embeddings, relations)
    weighted = sent(weighted).reshape(OWNERS, COLS, PART, WIDTH)
    after, factors, vr, vl = lax.optimization_barrier((negatives, factors, vr, vl))
    right, left = gather_near(place, src_rows, embeddings, after)
    heads = gather_own(place, src_rows, embeddings)
    pieces = [heads, after, shifted(right, 1), vr, shifted(left, -1), vl, shifted(vr, 1), shifted(vl, -1)]
    pulled, own, right, left = edge_scores(place, bucket_counts, weighted, pieces)
    pulled = sent(pulled).reshape(SLOTS, WIDTH)
    from_left, from_right = shifted(right, 1), shifted(left, -1)
    far_a, far_b = shifted(from_left[DIRECT:], 1), shifted(from_right[DIRECT:], -1)
    gradient = scatter_near(place, src_rows, own, from_right, from_left)
    gradient = scatter_far(place, src_rows, neg_rows, gradient, own, from_right, from_left, far_a, far_b)
    gradient, squares = scatter_tails(place, wanted, gradient, factors, pulled)

    table, step = stage(embeddings, gradient)
    squares = (squares + shifted(squares, 2)) + (shifted(squares, 1) + shifted(squares, 3))
    new_state = adagrad_state + squares.reshape(-1) / FULL
    new_embeddings = table - step / jnp.sqrt(new_state)[:, None]
    return (new_embeddings, new_state)


def solution(mesh):
    placed = (
        P("dom", "col"),
        P("dom"),
        P(None, "col"),
        P("dom"),
        P("dom"),
        P("dom"),
        P("dom", None),
        P("dom"),
    )
    return jax.shard_map(
        shards, mesh=mesh, in_specs=placed, out_specs=(P("dom", "col"), P("dom")), check_vma=False
    )
```

time: 161 us -> 155 us (0.963)
  waiting for transfers between devices: 35.1 us -> 28.7 us
  Pallas kernels: 62.6 us -> 57.6 us
  starting transfers between devices: 50.1 us -> 53.6 us
  local copies, waits for them, and re-layouts: 6.59 us -> 8.9 us
  other arithmetic: 5.35 us -> 3.61 us
    all_to_all x2, waiting for transfers between devices: 14.3 us -> 1.24 us  [sent(): lax.all_to_all(x.reshape(OWNERS * COLS, PART, WIDTH), axes, split_axis=0,...]
    pallas_call x5 -> x6, Pallas kernels: 39 us -> 33.6 us  [the longest x1 10.4 us: scatter_tails(): call(scatter_tails_body, 'scatter_tails', [(shape(SLOTS, F32), VMEM), (sh...]
    ppermute x15 -> x13, waiting for transfers between devices: 20.8 us -> 25.2 us  [shifted(): return lax.ppermute(x, 'col', [(i, (i + s) % COLS) for i in range(COLS)])]
    all_to_all x2, starting transfers between devices: 20.7 us -> 24.9 us  [sent(): lax.all_to_all(x.reshape(OWNERS * COLS, PART, WIDTH), axes, split_axis=0,...]
    reduce_sum x1 -> x0, other arithmetic: 2.35 us -> none  [shards(): squares = jnp.sum(gradient * gradient, axis=1).reshape(-1, WIDTH)]
    all_to_all x1, waiting for transfers between devices: 0.01 us -> 2.33 us  [shards(): lax.all_to_all(words, 'dom', split_axis=0, concat_axis=0, tiled=True)]
    unnamed x32 -> x14, local copies, waits for them, and re-layouts: 5.01 us -> 5.99 us
    ppermute x15 -> x13, starting transfers between devices: 17.4 us -> 16.7 us  [shifted(): return lax.ppermute(x, 'col', [(i, (i + s) % COLS) for i in range(COLS)])]
  transfers between devices with their start and end apart: 18 -> 16, of which waited for: 9 -> 7; matrix products, arithmetic and copies ran while one was open for 0% -> 1% of each run, Pallas kernels for 27% -> 26%
where the time goes in v3:
time: 155 us; the launch traced here: 153 us
  Pallas kernels  57.6 us (37%)
  starting transfers between devices  53.6 us (35%)
  waiting for transfers between devices  28.7 us (19%)
  local copies, waits for them, and re-layouts  8.9 us (6%)
  other arithmetic  3.61 us (2%)
    ppermute x13, waiting for transfers between devices, shifted(): return lax.ppermute(x, 'col', [(i, (i + s) % COLS) for i in range(COLS)])  25.2 us
    all_to_all x2, starting transfers between devices, sent(): lax.all_to_all(x.reshape(OWNERS * COLS, PART, WIDTH), axes, split_axis=0,...  24.9 us
    ppermute x13, starting transfers between devices, shifted(): return lax.ppermute(x, 'col', [(i, (i + s) % COLS) for i in range(COLS)])  16.7 us
    all_to_all x1, starting transfers between devices, shards(): lax.all_to_all(words, 'dom', split_axis=0, concat_axis=0, tiled=True)  11.9 us
    pallas_call x1, Pallas kernels, scatter_tails(): call(scatter_tails_body, 'scatter_tails', [(shape(SLOTS, F32), VMEM), (sh...  10.4 us
    pallas_call x1, Pallas kernels, gather_tails(): call(gather_tails_body, 'gather_tails', [(shape(SLOTS, BF16), HBM), (shap...  9.89 us
    pallas_call x1, Pallas kernels, scatter_near(): call(scatter_near_body, 'scatter_near', [(shape(SLOTS, F32), VMEM)], [SME...  8.44 us
    pallas_call x1, Pallas kernels, edge_scores(): call(edge_scores_body, 'edge_scores', [(jax.ShapeDtypeStruct(whole, BF16)...  7.91 us
  transfers between devices with their start and end apart: 16, of which 7 were waited for; matrix products, arithmetic and copies ran while one was open for 1% of the time, Pallas kernels for 26%

profile of v3, /device:TPU:8, one launch (start us, length us, event | category | flops | bytes accessed | tf_op | source)
XLA Modules:
  0.0 153.2 jit_solution(15317414655037381733)
XLA Ops:
  0.6 0.7 broadcast_in_dim.15
  1.4 0.7 broadcast_in_dim.18
  2.1 0.7 broadcast_select_fusion
  2.8 11.9 %all-to-all-start = ((s32[64,2,128]{2,1,0:T(2,128)}), s32[64,2,128]{2,1,0:T(2,128)S(1)}, u32[]{:S(2)}, u32[]{:S(2)}) async-start(s32[64,2,128]{2,1,0:T(2,128)} %broadcast_select_fusion), calls=%async_computation | async-start | bytes 131072 | tf_op jit(solution)/shard_map/all_to_all | solution.py:491
  14.8 0.6 pad_add_fusion.place.col
  15.4 4.7 %gather_far.1 = (bf16[1024,128]{1,0:T(8,128)(2,1)}, bf16[1024,128]{1,0:T(8,128)(2,1)}, bf16[1024,128]{1,0:T(8,128)(2,1)}) custom-call(s32[2]{0:T(128)} %pad_add_fusion.place.col, s32[4096]{0:T(1024)} %src.9, s32[1000]{0:T(1024)} %neg.3, f32[4096,128]{1,0:T(8,128)} %table.9), custom_call_target="tpu_custom_call" | custom-call | bytes 10000000 | tf_op jit(solution)/shard_map/gather_far/pallas_call | solution.py:95
  20.1 1.7 %collective-permute-start = (bf16[1024,128]{1,0:T(8,128)(2,1)}, bf16[1024,128]{1,0:T(8,128)(2,1)}, u32[]{:S(2)}, u32[]{:S(2)}) collective-permute-start(bf16[1024,128]{1,0:T(8,128)(2,1)} %get-tuple-element.26), channel_id=1, source_target_pairs={{0,1},{1,2},{2,3},{3,0},{4,5},{5,6},{6,7},{7,4},{8,9},{9,10},{10,1... | collective-permute-start | bytes 786440 | tf_op jit(solution)/shard_map/ppermute | solution.py:474
  21.7 0.4 collective-permute-start.1
  22.2 2.3 %all-to-all-done = s32[64,2,128]{2,1,0:T(2,128)S(1)} async-done(((s32[64,2,128]{2,1,0:T(2,128)}), s32[64,2,128]{2,1,0:T(2,128)S(1)}, u32[]{:S(2)}, u32[]{:S(2)}) %all-to-all-start) | async-done | bytes 65568 | tf_op jit(solution)/shard_map/all_to_all | solution.py:491
  24.5 0.6 copy-done.4
  25.1 9.9 %gather_tails.1 = (bf16[4096,128]{1,0:T(8,128)(2,1)}, f32[4096,128]{1,0:T(8,128)}, s32[16384]{0:T(1024)}) custom-call(s32[2]{0:T(128)} %pad_add_fusion.place.col, s32[16384]{0:T(1024)} %bitcast.18, f32[4096,128]{1,0:T(8,128)} %table.9, f32[1345,128]{1,0:T(8,128)} %relations.1), custom_call_target="tpu_custom_call" | custom-call | flops 10000000000 | bytes 20000000 | tf_op jit(solution)/shard_map/gather_tails/pallas_call | solution.py:162
  35.0 11.7 %all-to-all-start.1 = ((bf16[256,16,128]{2,1,0:T(8,128)(2,1)}), bf16[256,16,128]{2,1,0:T(8,128)(2,1)}, u32[]{:S(2)}, u32[]{:S(2)}) async-start(bf16[256,16,128]{2,1,0:T(8,128)(2,1)} %bitcast.15), calls=%async_computation.1 | async-start | bytes 2097152 | tf_op jit(solution)/shard_map/all_to_all | solution.py:484
  46.7 0.0 collective-permute-done.vr
  46.7 4.7 %gather_near.1 = (bf16[1536,128]{1,0:T(8,128)(2,1)}, bf16[1536,128]{1,0:T(8,128)(2,1)}) custom-call(s32[2]{0:T(128)} %pad_add_fusion.place.col, s32[4096]{0:T(1024)} %src.9, f32[4096,128]{1,0:T(8,128)} %table.9, bf16[1024,128]{1,0:T(8,128)(2,1)} %get-tuple-element.28.corrupt.n0), custom_call_target="tpu_custom_call" | custom-call | flops 16999999488 | bytes 20000000 | tf_op jit(solution)/shard_map/gather_near/pallas_call | solution.py:124
  51.4 1.5 %collective-permute-start.2 = (bf16[1536,128]{1,0:T(8,128)(2,1)}, bf16[1536,128]{1,0:T(8,128)(2,1)}, u32[]{:S(2)}, u32[]{:S(2)}) collective-permute-start(bf16[1536,128]{1,0:T(8,128)(2,1)} %get-tuple-element.29), channel_id=1, source_target_pairs={{0,1},{1,2},{2,3},{3,0},{4,5},{5,6},{6,7},{7,4},{8,9},{9,10},{10,1... | collective-permute-start | bytes 1179656 | tf_op jit(solution)/shard_map/ppermute | solution.py:474
  53.0 0.8 collective-permute-start.3
  53.8 1.2 collective-permute-start.4
  55.0 2.0 %collective-permute-start.5 = (bf16[1024,128]{1,0:T(8,128)(2,1)}, bf16[1024,128]{1,0:T(8,128)(2,1)}, u32[]{:S(2)}, u32[]{:S(2)}) collective-permute-start(bf16[1024,128]{1,0:T(8,128)(2,1)} %collective-permute-done.1.vl), channel_id=1, source_target_pairs={{0,3},{1,0},{2,1},{3,2},{4,7},{5,4},{6,5},{7,6},{8,11},{9,8},{10,9... | collective-permute-start | bytes 786440 | tf_op jit(solution)/shard_map/ppermute | solution.py:474
  56.9 3.6 %gather_own.1.h0 = bf16[1024,128]{1,0:T(8,128)(2,1)} custom-call(s32[2]{0:T(128)} %pad_add_fusion.place.col, s32[4096]{0:T(1024)} %src.9, f32[4096,128]{1,0:T(8,128)} %table.9), custom_call_target="tpu_custom_call" | custom-call | bytes 3000000 | tf_op jit(solution)/shard_map/gather_own/pallas_call | solution.py:187
  60.6 15.8 %collective-permute-done.4.wr = bf16[1024,128]{1,0:T(8,128)(2,1)} collective-permute-done((bf16[1024,128]{1,0:T(8,128)(2,1)}, bf16[1024,128]{1,0:T(8,128)(2,1)}, u32[]{:S(2)}, u32[]{:S(2)}) %collective-permute-start.4) | collective-permute-done | bytes 262176 | tf_op jit(solution)/shard_map/ppermute | solution.py:474
  76.4 1.1 collective-permute-done.5.wl
  77.5 0.0 collective-permute-done.2.dr
  77.5 0.3 all-to-all-done.1
  77.8 7.9 %edge_scores.1 = (bf16[64,4,16,128]{3,2,1,0:T(8,128)(2,1)}, bf16[2048,128]{1,0:T(8,128)(2,1)}, bf16[3072,128]{1,0:T(8,128)(2,1)}, bf16[3072,128]{1,0:T(8,128)(2,1)}) custom-call(s32[2]{0:T(128)} %pad_add_fusion.place.col, s32[1,64]{1,0:T(1,128)} %counts.1, bf16[64,4,16,128]{3,2,1,0:T(8,128)(2,1)} %bitcast.8.weighted_in, bf16[1024,128]{1,0:T(8,128)(2,1)} %gather_own.1.h0, ...), custom_call_target="tpu_custom_call" | custom-call | flops 3200000000 | bytes 8000000 | tf_op jit(solution)/shard_map/edge_scores/pallas_call | solution.py:282
  85.7 1.5 collective-permute-start.6
  87.2 0.8 collective-permute-start.7
  88.0 13.3 %all-to-all-start.2 = ((bf16[256,16,128]{2,1,0:T(8,128)(2,1)}), bf16[256,16,128]{2,1,0:T(8,128)(2,1)}, u32[]{:S(2)}, u32[]{:S(2)}) async-start(bf16[256,16,128]{2,1,0:T(8,128)(2,1)} %bitcast.14), calls=%async_computation.2 | async-start | bytes 2097152 | tf_op jit(solution)/shard_map/all_to_all | solution.py:484
  101.2 5.8 %collective-permute-done.6.g1 = bf16[3072,128]{1,0:T(8,128)(2,1)S(1)} collective-permute-done((bf16[3072,128]{1,0:T(8,128)(2,1)}, bf16[3072,128]{1,0:T(8,128)(2,1)S(1)}, u32[]{:S(2)}, u32[]{:S(2)}) %collective-permute-start.6) | collective-permute-done | bytes 786464 | tf_op jit(solution)/shard_map/ppermute | solution.py:474
  107.1 0.9 copy-done.2
  107.9 0.7 slice.9
  108.7 2.4 %collective-permute-start.9 = (bf16[1024,128]{1,0:T(8,128)(2,1)}, bf16[1024,128]{1,0:T(8,128)(2,1)}, u32[]{:S(2)}, u32[]{:S(2)}) collective-permute-start(bf16[1024,128]{1,0:T(8,128)(2,1)} %slice.9), channel_id=1, source_target_pairs={{0,3},{1,0},{2,1},{3,2},{4,7},{5,4},{6,5},{7,6},{8,11},{9,8},{10,9... | collective-permute-start | bytes 786440 | tf_op jit(solution)/shard_map/ppermute | solution.py:474
  111.1 0.9 copy-done.3
  112.0 0.7 slice.8
  112.7 8.4 %scatter_near.1.start = f32[4096,128]{1,0:T(8,128)} custom-call(s32[2]{0:T(128)} %pad_add_fusion.place.col, s32[4096]{0:T(1024)} %src.9, bf16[2048,128]{1,0:T(8,128)(2,1)} %get-tuple-element.33.g0, bf16[3072,128]{1,0:T(8,128)(2,1)} %copy-done.2, bf16[3072,128]{1,0:T(8,128)(2,1)} %copy-done.3), custom_call_target="tpu_custom_call" | custom-call | flops 10000000000 | bytes 20000000 | tf_op jit(solution)/shard_map/scatter_near/pallas_call | solution.py:339
  121.2 2.4 %collective-permute-done.8.wr = bf16[1024,128]{1,0:T(8,128)(2,1)} collective-permute-done((bf16[1024,128]{1,0:T(8,128)(2,1)}, bf16[1024,128]{1,0:T(8,128)(2,1)}, u32[]{:S(2)}, u32[]{:S(2)}) %collective-permute-start.8) | collective-permute-done | bytes 262176 | tf_op jit(solution)/shard_map/ppermute | solution.py:474
  123.6 7.6 %scatter_far.1.start = f32[4096,128]{1,0:T(8,128)} custom-call(s32[2]{0:T(128)} %pad_add_fusion.place.col, s32[4096]{0:T(1024)} %src.9, s32[1000]{0:T(1024)} %neg.3, f32[4096,128]{1,0:T(8,128)} %scatter_near.1.start, bf16[2048,128]{1,0:T(8,128)(2,1)} %get-tuple-element.33.g0, bf16[3072,128]{1,0:T(8,128)(2,1)} %copy-done.2, bf16[3072,128]{1,0:T(8,128)(2,1)} %copy-done.3, ...), custom_call_target="tpu_custom_call" | custom-call | flops 10000000000 | bytes 20000000 | tf_op jit(solution)/shard_map/scatter_far/pallas_call | solution.py:387
  131.2 1.0 all-to-all-done.2
  132.2 10.4 %scatter_tails.1 = (f32[4096,128]{1,0:T(8,128)}, f32[32,128]{1,0:T(8,128)}) custom-call(s32[2]{0:T(128)} %pad_add_fusion.place.col, s32[16384]{0:T(1024)} %get-tuple-element.22.wanted, f32[4096,128]{1,0:T(8,128)} %scatter_far.1.start, f32[4096,128]{1,0:T(8,128)} %get-tuple-element.36.factors, bf16[4096,128]{1,0:T(8,128)(2,1)} %bitcast.10.pulled), custom_call_target="tpu_custom_call" | custom-call | bytes 30000000 | tf_op jit(solution)/shard_map/scatter_tails/pallas_call | solution.py:443
  142.6 1.5 collective-permute-start.12
  144.1 0.7 collective-permute-start.11
  144.7 2.2 %collective-permute-start.10 = (f32[32,128]{1,0:T(8,128)}, f32[32,128]{1,0:T(8,128)S(1)}, u32[]{:S(2)}, u32[]{:S(2)}) collective-permute-start(f32[32,128]{1,0:T(8,128)} %get-tuple-element.41), channel_id=1, source_target_pairs={{0,2},{1,3},{2,0},{3,1},{4,6},{5,7},{6,4},{7,5},{8,10},{9,11},{10,... | collective-permute-start | bytes 49160 | tf_op jit(solution)/shard_map/ppermute | solution.py:474
  147.0 1.6 %copy-done = f32[4096,128]{1,0:T(8,128)S(1)} copy-done((f32[4096,128]{1,0:T(8,128)S(1)}, f32[4096,128]{1,0:T(8,128)}, u32[]{:S(2)}) %copy-start) | copy-done | bytes 2097176
  148.6 1.6 %copy-done.1 = f32[4096,128]{1,0:T(8,128)S(1)} copy-done((f32[4096,128]{1,0:T(8,128)S(1)}, f32[4096,128]{1,0:T(8,128)}, u32[]{:S(2)}) %copy-start.1) | copy-done | bytes 2097176
  150.2 0.3 stage.1
  150.5 0.4 copy-done.5
  150.9 0.0 copy-done.6
  150.9 0.6 fusion
  151.5 1.7 %divide_subtract_fusion = f32[4096,128]{1,0:T(8,128)} fusion(f32[4096,128]{1,0:T(8,128)S(1)} %get-tuple-element.39, f32[4096,128]{1,0:T(8,128)S(1)} %get-tuple-element.40, f32[4096]{0:T(1024)S(1)} %get-tuple-element.42), kind=kLoop, calls=%fused_computation | loop fusion | flops 1048576 | bytes 6307840 | tf_op jit(solution)/shard_map/sub | solution.py:512
  (16 shorter events, 0.0 us)
Async XLA Ops:
  2.8 21.7 %all-to-all-start = ((s32[64,2,128]{2,1,0:T(2,128)}), s32[64,2,128]{2,1,0:T(2,128)S(1)}, u32[]{:S(2)}, u32[]{:S(2)}) async-start(s32[64,2,128]{2,1,0:T(2,128)} %broadcast_select_fusion), calls=%async_computation | async-start | bytes 131072 | tf_op jit(solution)/shard_map/all_to_all | solution.py:491
  20.1 26.7 %collective-permute-start = (bf16[1024,128]{1,0:T(8,128)(2,1)}, bf16[1024,128]{1,0:T(8,128)(2,1)}, u32[]{:S(2)}, u32[]{:S(2)}) collective-permute-start(bf16[1024,128]{1,0:T(8,128)(2,1)} %get-tuple-element.26), channel_id=1, source_target_pairs={{0,1},{1,2},{2,3},{3,0},{4,5},{5,6},{6,7},{7,4},{8,9},{9,10},{10,1... | collective-permute-start | bytes 786440 | tf_op jit(solution)/shard_map/ppermute | solution.py:474
  21.7 25.0 %collective-permute-start.1 = (bf16[1024,128]{1,0:T(8,128)(2,1)}, bf16[1024,128]{1,0:T(8,128)(2,1)}, u32[]{:S(2)}, u32[]{:S(2)}) collective-permute-start(bf16[1024,128]{1,0:T(8,128)(2,1)} %get-tuple-element.27), channel_id=1, source_target_pairs={{0,3},{1,0},{2,1},{3,2},{4,7},{5,4},{6,5},{7,6},{8,11},{9,8},{10,9... | collective-permute-start | bytes 786440 | tf_op jit(solution)/shard_map/ppermute | solution.py:474
  24.5 0.6 copy-start.4
  35.0 42.7 %all-to-all-start.1 = ((bf16[256,16,128]{2,1,0:T(8,128)(2,1)}), bf16[256,16,128]{2,1,0:T(8,128)(2,1)}, u32[]{:S(2)}, u32[]{:S(2)}) async-start(bf16[256,16,128]{2,1,0:T(8,128)(2,1)} %bitcast.15), calls=%async_computation.1 | async-start | bytes 2097152 | tf_op jit(solution)/shard_map/all_to_all | solution.py:484
  51.4 26.1 %collective-permute-start.2 = (bf16[1536,128]{1,0:T(8,128)(2,1)}, bf16[1536,128]{1,0:T(8,128)(2,1)}, u32[]{:S(2)}, u32[]{:S(2)}) collective-permute-start(bf16[1536,128]{1,0:T(8,128)(2,1)} %get-tuple-element.29), channel_id=1, source_target_pairs={{0,1},{1,2},{2,3},{3,0},{4,5},{5,6},{6,7},{7,4},{8,9},{9,10},{10,1... | collective-permute-start | bytes 1179656 | tf_op jit(solution)/shard_map/ppermute | solution.py:474
  53.0 24.5 %collective-permute-start.3 = (bf16[1536,128]{1,0:T(8,128)(2,1)}, bf16[1536,128]{1,0:T(8,128)(2,1)}, u32[]{:S(2)}, u32[]{:S(2)}) collective-permute-start(bf16[1536,128]{1,0:T(8,128)(2,1)} %get-tuple-element.31), channel_id=1, source_target_pairs={{0,3},{1,0},{2,1},{3,2},{4,7},{5,4},{6,5},{7,6},{8,11},{9,8},{10,9... | collective-permute-start | bytes 1179656 | tf_op jit(solution)/shard_map/ppermute | solution.py:474
  53.8 22.6 %collective-permute-start.4 = (bf16[1024,128]{1,0:T(8,128)(2,1)}, bf16[1024,128]{1,0:T(8,128)(2,1)}, u32[]{:S(2)}, u32[]{:S(2)}) collective-permute-start(bf16[1024,128]{1,0:T(8,128)(2,1)} %collective-permute-done.vr), channel_id=1, source_target_pairs={{0,1},{1,2},{2,3},{3,0},{4,5},{5,6},{6,7},{7,4},{8,9},{9,10},{10,1... | collective-permute-start | bytes 786440 | tf_op jit(solution)/shard_map/ppermute | solution.py:474
  55.0 22.5 %collective-permute-start.5 = (bf16[1024,128]{1,0:T(8,128)(2,1)}, bf16[1024,128]{1,0:T(8,128)(2,1)}, u32[]{:S(2)}, u32[]{:S(2)}) collective-permute-start(bf16[1024,128]{1,0:T(8,128)(2,1)} %collective-permute-done.1.vl), channel_id=1, source_target_pairs={{0,3},{1,0},{2,1},{3,2},{4,7},{5,4},{6,5},{7,6},{8,11},{9,8},{10,9... | collective-permute-start | bytes 786440 | tf_op jit(solution)/shard_map/ppermute | solution.py:474
  85.7 21.4 %collective-permute-start.6 = (bf16[3072,128]{1,0:T(8,128)(2,1)}, bf16[3072,128]{1,0:T(8,128)(2,1)S(1)}, u32[]{:S(2)}, u32[]{:S(2)}) collective-permute-start(bf16[3072,128]{1,0:T(8,128)(2,1)} %get-tuple-element.34), channel_id=1, source_target_pairs={{0,3},{1,0},{2,1},{3,2},{4,7},{5,4},{6,5},{7,6},{8,11},{9,8},{10,9... | collective-permute-start | bytes 2359304 | tf_op jit(solution)/shard_map/ppermute | solution.py:474
  87.2 23.9 %collective-permute-start.7 = (bf16[3072,128]{1,0:T(8,128)(2,1)}, bf16[3072,128]{1,0:T(8,128)(2,1)S(1)}, u32[]{:S(2)}, u32[]{:S(2)}) collective-permute-start(bf16[3072,128]{1,0:T(8,128)(2,1)} %get-tuple-element.35), channel_id=1, source_target_pairs={{0,1},{1,2},{2,3},{3,0},{4,5},{5,6},{6,7},{7,4},{8,9},{9,10},{10,1... | collective-permute-start | bytes 2359304 | tf_op jit(solution)/shard_map/ppermute | solution.py:474
  88.0 44.2 %all-to-all-start.2 = ((bf16[256,16,128]{2,1,0:T(8,128)(2,1)}), bf16[256,16,128]{2,1,0:T(8,128)(2,1)}, u32[]{:S(2)}, u32[]{:S(2)}) async-start(bf16[256,16,128]{2,1,0:T(8,128)(2,1)} %bitcast.14), calls=%async_computation.2 | async-start | bytes 2097152 | tf_op jit(solution)/shard_map/all_to_all | solution.py:484
  107.1 0.9 copy-start.2
  108.7 12.5 %collective-permute-start.9 = (bf16[1024,128]{1,0:T(8,128)(2,1)}, bf16[1024,128]{1,0:T(8,128)(2,1)}, u32[]{:S(2)}, u32[]{:S(2)}) collective-permute-start(bf16[1024,128]{1,0:T(8,128)(2,1)} %slice.9), channel_id=1, source_target_pairs={{0,3},{1,0},{2,1},{3,2},{4,7},{5,4},{6,5},{7,6},{8,11},{9,8},{10,9... | collective-permute-start | bytes 786440 | tf_op jit(solution)/shard_map/ppermute | solution.py:474
  111.1 0.9 copy-start.3
  112.7 10.9 %collective-permute-start.8 = (bf16[1024,128]{1,0:T(8,128)(2,1)}, bf16[1024,128]{1,0:T(8,128)(2,1)}, u32[]{:S(2)}, u32[]{:S(2)}) collective-permute-start(bf16[1024,128]{1,0:T(8,128)(2,1)} %slice.8), channel_id=1, source_target_pairs={{0,1},{1,2},{2,3},{3,0},{4,5},{5,6},{6,7},{7,4},{8,9},{9,10},{10,1... | collective-permute-start | bytes 786440 | tf_op jit(solution)/shard_map/ppermute | solution.py:474
  142.6 7.9 %collective-permute-start.12 = (f32[32,128]{1,0:T(8,128)}, f32[32,128]{1,0:T(8,128)S(1)}, u32[]{:S(2)}, u32[]{:S(2)}) collective-permute-start(f32[32,128]{1,0:T(8,128)} %get-tuple-element.41), channel_id=1, source_target_pairs={{0,3},{1,0},{2,1},{3,2},{4,7},{5,4},{6,5},{7,6},{8,11},{9,8},{10,9... | collective-permute-start | bytes 49160 | tf_op jit(solution)/shard_map/ppermute | solution.py:474
  144.1 6.4 %collective-permute-start.11 = (f32[32,128]{1,0:T(8,128)}, f32[32,128]{1,0:T(8,128)S(1)}, u32[]{:S(2)}, u32[]{:S(2)}) collective-permute-start(f32[32,128]{1,0:T(8,128)} %get-tuple-element.41), channel_id=1, source_target_pairs={{0,1},{1,2},{2,3},{3,0},{4,5},{5,6},{6,7},{7,4},{8,9},{9,10},{10,1... | collective-permute-start | bytes 49160 | tf_op jit(solution)/shard_map/ppermute | solution.py:474
  144.7 5.8 %collective-permute-start.10 = (f32[32,128]{1,0:T(8,128)}, f32[32,128]{1,0:T(8,128)S(1)}, u32[]{:S(2)}, u32[]{:S(2)}) collective-permute-start(f32[32,128]{1,0:T(8,128)} %get-tuple-element.41), channel_id=1, source_target_pairs={{0,2},{1,3},{2,0},{3,1},{4,6},{5,7},{6,4},{7,5},{8,10},{9,11},{10,... | collective-permute-start | bytes 49160 | tf_op jit(solution)/shard_map/ppermute | solution.py:474
  147.0 1.6 %copy-start = (f32[4096,128]{1,0:T(8,128)S(1)}, f32[4096,128]{1,0:T(8,128)}, u32[]{:S(2)}) copy-start(f32[4096,128]{1,0:T(8,128)} %table.9) | copy-start | bytes 6291460
  148.6 1.6 %copy-start.1 = (f32[4096,128]{1,0:T(8,128)S(1)}, f32[4096,128]{1,0:T(8,128)}, u32[]{:S(2)}) copy-start(f32[4096,128]{1,0:T(8,128)} %get-tuple-element.38.gradient) | copy-start | bytes 6291460
  150.2 0.7 copy-start.5
  150.2 0.7 copy-start.6

commit v4 on v3

--- a/solution.py
+++ b/solution.py
@@ -19,7 +19,7 @@
 DIRECT = EDGES + NEG_PAD
 HALF = 512
 BLOCK = 256
-CHAINS = 4
+CHAINS = 8
 WHOLE = 65_300
 
 F32, BF16, I32 = jnp.float32, jnp.bfloat16, jnp.int32
@@ -57,6 +57,7 @@
     def start(self, source, target):
         self.all.append(pltpu.make_async_copy(source, target, self.sems.at[len(self.all)]))
         self.all[-1].start()
+        return self.all[-1]
 
     def wait(self):
         for copy in self.all:
@@ -135,20 +136,38 @@
     )(place, src, table, corrupt)
 
 
-LINES = 4 * BUCKET
-
-
-def gather_tails_body(place, wanted, table, relations, out, factors_out, words, rows, factors, weighted, sems):
+LINE = 2 * BUCKET
+
+
+def request_body(rows, kinds, out):
+    first = lax.broadcasted_iota(I32, (OWNERS // 2, WIDTH), 1) < BUCKET
+    rows, kinds = rows[...], kinds[...]
+    out[pl.ds(0, OWNERS // 2, stride=2), :] = jnp.where(first, rows, pltpu.roll(kinds, BUCKET, 1))
+    out[pl.ds(1, OWNERS // 2, stride=2), :] = jnp.where(first, pltpu.roll(rows, BUCKET, 1), kinds)
+
+
+def request(rows, kinds):
+    return call(
+        request_body,
+        "request",
+        [(shape(OWNERS, I32), VMEM)],
+        [VMEM] * 2,
+        [],
+        WHOLE,
+        moved=100_000,
+    )(rows.reshape(-1, WIDTH), kinds.reshape(-1, WIDTH))[0]
+
+
+def gather_tails_body(wanted, table, relations, out, factors_out, rows, factors, weighted, sems):
     copies = Copies(sems)
-    copies.start(wanted, words)
     for k in range(4):
 
         @pl.loop(k * OWNERS // 4, (k + 1) * OWNERS // 4)
         def _(b):
-            base = b * LINES + place[1] * BUCKET
+            base = b * LINE
             for i in range(BUCKET):
                 rows[pl.ds(b * BUCKET + i, 1), :] = table[pl.ds(wanted[base + i], 1), :]
-                row = wanted[base + 2 * BUCKET + i]
+                row = wanted[base + BUCKET + i]
                 factors[pl.ds(b * BUCKET + i, 1), :] = relations[pl.ds(row, 1), :]
 
         part = pl.ds(k * SLOTS // 4, SLOTS // 4)
@@ -158,21 +177,20 @@
     copies.wait()
 
 
-def gather_tails(place, wanted, table, relations):
+def gather_tails(wanted, table, relations):
     return call(
         gather_tails_body,
         "gather_tails",
         [
             (shape(SLOTS, BF16), HBM),
             (shape(SLOTS, F32), HBM),
-            (jax.ShapeDtypeStruct((OWNERS * LINES,), I32), HBM),
         ],
-        [SMEM, SMEM, VMEM, VMEM],
-        [TABLE, TABLE, pltpu.VMEM((SLOTS, WIDTH), BF16), pltpu.SemaphoreType.DMA((9,))],
+        [SMEM, VMEM, VMEM],
+        [TABLE, TABLE, pltpu.VMEM((SLOTS, WIDTH), BF16), pltpu.SemaphoreType.DMA((8,))],
         WHOLE,
         flops=10_000_000_000,
         moved=20_000_000,
-    )(place, wanted, table, relations)
+    )(wanted, table, relations)
 
 
 def gather_own_body(place, src, table, out, rows, held, sems):
@@ -195,6 +213,7 @@
             pltpu.SemaphoreType.DMA((1,)),
         ],
         WHOLE,
+        flops=3_000_000_000,
         moved=3_000_000,
     )(place, src, table)[0]
 
@@ -208,22 +227,29 @@
     arrivals, copies = Copies(in_sems), Copies(sems)
 
     def fetch(source, begin, target, row, s, n):
-        arrivals.start(source.at[pl.ds(begin, n)], target.at[pl.ds(row, n), pl.ds(s * WIDTH, WIDTH)])
-
-    fetch(n0, 0, corrupt, 0, 0, NEG_PAD)
-    fetch(vr, HALF, corrupt, 0, 1, HALF)
-    fetch(dr, EDGES, corrupt, HALF, 1, HALF)
-    fetch(wr, HALF, corrupt, 0, 2, HALF)
-    fetch(wl, HALF, corrupt, HALF, 2, HALF)
-    fetch(dl, EDGES, corrupt, 0, 3, HALF)
-    fetch(vl, HALF, corrupt, HALF, 3, HALF)
-    arrivals.start(weighted_in, weighted)
-    fetch(h0, 0, heads, 0, 0, EDGES)
-    fetch(dr, 0, heads, 0, 1, EDGES)
-    fetch(wr, 0, heads, 0, 2, HALF)
-    fetch(wl, 0, heads, HALF, 2, HALF)
-    fetch(dl, 0, heads, 0, 3, EDGES)
-    arrivals.wait()
+        return arrivals.start(source.at[pl.ds(begin, n)], target.at[pl.ds(row, n), pl.ds(s * WIDTH, WIDTH)])
+
+    buckets = BLOCK // PART
+    blocks = [pl.ds(k * buckets, buckets) for k in range(EDGES // BLOCK)]
+    for_scores = [
+        fetch(n0, 0, corrupt, 0, 0, NEG_PAD),
+        fetch(vr, HALF, corrupt, 0, 1, HALF),
+        fetch(dr, EDGES, corrupt, HALF, 1, HALF),
+        fetch(wr, HALF, corrupt, 0, 2, HALF),
+        fetch(wl, HALF, corrupt, HALF, 2, HALF),
+        fetch(dl, EDGES, corrupt, 0, 3, HALF),
+        fetch(vl, HALF, corrupt, HALF, 3, HALF),
+    ]
+    for_weights = [arrivals.start(weighted_in.at[at], weighted.at[at]) for at in blocks]
+    for_heads = [
+        fetch(h0, 0, heads, 0, 0, EDGES),
+        fetch(dr, 0, heads, 0, 1, EDGES),
+        fetch(wr, 0, heads, 0, 2, HALF),
+        fetch(wl, 0, heads, HALF, 2, HALF),
+        fetch(dl, 0, heads, 0, 3, EDGES),
+    ]
+    for copy in for_scores:
+        copy.wait()
 
     def send(values, at, where, second):
         n = values.shape[0]
@@ -234,27 +260,30 @@
 
     negatives = corrupt[...]
     slot = lax.broadcasted_iota(I32, (PART, 1), 0) + place[0] * PART
-    buckets = BLOCK // PART
     whole = []
     for k in range(EDGES // BLOCK):
         rows = slice(k * BLOCK, (k + 1) * BLOCK)
         live = jnp.concatenate(
             [(slot < counts[0, b]).astype(F32) for b in range(k * buckets, (k + 1) * buckets)], axis=0
         )
+        for_weights[k].wait()
         wk = jnp.concatenate(
             [weighted[k * buckets : (k + 1) * buckets, owner[s]].reshape(BLOCK, WIDTH) for s in range(COLS)],
             axis=1,
         )
         whole.append(wk)
+        scores = lax.dot_general(wk, negatives, (((1,), (1,)), ((), ())), preferred_element_type=F32)
+        if k == 0:
+            for copy in for_heads:
+                copy.wait()
         wf, hf = wk.astype(F32), heads[rows, :].astype(F32)
         positive = jnp.sum(hf * wf, axis=1, keepdims=True)
         grad_positive = -live * jax.nn.sigmoid(-positive)
-        scores = lax.dot_general(wk, negatives, (((1,), (1,)), ((), ())), preferred_element_type=F32)
         grad = (live * jax.nn.sigmoid(scores) * (1.0 / NEG)).astype(BF16)
         grad_scores[rows, :] = grad
         total = jnp.dot(grad, negatives, preferred_element_type=F32) + grad_positive * hf
         total = total.astype(BF16)
-        at = pl.ds(k * buckets, buckets)
+        at = blocks[k]
         for s in range(COLS):
             pulled[at, owner[s]] = total[:, span[s]].reshape(buckets, PART, WIDTH)
         copies.start(pulled.at[at], pulled_out.at[at])
@@ -292,7 +321,7 @@
             pltpu.VMEM(whole, BF16),
         ]
         + [pltpu.VMEM((n, WIDTH), BF16) for n in sizes]
-        + [pltpu.SemaphoreType.DMA((13,)), pltpu.SemaphoreType.DMA((36,))],
+        + [pltpu.SemaphoreType.DMA((16,)), pltpu.SemaphoreType.DMA((36,))],
         WHOLE,
         flops=3_200_000_000,
         moved=8_000_000,
@@ -399,29 +428,27 @@
     )(col, src, neg, start, g0, g1, g3, wr, wl)[0]
 
 
-def scatter_tails_body(place, wanted, start, factors, pulled, out, squares, held, scale, rows, first, in_sems, *tables):
-    arrivals = []
+def scatter_tails_body(wanted, start, factors, pulled, out, squares, held, scale, rows, first, in_sems, *tables):
+    arrivals = Copies(in_sems)
     parts = [pl.ds(k * SLOTS // 4, SLOTS // 4) for k in range(4)]
-    for k, part in enumerate(parts):
-        for n, (source, target) in enumerate(((pulled, held), (factors, scale))):
-            arrivals.append(pltpu.make_async_copy(source.at[part], target.at[part], in_sems.at[2 * k + n]))
-            arrivals[-1].start()
-    arrivals.append(pltpu.make_async_copy(start, first, in_sems.at[8]))
-    arrivals[-1].start()
+    needed = [
+        [arrivals.start(source.at[part], target.at[part]) for source, target in ((pulled, held), (factors, scale))]
+        for part in parts
+    ]
+    last = arrivals.start(start, first)
     begin(tables)
     for k, part in enumerate(parts):
-        arrivals[2 * k].wait()
-        arrivals[2 * k + 1].wait()
+        for copy in needed[k]:
+            copy.wait()
         rows[part, :] = scale[part, :] * held[part, :].astype(F32)
 
         @pl.loop(k * OWNERS // 4, (k + 1) * OWNERS // 4)
         def _(b):
-            base = b * LINES + place[1] * BUCKET
             for i in range(BUCKET):
                 into = tables[i % CHAINS]
-                into[pl.ds(wanted[base + i], 1), :] += rows[pl.ds(b * BUCKET + i, 1), :]
-
-    arrivals[-1].wait()
+                into[pl.ds(wanted[b * BUCKET + i], 1), :] += rows[pl.ds(b * BUCKET + i, 1), :]
+
+    last.wait()
     ones = jnp.ones((16, 2 * WIDTH), BF16)
     for k, part in enumerate(parts):
         total = first[part, :]
@@ -439,18 +466,18 @@
             squares[line : line + 1, :] = sums[0:1, n * WIDTH : (n + 1) * WIDTH]
 
 
-def scatter_tails(place, wanted, start, factors, pulled):
+def scatter_tails(wanted, start, factors, pulled):
     return call(
         scatter_tails_body,
         "scatter_tails",
         [(shape(SLOTS, F32), VMEM), (shape(SLOTS // WIDTH, F32), VMEM)],
-        [SMEM] * 2 + [HBM] * 3,
+        [SMEM] + [HBM] * 3,
         [pltpu.VMEM((SLOTS, WIDTH), BF16), TABLE, TABLE, TABLE]
         + [pltpu.SemaphoreType.DMA((9,))]
         + [TABLE] * CHAINS,
         WHOLE,
         moved=30_000_000,
-    )(place, wanted, start, factors, pulled)
+    )(wanted, start, factors, pulled)
 
 
 def stage_body(table, gradient, table_out, step_out):
@@ -470,6 +497,27 @@
     )(table, gradient)
 
 
+def pass_on_body(g1, g3, out_r, out_l, r, l, in_sems, sems):
+    arrivals, copies = Copies(in_sems), Copies(sems)
+    arrivals.start(g3.at[pl.ds(DIRECT, 2 * HALF)], r)
+    arrivals.start(g1.at[pl.ds(DIRECT, 2 * HALF)], l)
+    arrivals.wait()
+    copies.start(r, out_r)
+    copies.start(l, out_l)
+    copies.wait()
+
+
+def pass_on(g1, g3):
+    return call(
+        pass_on_body,
+        "pass_on",
+        [(shape(2 * HALF, BF16), HBM)] * 2,
+        [HBM] * 2,
+        [pltpu.VMEM((2 * HALF, WIDTH), BF16)] * 2 + [pltpu.SemaphoreType.DMA((2,))] * 2,
+        moved=1_000_000,
+    )(g1, g3)
+
+
 def shifted(x, s):
     return lax.ppermute(x, "col", [(i, (i + s) % COLS) for i in range(COLS)])
 
@@ -478,33 +526,36 @@
     embeddings, adagrad_state, relations, src_rows, dst_rows, rel_ids, bucket_counts, neg_rows
 ):
     axes = ("dom", "col")
-    place = jnp.stack([lax.axis_index("col"), lax.axis_index("dom") & 1]).astype(I32)
+    place = lax.axis_index("col").astype(I32).reshape(1)
 
     def sent(x):
         return lax.all_to_all(
             x.reshape(OWNERS * COLS, PART, WIDTH), axes, split_axis=0, concat_axis=0, tiled=True
         )
 
-    pairs = (OWNERS // 2, 2, 2, WIDTH)
-    rows, kinds = (lax.broadcast_in_dim(x.reshape(-1, WIDTH), pairs, (0, 3)) for x in (dst_rows, rel_ids))
-    words = jnp.where(lax.broadcasted_iota(I32, pairs, 2) == 0, rows, kinds).reshape(OWNERS, 2, WIDTH)
-    wanted = lax.all_to_all(words, "dom", split_axis=0, concat_axis=0, tiled=True).reshape(-1)
-
+    words = request(dst_rows, rel_ids)
+    wanted = lax.all_to_all(words, "dom", split_axis=0, concat_axis=0, tiled=True)
     via_r, via_l, negatives = gather_far(place, src_rows, neg_rows, embeddings)
     vr, vl = shifted(via_r, 1), shifted(via_l, -1)
-    weighted, factors, wanted = gather_tails(place, wanted, embeddings, relations)
+    weighted, factors = gather_tails(wanted.reshape(-1), embeddings, relations)
     weighted = sent(weighted).reshape(OWNERS, COLS, PART, WIDTH)
     after, factors, vr, vl = lax.optimization_barrier((negatives, factors, vr, vl))
     right, left = gather_near(place, src_rows, embeddings, after)
-    heads = gather_own(place, src_rows, embeddings)
-    pieces = [heads, after, shifted(right, 1), vr, shifted(left, -1), vl, shifted(vr, 1), shifted(vl, -1)]
+    near_r, near_l = shifted(right, 1), shifted(left, -1)
+    wr, wl = shifted(vr, 1), shifted(vl, -1)
+    own_rows, wr, wl = lax.optimization_barrier((src_rows, wr, wl))
+    heads = gather_own(place, own_rows, embeddings)
+    pieces = [heads, after, near_r, vr, near_l, vl, wr, wl]
     pulled, own, right, left = edge_scores(place, bucket_counts, weighted, pieces)
     pulled = sent(pulled).reshape(SLOTS, WIDTH)
     from_left, from_right = shifted(right, 1), shifted(left, -1)
-    far_a, far_b = shifted(from_left[DIRECT:], 1), shifted(from_right[DIRECT:], -1)
+    on_r, on_l = pass_on(from_right, from_left)
+    far_a, far_b = shifted(on_r, 1), shifted(on_l, -1)
     gradient = scatter_near(place, src_rows, own, from_right, from_left)
     gradient = scatter_far(place, src_rows, neg_rows, gradient, own, from_right, from_left, far_a, far_b)
-    gradient, squares = scatter_tails(place, wanted, gradient, factors, pulled)
+    gradient, squares = scatter_tails(
+        wanted[:, :BUCKET].reshape(-1), gradient, factors, pulled
+    )
 
     table, step = stage(embeddings, gradient)
     squares = (squares + shifted(squares, 2)) + (shifted(squares, 1) + shifted(squares, 3))

time: 155 us -> 151 us (0.974)
  local copies, waits for them, and re-layouts: 8.9 us -> 4.86 us
  waiting for transfers between devices: 28.7 us -> 32.5 us
    pallas_call x0 -> x2, Pallas kernels: none -> 3.29 us  [the longest x1 1.87 us: pass_on(): call(pass_on_body, 'pass_on', [(shape(2 * HALF, BF16), HBM)] * 2, [HBM] *...]
    all_to_all x2, starting transfers between devices: 24.9 us -> 22.1 us  [sent(): lax.all_to_all(x.reshape(OWNERS * COLS, PART, WIDTH), axes, split_axis=0,...]
    pallas_call x1, Pallas kernels: 10.4 us -> 8.04 us  [scatter_tails(): call(scatter_tails_body, 'scatter_tails', [(shape(SLOTS, F32), VMEM), (sh...]
    all_to_all x2, waiting for transfers between devices: 1.24 us -> 3.07 us  [sent(): lax.all_to_all(x.reshape(OWNERS * COLS, PART, WIDTH), axes, split_axis=0,...]
    unnamed x14 -> x12, local copies, waits for them, and re-layouts: 5.99 us -> 4.18 us
    ppermute x13, waiting for transfers between devices: 25.2 us -> 26.8 us  [shifted(): return lax.ppermute(x, 'col', [(i, (i + s) % COLS) for i in range(COLS)])]
  transfers between devices with their start and end apart: 16 -> 16, of which waited for: 7 -> 9; matrix products, arithmetic and copies ran while one was open for 1% -> 0% of each run, Pallas kernels for 26% -> 27%
where the time goes in v4:
time: 151 us; the launch traced here: 149 us
  Pallas kernels  57 us (38%)
  starting transfers between devices  52.1 us (35%)
  waiting for transfers between devices  32.5 us (22%)
  local copies, waits for them, and re-layouts  4.86 us (3%)
  other arithmetic  2.28 us (2%)
    ppermute x13, waiting for transfers between devices, shifted(): return lax.ppermute(x, 'col', [(i, (i + s) % COLS) for i in range(COLS)])  26.8 us
    all_to_all x2, starting transfers between devices, sent(): lax.all_to_all(x.reshape(OWNERS * COLS, PART, WIDTH), axes, split_axis=0,...  22.1 us
    ppermute x13, starting transfers between devices, shifted(): return lax.ppermute(x, 'col', [(i, (i + s) % COLS) for i in range(COLS)])  18 us
    all_to_all x1, starting transfers between devices, shards(): lax.all_to_all(words, 'dom', split_axis=0, concat_axis=0, tiled=True)  11.9 us
    pallas_call x1, Pallas kernels, gather_tails(): call(gather_tails_body, 'gather_tails', [(shape(SLOTS, BF16), HBM), (shap...  9.74 us
    pallas_call x1, Pallas kernels, scatter_tails(): call(scatter_tails_body, 'scatter_tails', [(shape(SLOTS, F32), VMEM), (sh...  8.04 us
    pallas_call x1, Pallas kernels, edge_scores(): call(edge_scores_body, 'edge_scores', [(jax.ShapeDtypeStruct(whole, BF16)...  7.87 us
    pallas_call x1, Pallas kernels, scatter_near(): call(scatter_near_body, 'scatter_near', [(shape(SLOTS, F32), VMEM)], [SME...  7.6 us
  transfers between devices with their start and end apart: 16, of which 9 were waited for; matrix products, arithmetic and copies ran while one was open for 0% of the time, Pallas kernels for 27%

profile of v4, /device:TPU:8, one launch (start us, length us, event | category | flops | bytes accessed | tf_op | source)
XLA Modules:
  0.0 149.5 jit_solution(16954435222083582455)
XLA Ops:
  0.6 1.4 request.1
  2.1 11.9 %all-to-all-start = ((s32[64,1,128]{2,1,0:T(1,128)}), s32[64,1,128]{2,1,0:T(1,128)S(1)}, u32[]{:S(2)}, u32[]{:S(2)}) async-start(s32[64,1,128]{2,1,0:T(1,128)} %bitcast.20), calls=%async_computation | async-start | bytes 65536 | tf_op jit(solution)/shard_map/all_to_all | solution.py:537
  14.0 4.7 %gather_far.1 = (bf16[1024,128]{1,0:T(8,128)(2,1)}, bf16[1024,128]{1,0:T(8,128)(2,1)}, bf16[1024,128]{1,0:T(8,128)(2,1)}) custom-call(s32[1]{0:T(128)} %bitcast.5.place.col, s32[4096]{0:T(1024)} %src.8, s32[1000]{0:T(1024)} %neg.3, f32[4096,128]{1,0:T(8,128)} %table.9), custom_call_target="tpu_custom_call" | custom-call | bytes 10000000 | tf_op jit(solution)/shard_map/gather_far/pallas_call | solution.py:96
  18.7 1.7 %collective-permute-start = (bf16[1024,128]{1,0:T(8,128)(2,1)}, bf16[1024,128]{1,0:T(8,128)(2,1)}, u32[]{:S(2)}, u32[]{:S(2)}) collective-permute-start(bf16[1024,128]{1,0:T(8,128)(2,1)} %get-tuple-element.29), channel_id=1, source_target_pairs={{0,1},{1,2},{2,3},{3,0},{4,5},{5,6},{6,7},{7,4},{8,9},{9,10},{10,1... | collective-permute-start | bytes 786440 | tf_op jit(solution)/shard_map/ppermute | solution.py:522
  20.4 0.4 collective-permute-start.1
  20.8 2.6 %all-to-all-done = s32[64,1,128]{2,1,0:T(1,128)S(1)} async-done(((s32[64,1,128]{2,1,0:T(1,128)}), s32[64,1,128]{2,1,0:T(1,128)S(1)}, u32[]{:S(2)}, u32[]{:S(2)}) %all-to-all-start) | async-done | bytes 32800 | tf_op jit(solution)/shard_map/all_to_all | solution.py:537
  23.4 0.6 copy-done.2
  24.0 9.7 %gather_tails.1 = (bf16[4096,128]{1,0:T(8,128)(2,1)}, f32[4096,128]{1,0:T(8,128)}) custom-call(s32[8192]{0:T(1024)} %bitcast.18, f32[4096,128]{1,0:T(8,128)} %table.9, f32[1345,128]{1,0:T(8,128)} %relations.1), custom_call_target="tpu_custom_call" | custom-call | flops 10000000000 | bytes 20000000 | tf_op jit(solution)/shard_map/gather_tails/pallas_call | solution.py:181
  33.8 11.4 %all-to-all-start.1 = ((bf16[256,16,128]{2,1,0:T(8,128)(2,1)}), bf16[256,16,128]{2,1,0:T(8,128)(2,1)}, u32[]{:S(2)}, u32[]{:S(2)}) async-start(bf16[256,16,128]{2,1,0:T(8,128)(2,1)} %bitcast.17), calls=%async_computation.1 | async-start | bytes 2097152 | tf_op jit(solution)/shard_map/all_to_all | solution.py:532
  45.2 0.0 collective-permute-done.vr
  45.2 1.5 %collective-permute-start.2 = (bf16[1024,128]{1,0:T(8,128)(2,1)}, bf16[1024,128]{1,0:T(8,128)(2,1)}, u32[]{:S(2)}, u32[]{:S(2)}) collective-permute-start(bf16[1024,128]{1,0:T(8,128)(2,1)} %collective-permute-done.vr), channel_id=1, source_target_pairs={{0,1},{1,2},{2,3},{3,0},{4,5},{5,6},{6,7},{7,4},{8,9},{9,10},{10,1... | collective-permute-start | bytes 786440 | tf_op jit(solution)/shard_map/ppermute | solution.py:522
  46.7 0.8 collective-permute-start.3
  47.6 4.7 %gather_near.1 = (bf16[1536,128]{1,0:T(8,128)(2,1)}, bf16[1536,128]{1,0:T(8,128)(2,1)}) custom-call(s32[1]{0:T(128)} %bitcast.5.place.col, s32[4096]{0:T(1024)} %src.8, f32[4096,128]{1,0:T(8,128)} %table.9, bf16[1024,128]{1,0:T(8,128)(2,1)} %get-tuple-element.34.corrupt.n0), custom_call_target="tpu_custom_call" | custom-call | flops 16999999488 | bytes 20000000 | tf_op jit(solution)/shard_map/gather_near/pallas_call | solution.py:125
  52.2 1.3 collective-permute-start.4
  53.5 2.1 %collective-permute-start.5 = (bf16[1536,128]{1,0:T(8,128)(2,1)}, bf16[1536,128]{1,0:T(8,128)(2,1)}, u32[]{:S(2)}, u32[]{:S(2)}) collective-permute-start(bf16[1536,128]{1,0:T(8,128)(2,1)} %get-tuple-element.36), channel_id=1, source_target_pairs={{0,3},{1,0},{2,1},{3,2},{4,7},{5,4},{6,5},{7,6},{8,11},{9,8},{10,9... | collective-permute-start | bytes 1179656 | tf_op jit(solution)/shard_map/ppermute | solution.py:522
  55.6 3.7 %collective-permute-done.2.wr = bf16[1024,128]{1,0:T(8,128)(2,1)} collective-permute-done((bf16[1024,128]{1,0:T(8,128)(2,1)}, bf16[1024,128]{1,0:T(8,128)(2,1)}, u32[]{:S(2)}, u32[]{:S(2)}) %collective-permute-start.2) | collective-permute-done | bytes 262176 | tf_op jit(solution)/shard_map/ppermute | solution.py:522
  59.3 1.2 collective-permute-done.3.wl
  60.5 3.6 %gather_own.1.h0 = bf16[1024,128]{1,0:T(8,128)(2,1)} custom-call(s32[1]{0:T(128)} %bitcast.5.place.col, s32[4096]{0:T(1024)} %src.8, f32[4096,128]{1,0:T(8,128)} %table.9), custom_call_target="tpu_custom_call" | custom-call | flops 3000000000 | bytes 3000000 | tf_op jit(solution)/shard_map/gather_own/pallas_call | solution.py:205
  64.1 7.9 %collective-permute-done.4.dr = bf16[1536,128]{1,0:T(8,128)(2,1)} collective-permute-done((bf16[1536,128]{1,0:T(8,128)(2,1)}, bf16[1536,128]{1,0:T(8,128)(2,1)}, u32[]{:S(2)}, u32[]{:S(2)}) %collective-permute-start.4) | collective-permute-done | bytes 393248 | tf_op jit(solution)/shard_map/ppermute | solution.py:522
  72.1 1.0 collective-permute-done.5.dl
  73.1 3.1 %all-to-all-done.1 = bf16[256,16,128]{2,1,0:T(8,128)(2,1)} async-done(((bf16[256,16,128]{2,1,0:T(8,128)(2,1)}), bf16[256,16,128]{2,1,0:T(8,128)(2,1)}, u32[]{:S(2)}, u32[]{:S(2)}) %all-to-all-start.1) | async-done | bytes 1048608 | tf_op jit(solution)/shard_map/all_to_all | solution.py:532
  76.1 7.9 %edge_scores.1 = (bf16[64,4,16,128]{3,2,1,0:T(8,128)(2,1)}, bf16[2048,128]{1,0:T(8,128)(2,1)}, bf16[3072,128]{1,0:T(8,128)(2,1)}, bf16[3072,128]{1,0:T(8,128)(2,1)}) custom-call(s32[1]{0:T(128)} %bitcast.5.place.col, s32[1,64]{1,0:T(1,128)} %counts.1, bf16[64,4,16,128]{3,2,1,0:T(8,128)(2,1)} %bitcast.8.weighted_in, bf16[1024,128]{1,0:T(8,128)(2,1)} %gather_own.1.h0, ...), custom_call_target="tpu_custom_call" | custom-call | flops 3200000000 | bytes 8000000 | tf_op jit(solution)/shard_map/edge_scores/pallas_call | solution.py:311
  84.0 1.6 %collective-permute-start.6 = (bf16[3072,128]{1,0:T(8,128)(2,1)}, bf16[3072,128]{1,0:T(8,128)(2,1)}, u32[]{:S(2)}, u32[]{:S(2)}) collective-permute-start(bf16[3072,128]{1,0:T(8,128)(2,1)} %get-tuple-element.40), channel_id=1, source_target_pairs={{0,3},{1,0},{2,1},{3,2},{4,7},{5,4},{6,5},{7,6},{8,11},{9,8},{10,9... | collective-permute-start | bytes 2359304 | tf_op jit(solution)/shard_map/ppermute | solution.py:522
  85.7 0.6 collective-permute-start.7
  86.3 10.8 %all-to-all-start.2 = ((bf16[256,16,128]{2,1,0:T(8,128)(2,1)}), bf16[256,16,128]{2,1,0:T(8,128)(2,1)}, u32[]{:S(2)}, u32[]{:S(2)}) async-start(bf16[256,16,128]{2,1,0:T(8,128)(2,1)} %bitcast.16), calls=%async_computation.2 | async-start | bytes 2097152 | tf_op jit(solution)/shard_map/all_to_all | solution.py:532
  97.1 0.7 reshape.40.wanted
  97.8 9.8 %collective-permute-done.6.g1 = bf16[3072,128]{1,0:T(8,128)(2,1)} collective-permute-done((bf16[3072,128]{1,0:T(8,128)(2,1)}, bf16[3072,128]{1,0:T(8,128)(2,1)}, u32[]{:S(2)}, u32[]{:S(2)}) %collective-permute-start.6) | collective-permute-done | bytes 786464 | tf_op jit(solution)/shard_map/ppermute | solution.py:522
  107.6 2.8 %collective-permute-done.7.g3 = bf16[3072,128]{1,0:T(8,128)(2,1)} collective-permute-done((bf16[3072,128]{1,0:T(8,128)(2,1)}, bf16[3072,128]{1,0:T(8,128)(2,1)}, u32[]{:S(2)}, u32[]{:S(2)}) %collective-permute-start.7) | collective-permute-done | bytes 786464 | tf_op jit(solution)/shard_map/ppermute | solution.py:522
  110.4 1.9 %pass_on.1 = (bf16[1024,128]{1,0:T(8,128)(2,1)}, bf16[1024,128]{1,0:T(8,128)(2,1)}) custom-call(bf16[3072,128]{1,0:T(8,128)(2,1)} %collective-permute-done.6.g1, bf16[3072,128]{1,0:T(8,128)(2,1)} %collective-permute-done.7.g3), custom_call_target="tpu_custom_call" | custom-call | bytes 1000000 | tf_op jit(solution)/shard_map/pass_on/pallas_call | solution.py:511
  112.2 0.1 collective-permute-start.8
  112.3 2.0 %collective-permute-start.9 = (bf16[1024,128]{1,0:T(8,128)(2,1)}, bf16[1024,128]{1,0:T(8,128)(2,1)}, u32[]{:S(2)}, u32[]{:S(2)}) collective-permute-start(bf16[1024,128]{1,0:T(8,128)(2,1)} %get-tuple-element.43), channel_id=1, source_target_pairs={{0,3},{1,0},{2,1},{3,2},{4,7},{5,4},{6,5},{7,6},{8,11},{9,8},{10,9... | collective-permute-start | bytes 786440 | tf_op jit(solution)/shard_map/ppermute | solution.py:522
  114.3 7.6 %scatter_near.1.start = f32[4096,128]{1,0:T(8,128)} custom-call(s32[1]{0:T(128)} %bitcast.5.place.col, s32[4096]{0:T(1024)} %src.8, bf16[2048,128]{1,0:T(8,128)(2,1)} %get-tuple-element.39.g0, bf16[3072,128]{1,0:T(8,128)(2,1)} %collective-permute-done.6.g1, bf16[3072,128]{1,0:T(8,128)(2,1)} %collective-permute-done.7.g3), custom_call_target="tpu_custom_call" | custom-call | flops 10000000000 | bytes 20000000 | tf_op jit(solution)/shard_map/scatter_near/pallas_call | solution.py:368
  122.0 0.0 collective-permute-done.8.wr
  122.0 0.3 collective-permute-done.9.wl
  122.3 7.2 %scatter_far.1.start = f32[4096,128]{1,0:T(8,128)} custom-call(s32[1]{0:T(128)} %bitcast.5.place.col, s32[4096]{0:T(1024)} %src.8, s32[1000]{0:T(1024)} %neg.3, f32[4096,128]{1,0:T(8,128)} %scatter_near.1.start, bf16[2048,128]{1,0:T(8,128)(2,1)} %get-tuple-element.39.g0, bf16[3072,128]{1,0:T(8,128)(2,1)} %collective-permute-done.6.g1, ...), custom_call_target="tpu_custom_call" | custom-call | flops 10000000000 | bytes 20000000 | tf_op jit(solution)/shard_map/scatter_far/pallas_call | solution.py:416
  129.4 8.0 %scatter_tails.1 = (f32[4096,128]{1,0:T(8,128)}, f32[32,128]{1,0:T(8,128)}) custom-call(s32[4096]{0:T(1024)} %reshape.40.wanted, f32[4096,128]{1,0:T(8,128)} %scatter_far.1.start, f32[4096,128]{1,0:T(8,128)} %get-tuple-element.44.factors, bf16[4096,128]{1,0:T(8,128)(2,1)} %bitcast.10.pulled), custom_call_target="tpu_custom_call" | custom-call | bytes 30000000 | tf_op jit(solution)/shard_map/scatter_tails/pallas_call | solution.py:470
  137.5 1.7 %collective-permute-start.12 = (f32[32,128]{1,0:T(8,128)}, f32[32,128]{1,0:T(8,128)S(1)}, u32[]{:S(2)}, u32[]{:S(2)}) collective-permute-start(f32[32,128]{1,0:T(8,128)} %get-tuple-element.49), channel_id=1, source_target_pairs={{0,3},{1,0},{2,1},{3,2},{4,7},{5,4},{6,5},{7,6},{8,11},{9,8},{10,9... | collective-permute-start | bytes 49160 | tf_op jit(solution)/shard_map/ppermute | solution.py:522
  139.2 0.4 collective-permute-start.11
  139.6 3.7 %collective-permute-start.10 = (f32[32,128]{1,0:T(8,128)}, f32[32,128]{1,0:T(8,128)S(1)}, u32[]{:S(2)}, u32[]{:S(2)}) collective-permute-start(f32[32,128]{1,0:T(8,128)} %get-tuple-element.49), channel_id=1, source_target_pairs={{0,2},{1,3},{2,0},{3,1},{4,6},{5,7},{6,4},{7,5},{8,10},{9,11},{10,... | collective-permute-start | bytes 49160 | tf_op jit(solution)/shard_map/ppermute | solution.py:522
  143.3 1.6 %copy-done = f32[4096,128]{1,0:T(8,128)S(1)} copy-done((f32[4096,128]{1,0:T(8,128)S(1)}, f32[4096,128]{1,0:T(8,128)}, u32[]{:S(2)}) %copy-start) | copy-done | bytes 2097176
  144.9 1.6 %copy-done.1 = f32[4096,128]{1,0:T(8,128)S(1)} copy-done((f32[4096,128]{1,0:T(8,128)S(1)}, f32[4096,128]{1,0:T(8,128)}, u32[]{:S(2)}) %copy-start.1) | copy-done | bytes 2097176
  146.5 0.3 stage.1
  146.8 0.0 collective-permute-done.11
  146.8 0.0 collective-permute-done.10
  146.8 0.4 copy-done.4
  147.2 0.0 copy-done.5
  147.2 0.6 fusion
  147.8 1.7 %divide_subtract_fusion = f32[4096,128]{1,0:T(8,128)} fusion(f32[4096,128]{1,0:T(8,128)S(1)} %get-tuple-element.47, f32[4096,128]{1,0:T(8,128)S(1)} %get-tuple-element.48, f32[4096]{0:T(1024)S(1)} %get-tuple-element.50), kind=kLoop, calls=%fused_computation | loop fusion | flops 1048576 | bytes 6307840 | tf_op jit(solution)/shard_map/sub | solution.py:563
  (10 shorter events, 0.0 us)
Async XLA Ops:
  2.1 21.4 %all-to-all-start = ((s32[64,1,128]{2,1,0:T(1,128)}), s32[64,1,128]{2,1,0:T(1,128)S(1)}, u32[]{:S(2)}, u32[]{:S(2)}) async-start(s32[64,1,128]{2,1,0:T(1,128)} %bitcast.20), calls=%async_computation | async-start | bytes 65536 | tf_op jit(solution)/shard_map/all_to_all | solution.py:537
  18.7 26.5 %collective-permute-start = (bf16[1024,128]{1,0:T(8,128)(2,1)}, bf16[1024,128]{1,0:T(8,128)(2,1)}, u32[]{:S(2)}, u32[]{:S(2)}) collective-permute-start(bf16[1024,128]{1,0:T(8,128)(2,1)} %get-tuple-element.29), channel_id=1, source_target_pairs={{0,1},{1,2},{2,3},{3,0},{4,5},{5,6},{6,7},{7,4},{8,9},{9,10},{10,1... | collective-permute-start | bytes 786440 | tf_op jit(solution)/shard_map/ppermute | solution.py:522
  20.4 24.8 %collective-permute-start.1 = (bf16[1024,128]{1,0:T(8,128)(2,1)}, bf16[1024,128]{1,0:T(8,128)(2,1)}, u32[]{:S(2)}, u32[]{:S(2)}) collective-permute-start(bf16[1024,128]{1,0:T(8,128)(2,1)} %get-tuple-element.30), channel_id=1, source_target_pairs={{0,3},{1,0},{2,1},{3,2},{4,7},{5,4},{6,5},{7,6},{8,11},{9,8},{10,9... | collective-permute-start | bytes 786440 | tf_op jit(solution)/shard_map/ppermute | solution.py:522
  23.4 0.6 copy-start.2
  33.8 42.3 %all-to-all-start.1 = ((bf16[256,16,128]{2,1,0:T(8,128)(2,1)}), bf16[256,16,128]{2,1,0:T(8,128)(2,1)}, u32[]{:S(2)}, u32[]{:S(2)}) async-start(bf16[256,16,128]{2,1,0:T(8,128)(2,1)} %bitcast.17), calls=%async_computation.1 | async-start | bytes 2097152 | tf_op jit(solution)/shard_map/all_to_all | solution.py:532
  45.2 14.1 %collective-permute-start.2 = (bf16[1024,128]{1,0:T(8,128)(2,1)}, bf16[1024,128]{1,0:T(8,128)(2,1)}, u32[]{:S(2)}, u32[]{:S(2)}) collective-permute-start(bf16[1024,128]{1,0:T(8,128)(2,1)} %collective-permute-done.vr), channel_id=1, source_target_pairs={{0,1},{1,2},{2,3},{3,0},{4,5},{5,6},{6,7},{7,4},{8,9},{9,10},{10,1... | collective-permute-start | bytes 786440 | tf_op jit(solution)/shard_map/ppermute | solution.py:522
  46.7 13.7 %collective-permute-start.3 = (bf16[1024,128]{1,0:T(8,128)(2,1)}, bf16[1024,128]{1,0:T(8,128)(2,1)}, u32[]{:S(2)}, u32[]{:S(2)}) collective-permute-start(bf16[1024,128]{1,0:T(8,128)(2,1)} %collective-permute-done.1.vl), channel_id=1, source_target_pairs={{0,3},{1,0},{2,1},{3,2},{4,7},{5,4},{6,5},{7,6},{8,11},{9,8},{10,9... | collective-permute-start | bytes 786440 | tf_op jit(solution)/shard_map/ppermute | solution.py:522
  52.2 19.8 %collective-permute-start.4 = (bf16[1536,128]{1,0:T(8,128)(2,1)}, bf16[1536,128]{1,0:T(8,128)(2,1)}, u32[]{:S(2)}, u32[]{:S(2)}) collective-permute-start(bf16[1536,128]{1,0:T(8,128)(2,1)} %get-tuple-element.35), channel_id=1, source_target_pairs={{0,1},{1,2},{2,3},{3,0},{4,5},{5,6},{6,7},{7,4},{8,9},{9,10},{10,1... | collective-permute-start | bytes 1179656 | tf_op jit(solution)/shard_map/ppermute | solution.py:522
  53.5 19.6 %collective-permute-start.5 = (bf16[1536,128]{1,0:T(8,128)(2,1)}, bf16[1536,128]{1,0:T(8,128)(2,1)}, u32[]{:S(2)}, u32[]{:S(2)}) collective-permute-start(bf16[1536,128]{1,0:T(8,128)(2,1)} %get-tuple-element.36), channel_id=1, source_target_pairs={{0,3},{1,0},{2,1},{3,2},{4,7},{5,4},{6,5},{7,6},{8,11},{9,8},{10,9... | collective-permute-start | bytes 1179656 | tf_op jit(solution)/shard_map/ppermute | solution.py:522
  84.0 13.1 %copy-start.3 = (s32[64,1,128]{2,1,0:T(1,128)S(1)}, s32[64,1,128]{2,1,0:T(1,128)}, u32[]{:S(2)}) copy-start(s32[64,1,128]{2,1,0:T(1,128)} %copy-done.2) | copy-start | bytes 98308
  84.0 23.6 %collective-permute-start.6 = (bf16[3072,128]{1,0:T(8,128)(2,1)}, bf16[3072,128]{1,0:T(8,128)(2,1)}, u32[]{:S(2)}, u32[]{:S(2)}) collective-permute-start(bf16[3072,128]{1,0:T(8,128)(2,1)} %get-tuple-element.40), channel_id=1, source_target_pairs={{0,3},{1,0},{2,1},{3,2},{4,7},{5,4},{6,5},{7,6},{8,11},{9,8},{10,9... | collective-permute-start | bytes 2359304 | tf_op jit(solution)/shard_map/ppermute | solution.py:522
  85.7 24.7 %collective-permute-start.7 = (bf16[3072,128]{1,0:T(8,128)(2,1)}, bf16[3072,128]{1,0:T(8,128)(2,1)}, u32[]{:S(2)}, u32[]{:S(2)}) collective-permute-start(bf16[3072,128]{1,0:T(8,128)(2,1)} %get-tuple-element.41), channel_id=1, source_target_pairs={{0,1},{1,2},{2,3},{3,0},{4,5},{5,6},{6,7},{7,4},{8,9},{9,10},{10,1... | collective-permute-start | bytes 2359304 | tf_op jit(solution)/shard_map/ppermute | solution.py:522
  86.3 43.1 %all-to-all-start.2 = ((bf16[256,16,128]{2,1,0:T(8,128)(2,1)}), bf16[256,16,128]{2,1,0:T(8,128)(2,1)}, u32[]{:S(2)}, u32[]{:S(2)}) async-start(bf16[256,16,128]{2,1,0:T(8,128)(2,1)} %bitcast.16), calls=%async_computation.2 | async-start | bytes 2097152 | tf_op jit(solution)/shard_map/all_to_all | solution.py:532
  112.2 9.7 %collective-permute-start.8 = (bf16[1024,128]{1,0:T(8,128)(2,1)}, bf16[1024,128]{1,0:T(8,128)(2,1)}, u32[]{:S(2)}, u32[]{:S(2)}) collective-permute-start(bf16[1024,128]{1,0:T(8,128)(2,1)} %get-tuple-element.42), channel_id=1, source_target_pairs={{0,1},{1,2},{2,3},{3,0},{4,5},{5,6},{6,7},{7,4},{8,9},{9,10},{10,1... | collective-permute-start | bytes 786440 | tf_op jit(solution)/shard_map/ppermute | solution.py:522
  112.3 9.9 %collective-permute-start.9 = (bf16[1024,128]{1,0:T(8,128)(2,1)}, bf16[1024,128]{1,0:T(8,128)(2,1)}, u32[]{:S(2)}, u32[]{:S(2)}) collective-permute-start(bf16[1024,128]{1,0:T(8,128)(2,1)} %get-tuple-element.43), channel_id=1, source_target_pairs={{0,3},{1,0},{2,1},{3,2},{4,7},{5,4},{6,5},{7,6},{8,11},{9,8},{10,9... | collective-permute-start | bytes 786440 | tf_op jit(solution)/shard_map/ppermute | solution.py:522
  137.5 9.3 %collective-permute-start.12 = (f32[32,128]{1,0:T(8,128)}, f32[32,128]{1,0:T(8,128)S(1)}, u32[]{:S(2)}, u32[]{:S(2)}) collective-permute-start(f32[32,128]{1,0:T(8,128)} %get-tuple-element.49), channel_id=1, source_target_pairs={{0,3},{1,0},{2,1},{3,2},{4,7},{5,4},{6,5},{7,6},{8,11},{9,8},{10,9... | collective-permute-start | bytes 49160 | tf_op jit(solution)/shard_map/ppermute | solution.py:522
  139.2 7.6 %collective-permute-start.11 = (f32[32,128]{1,0:T(8,128)}, f32[32,128]{1,0:T(8,128)S(1)}, u32[]{:S(2)}, u32[]{:S(2)}) collective-permute-start(f32[32,128]{1,0:T(8,128)} %get-tuple-element.49), channel_id=1, source_target_pairs={{0,1},{1,2},{2,3},{3,0},{4,5},{5,6},{6,7},{7,4},{8,9},{9,10},{10,1... | collective-permute-start | bytes 49160 | tf_op jit(solution)/shard_map/ppermute | solution.py:522
  139.6 7.3 %collective-permute-start.10 = (f32[32,128]{1,0:T(8,128)}, f32[32,128]{1,0:T(8,128)S(1)}, u32[]{:S(2)}, u32[]{:S(2)}) collective-permute-start(f32[32,128]{1,0:T(8,128)} %get-tuple-element.49), channel_id=1, source_target_pairs={{0,2},{1,3},{2,0},{3,1},{4,6},{5,7},{6,4},{7,5},{8,10},{9,11},{10,... | collective-permute-start | bytes 49160 | tf_op jit(solution)/shard_map/ppermute | solution.py:522
  143.3 1.6 %copy-start = (f32[4096,128]{1,0:T(8,128)S(1)}, f32[4096,128]{1,0:T(8,128)}, u32[]{:S(2)}) copy-start(f32[4096,128]{1,0:T(8,128)} %table.9) | copy-start | bytes 6291460
  144.9 1.6 %copy-start.1 = (f32[4096,128]{1,0:T(8,128)S(1)}, f32[4096,128]{1,0:T(8,128)}, u32[]{:S(2)}) copy-start(f32[4096,128]{1,0:T(8,128)} %get-tuple-element.46.gradient) | copy-start | bytes 6291460
  146.5 0.7 copy-start.4
  146.5 0.7 copy-start.5

commit v5 on v4

--- a/solution.py
+++ b/solution.py
@@ -17,10 +17,12 @@
 NEG = 1000
 NEG_PAD = 1024
 DIRECT = EDGES + NEG_PAD
+BUCKETS_END = OWNERS
 HALF = 512
 BLOCK = 256
 CHAINS = 8
 WHOLE = 65_300
+WORDS_STAY = 54_528
 
 F32, BF16, I32 = jnp.float32, jnp.bfloat16, jnp.int32
 SMEM = pl.BlockSpec(memory_space=pltpu.SMEM)
@@ -158,17 +160,36 @@
     )(rows.reshape(-1, WIDTH), kinds.reshape(-1, WIDTH))[0]
 
 
-def gather_tails_body(wanted, table, relations, out, factors_out, rows, factors, weighted, sems):
-    copies = Copies(sems)
+def gather_tails_body(
+    wanted_in, table_in, relations_in, out, factors_out, wanted, table, relations, rows, factors, weighted, in_sems, sems
+):
+    arrivals, copies = Copies(in_sems), Copies(sems)
+    arrivals.start(wanted_in, wanted)
+    arrivals.start(relations_in, relations)
+    last = arrivals.start(table_in, table)
+    for copy in arrivals.all[:2]:
+        copy.wait()
+
+    def factor(b, i):
+        row = wanted[b * LINE + BUCKET + i]
+        factors[pl.ds(b * BUCKET + i, 1), :] = relations[pl.ds(row, 1), :]
+
     for k in range(4):
+        if k == 0:
+
+            @pl.loop(0, OWNERS // 4)
+            def _(b):
+                for i in range(BUCKET):
+                    factor(b, i)
+
+            last.wait()
 
         @pl.loop(k * OWNERS // 4, (k + 1) * OWNERS // 4)
         def _(b):
-            base = b * LINE
             for i in range(BUCKET):
-                rows[pl.ds(b * BUCKET + i, 1), :] = table[pl.ds(wanted[base + i], 1), :]
-                row = wanted[base + BUCKET + i]
-                factors[pl.ds(b * BUCKET + i, 1), :] = relations[pl.ds(row, 1), :]
+                rows[pl.ds(b * BUCKET + i, 1), :] = table[pl.ds(wanted[b * LINE + i], 1), :]
+                if k > 0:
+                    factor(b, i)
 
         part = pl.ds(k * SLOTS // 4, SLOTS // 4)
         weighted[part, :] = (factors[part, :] * rows[part, :].astype(BF16).astype(F32)).astype(BF16)
@@ -185,9 +206,10 @@
             (shape(SLOTS, BF16), HBM),
             (shape(SLOTS, F32), HBM),
         ],
-        [SMEM, VMEM, VMEM],
-        [TABLE, TABLE, pltpu.VMEM((SLOTS, WIDTH), BF16), pltpu.SemaphoreType.DMA((8,))],
-        WHOLE,
+        [HBM] * 3,
+        [pltpu.SMEM(wanted.shape, I32), TABLE, pltpu.VMEM(relations.shape, F32), TABLE, TABLE]
+        + [pltpu.VMEM((SLOTS, WIDTH), BF16), pltpu.SemaphoreType.DMA((3,)), pltpu.SemaphoreType.DMA((8,))],
+        WORDS_STAY,
         flops=10_000_000_000,
         moved=20_000_000,
     )(wanted, table, relations)
@@ -219,12 +241,12 @@
 
 
 def edge_scores_body(
-    place, counts, weighted_in, h0, n0, dr, vr, dl, vl, wr, wl, pulled_out, own, right, left, *rest
+    settings_in, weighted_in, h0, n0, dr, vr, dl, vl, wr, wl, pulled_out, own, right, left, *rest
 ):
-    weighted, heads, corrupt, grad_scores, pulled, o, r, l, in_sems, sems = rest
-    owner = [(place[0] + COLS - s) & (COLS - 1) for s in range(COLS)]
+    settings, weighted, heads, corrupt, grad_scores, pulled, o, r, l, in_sems, sems = rest
     span = [slice(s * WIDTH, (s + 1) * WIDTH) for s in range(COLS)]
     arrivals, copies = Copies(in_sems), Copies(sems)
+    for_masks = arrivals.start(settings_in, settings)
 
     def fetch(source, begin, target, row, s, n):
         return arrivals.start(source.at[pl.ds(begin, n)], target.at[pl.ds(row, n), pl.ds(s * WIDTH, WIDTH)])
@@ -248,6 +270,9 @@
         fetch(wl, 0, heads, HALF, 2, HALF),
         fetch(dl, 0, heads, 0, 3, EDGES),
     ]
+    for_masks.wait()
+    place = settings[0, BUCKETS_END]
+    owner = [(place + COLS - s) & (COLS - 1) for s in range(COLS)]
     for copy in for_scores:
         copy.wait()
 
@@ -259,12 +284,12 @@
             copies.start(held.at[pl.ds(begins, n)], out.at[pl.ds(begins, n)])
 
     negatives = corrupt[...]
-    slot = lax.broadcasted_iota(I32, (PART, 1), 0) + place[0] * PART
+    slot = lax.broadcasted_iota(I32, (PART, 1), 0) + place * PART
     whole = []
     for k in range(EDGES // BLOCK):
         rows = slice(k * BLOCK, (k + 1) * BLOCK)
         live = jnp.concatenate(
-            [(slot < counts[0, b]).astype(F32) for b in range(k * buckets, (k + 1) * buckets)], axis=0
+            [(slot < settings[0, b]).astype(F32) for b in range(k * buckets, (k + 1) * buckets)], axis=0
         )
         for_weights[k].wait()
         wk = jnp.concatenate(
@@ -305,15 +330,16 @@
     copies.wait()
 
 
-def edge_scores(place, counts, weighted, pieces):
+def edge_scores(settings, weighted, pieces):
     whole = (OWNERS, COLS, PART, WIDTH)
     sizes = (DIRECT, DIRECT + 2 * HALF, DIRECT + 2 * HALF)
     return call(
         edge_scores_body,
         "edge_scores",
         [(jax.ShapeDtypeStruct(whole, BF16), HBM)] + [(shape(n, BF16), HBM) for n in sizes],
-        [SMEM, SMEM] + [HBM] * 9,
+        [HBM] * 10,
         [
+            pltpu.SMEM(settings.shape, I32),
             pltpu.VMEM(whole, BF16),
             pltpu.VMEM((EDGES, FULL), BF16),
             pltpu.VMEM((NEG_PAD, FULL), BF16),
@@ -321,11 +347,11 @@
             pltpu.VMEM(whole, BF16),
         ]
         + [pltpu.VMEM((n, WIDTH), BF16) for n in sizes]
-        + [pltpu.SemaphoreType.DMA((16,)), pltpu.SemaphoreType.DMA((36,))],
+        + [pltpu.SemaphoreType.DMA((17,)), pltpu.SemaphoreType.DMA((36,))],
         WHOLE,
         flops=3_200_000_000,
         moved=8_000_000,
-    )(place, counts, weighted, *pieces)
+    )(settings, weighted, *pieces)
 
 
 def begin(tables, start=None):
@@ -428,8 +454,11 @@
     )(col, src, neg, start, g0, g1, g3, wr, wl)[0]
 
 
-def scatter_tails_body(wanted, start, factors, pulled, out, squares, held, scale, rows, first, in_sems, *tables):
+def scatter_tails_body(
+    wanted_in, start, factors, pulled, out, squares, wanted, held, scale, rows, first, in_sems, *tables
+):
     arrivals = Copies(in_sems)
+    for_rows = arrivals.start(wanted_in, wanted)
     parts = [pl.ds(k * SLOTS // 4, SLOTS // 4) for k in range(4)]
     needed = [
         [arrivals.start(source.at[part], target.at[part]) for source, target in ((pulled, held), (factors, scale))]
@@ -437,6 +466,7 @@
     ]
     last = arrivals.start(start, first)
     begin(tables)
+    for_rows.wait()
     for k, part in enumerate(parts):
         for copy in needed[k]:
             copy.wait()
@@ -471,9 +501,9 @@
         scatter_tails_body,
         "scatter_tails",
         [(shape(SLOTS, F32), VMEM), (shape(SLOTS // WIDTH, F32), VMEM)],
-        [SMEM] + [HBM] * 3,
-        [pltpu.VMEM((SLOTS, WIDTH), BF16), TABLE, TABLE, TABLE]
-        + [pltpu.SemaphoreType.DMA((9,))]
+        [HBM] * 4,
+        [pltpu.SMEM((SLOTS,), I32), pltpu.VMEM((SLOTS, WIDTH), BF16), TABLE, TABLE, TABLE]
+        + [pltpu.SemaphoreType.DMA((10,))]
         + [TABLE] * CHAINS,
         WHOLE,
         moved=30_000_000,
@@ -527,6 +557,7 @@
 ):
     axes = ("dom", "col")
     place = lax.axis_index("col").astype(I32).reshape(1)
+    settings = jnp.concatenate([bucket_counts, jnp.broadcast_to(place, bucket_counts.shape)], axis=1)
 
     def sent(x):
         return lax.all_to_all(
@@ -546,7 +577,7 @@
     own_rows, wr, wl = lax.optimization_barrier((src_rows, wr, wl))
     heads = gather_own(place, own_rows, embeddings)
     pieces = [heads, after, near_r, vr, near_l, vl, wr, wl]
-    pulled, own, right, left = edge_scores(place, bucket_counts, weighted, pieces)
+    pulled, own, right, left = edge_scores(settings, weighted, pieces)
     pulled = sent(pulled).reshape(SLOTS, WIDTH)
     from_left, from_right = shifted(right, 1), shifted(left, -1)
     on_r, on_l = pass_on(from_right, from_left)

time: 151 us -> 148 us (0.980)
  Pallas kernels: 57 us -> 54.8 us
    unnamed x12 -> x10, local copies, waits for them, and re-layouts: 4.18 us -> 3.57 us
  transfers between devices with their start and end apart: 16 -> 16, of which waited for: 9 -> 9; matrix products, arithmetic and copies ran while one was open for 0% -> 1% of each run, Pallas kernels for 27% -> 27%
where the time goes in v5:
time: 148 us; the launch traced here: 147 us
  Pallas kernels  54.8 us (37%)
  starting transfers between devices  52.1 us (35%)
  waiting for transfers between devices  32 us (22%)
  local copies, waits for them, and re-layouts  4.76 us (3%)
  other arithmetic  2.28 us (2%)
    ppermute x13, waiting for transfers between devices, shifted(): return lax.ppermute(x, 'col', [(i, (i + s) % COLS) for i in range(COLS)])  26.3 us
    all_to_all x2, starting transfers between devices, sent(): lax.all_to_all(x.reshape(OWNERS * COLS, PART, WIDTH), axes, split_axis=0,...  22.2 us
    ppermute x13, starting transfers between devices, shifted(): return lax.ppermute(x, 'col', [(i, (i + s) % COLS) for i in range(COLS)])  18 us
    all_to_all x1, starting transfers between devices, shards(): lax.all_to_all(words, 'dom', split_axis=0, concat_axis=0, tiled=True)  11.9 us
    pallas_call x1, Pallas kernels, gather_tails(): call(gather_tails_body, 'gather_tails', [(shape(SLOTS, BF16), HBM), (shap...  9.19 us
    pallas_call x1, Pallas kernels, scatter_near(): call(scatter_near_body, 'scatter_near', [(shape(SLOTS, F32), VMEM)], [SME...  7.59 us
    pallas_call x1, Pallas kernels, edge_scores(): call(edge_scores_body, 'edge_scores', [(jax.ShapeDtypeStruct(whole, BF16)...  7.19 us
    pallas_call x1, Pallas kernels, scatter_far(): call(scatter_far_body, 'scatter_far', [(shape(SLOTS, F32), VMEM)], [SMEM]...  7.14 us
  transfers between devices with their start and end apart: 16, of which 9 were waited for; matrix products, arithmetic and copies ran while one was open for 1% of the time, Pallas kernels for 27%

profile of v5, /device:TPU:8, one launch (start us, length us, event | category | flops | bytes accessed | tf_op | source)
XLA Modules:
  0.0 146.7 jit_solution(16479824813610830493)
XLA Ops:
  0.6 1.4 request.1
  2.1 11.9 %all-to-all-start = ((s32[64,1,128]{2,1,0:T(1,128)}), s32[64,1,128]{2,1,0:T(1,128)S(1)}, u32[]{:S(2)}, u32[]{:S(2)}) async-start(s32[64,1,128]{2,1,0:T(1,128)} %bitcast.20), calls=%async_computation | async-start | bytes 65536 | tf_op jit(solution)/shard_map/all_to_all | solution.py:568
  14.0 4.7 %gather_far.1 = (bf16[1024,128]{1,0:T(8,128)(2,1)}, bf16[1024,128]{1,0:T(8,128)(2,1)}, bf16[1024,128]{1,0:T(8,128)(2,1)}) custom-call(s32[1]{0:T(128)} %bitcast.5.place.col, s32[4096]{0:T(1024)} %src.8, s32[1000]{0:T(1024)} %neg.3, f32[4096,128]{1,0:T(8,128)} %table.7), custom_call_target="tpu_custom_call" | custom-call | bytes 10000000 | tf_op jit(solution)/shard_map/gather_far/pallas_call | solution.py:98
  18.7 1.7 %collective-permute-start = (bf16[1024,128]{1,0:T(8,128)(2,1)}, bf16[1024,128]{1,0:T(8,128)(2,1)}, u32[]{:S(2)}, u32[]{:S(2)}) collective-permute-start(bf16[1024,128]{1,0:T(8,128)(2,1)} %get-tuple-element.29), channel_id=1, source_target_pairs={{0,1},{1,2},{2,3},{3,0},{4,5},{5,6},{6,7},{7,4},{8,9},{9,10},{10,1... | collective-permute-start | bytes 786440 | tf_op jit(solution)/shard_map/ppermute | solution.py:552
  20.4 0.4 collective-permute-start.1
  20.8 2.6 %all-to-all-done = s32[64,1,128]{2,1,0:T(1,128)S(1)} async-done(((s32[64,1,128]{2,1,0:T(1,128)}), s32[64,1,128]{2,1,0:T(1,128)S(1)}, u32[]{:S(2)}, u32[]{:S(2)}) %all-to-all-start) | async-done | bytes 32800 | tf_op jit(solution)/shard_map/all_to_all | solution.py:568
  23.4 9.2 %gather_tails.1 = (bf16[4096,128]{1,0:T(8,128)(2,1)}, f32[4096,128]{1,0:T(8,128)}) custom-call(s32[8192]{0:T(1024)S(1)} %bitcast.16, f32[4096,128]{1,0:T(8,128)} %table.7, f32[1345,128]{1,0:T(8,128)} %relations_in.1), custom_call_target="tpu_custom_call" | custom-call | flops 10000000000 | bytes 20000000 | tf_op jit(solution)/shard_map/gather_tails/pallas_call | solution.py:202
  32.6 11.4 %all-to-all-start.1 = ((bf16[256,16,128]{2,1,0:T(8,128)(2,1)}), bf16[256,16,128]{2,1,0:T(8,128)(2,1)}, u32[]{:S(2)}, u32[]{:S(2)}) async-start(bf16[256,16,128]{2,1,0:T(8,128)(2,1)} %bitcast.19), calls=%async_computation.1 | async-start | bytes 2097152 | tf_op jit(solution)/shard_map/all_to_all | solution.py:563
  44.0 0.0 collective-permute-done.1.vl
  44.0 0.0 copy-start.4
  44.1 1.5 %collective-permute-start.2 = (bf16[1024,128]{1,0:T(8,128)(2,1)}, bf16[1024,128]{1,0:T(8,128)(2,1)}, u32[]{:S(2)}, u32[]{:S(2)}) collective-permute-start(bf16[1024,128]{1,0:T(8,128)(2,1)} %collective-permute-done.vr), channel_id=1, source_target_pairs={{0,1},{1,2},{2,3},{3,0},{4,5},{5,6},{6,7},{7,4},{8,9},{9,10},{10,1... | collective-permute-start | bytes 786440 | tf_op jit(solution)/shard_map/ppermute | solution.py:552
  45.6 0.8 collective-permute-start.3
  46.4 4.7 %gather_near.1 = (bf16[1536,128]{1,0:T(8,128)(2,1)}, bf16[1536,128]{1,0:T(8,128)(2,1)}) custom-call(s32[1]{0:T(128)} %bitcast.5.place.col, s32[4096]{0:T(1024)} %src.8, f32[4096,128]{1,0:T(8,128)} %table.7, bf16[1024,128]{1,0:T(8,128)(2,1)} %get-tuple-element.34.corrupt.n0), custom_call_target="tpu_custom_call" | custom-call | flops 16999999488 | bytes 20000000 | tf_op jit(solution)/shard_map/gather_near/pallas_call | solution.py:127
  51.1 1.3 collective-permute-start.4
  52.4 2.1 %collective-permute-start.5 = (bf16[1536,128]{1,0:T(8,128)(2,1)}, bf16[1536,128]{1,0:T(8,128)(2,1)}, u32[]{:S(2)}, u32[]{:S(2)}) collective-permute-start(bf16[1536,128]{1,0:T(8,128)(2,1)} %get-tuple-element.36), channel_id=1, source_target_pairs={{0,3},{1,0},{2,1},{3,2},{4,7},{5,4},{6,5},{7,6},{8,11},{9,8},{10,9... | collective-permute-start | bytes 1179656 | tf_op jit(solution)/shard_map/ppermute | solution.py:552
  54.4 0.5 concatenate.3.settings_in
  54.9 3.2 %collective-permute-done.2.wr = bf16[1024,128]{1,0:T(8,128)(2,1)} collective-permute-done((bf16[1024,128]{1,0:T(8,128)(2,1)}, bf16[1024,128]{1,0:T(8,128)(2,1)}, u32[]{:S(2)}, u32[]{:S(2)}) %collective-permute-start.2) | collective-permute-done | bytes 262176 | tf_op jit(solution)/shard_map/ppermute | solution.py:552
  58.1 1.2 collective-permute-done.3.wl
  59.4 3.6 %gather_own.1.h0 = bf16[1024,128]{1,0:T(8,128)(2,1)} custom-call(s32[1]{0:T(128)} %bitcast.5.place.col, s32[4096]{0:T(1024)} %src.8, f32[4096,128]{1,0:T(8,128)} %table.7), custom_call_target="tpu_custom_call" | custom-call | flops 3000000000 | bytes 3000000 | tf_op jit(solution)/shard_map/gather_own/pallas_call | solution.py:227
  63.0 7.9 %collective-permute-done.4.dr = bf16[1536,128]{1,0:T(8,128)(2,1)} collective-permute-done((bf16[1536,128]{1,0:T(8,128)(2,1)}, bf16[1536,128]{1,0:T(8,128)(2,1)}, u32[]{:S(2)}, u32[]{:S(2)}) %collective-permute-start.4) | collective-permute-done | bytes 393248 | tf_op jit(solution)/shard_map/ppermute | solution.py:552
  70.9 1.0 collective-permute-done.5.dl
  71.9 3.1 %all-to-all-done.1 = bf16[256,16,128]{2,1,0:T(8,128)(2,1)} async-done(((bf16[256,16,128]{2,1,0:T(8,128)(2,1)}), bf16[256,16,128]{2,1,0:T(8,128)(2,1)}, u32[]{:S(2)}, u32[]{:S(2)}) %all-to-all-start.1) | async-done | bytes 1048608 | tf_op jit(solution)/shard_map/all_to_all | solution.py:563
  75.0 7.2 %edge_scores.1 = (bf16[64,4,16,128]{3,2,1,0:T(8,128)(2,1)}, bf16[2048,128]{1,0:T(8,128)(2,1)}, bf16[3072,128]{1,0:T(8,128)(2,1)}, bf16[3072,128]{1,0:T(8,128)(2,1)}) custom-call(s32[1,128]{1,0:T(1,128)} %concatenate.3.settings_in, bf16[64,4,16,128]{3,2,1,0:T(8,128)(2,1)} %bitcast.8.weighted_in, bf16[1024,128]{1,0:T(8,128)(2,1)} %gather_own.1.h0, ...), custom_call_target="tpu_custom_call" | custom-call | flops 3200000000 | bytes 8000000 | tf_op jit(solution)/shard_map/edge_scores/pallas_call | solution.py:336
  82.2 1.6 %collective-permute-start.6 = (bf16[3072,128]{1,0:T(8,128)(2,1)}, bf16[3072,128]{1,0:T(8,128)(2,1)}, u32[]{:S(2)}, u32[]{:S(2)}) collective-permute-start(bf16[3072,128]{1,0:T(8,128)(2,1)} %get-tuple-element.40), channel_id=1, source_target_pairs={{0,3},{1,0},{2,1},{3,2},{4,7},{5,4},{6,5},{7,6},{8,11},{9,8},{10,9... | collective-permute-start | bytes 2359304 | tf_op jit(solution)/shard_map/ppermute | solution.py:552
  83.8 0.6 collective-permute-start.7
  84.5 10.8 %all-to-all-start.2 = ((bf16[256,16,128]{2,1,0:T(8,128)(2,1)}), bf16[256,16,128]{2,1,0:T(8,128)(2,1)}, u32[]{:S(2)}, u32[]{:S(2)}) async-start(bf16[256,16,128]{2,1,0:T(8,128)(2,1)} %bitcast.18), calls=%async_computation.2 | async-start | bytes 2097152 | tf_op jit(solution)/shard_map/all_to_all | solution.py:563
  95.2 0.7 reshape.40.wanted_in
  95.9 9.9 %collective-permute-done.6.g1 = bf16[3072,128]{1,0:T(8,128)(2,1)} collective-permute-done((bf16[3072,128]{1,0:T(8,128)(2,1)}, bf16[3072,128]{1,0:T(8,128)(2,1)}, u32[]{:S(2)}, u32[]{:S(2)}) %collective-permute-start.6) | collective-permute-done | bytes 786464 | tf_op jit(solution)/shard_map/ppermute | solution.py:552
  105.8 2.7 %collective-permute-done.7.g3 = bf16[3072,128]{1,0:T(8,128)(2,1)} collective-permute-done((bf16[3072,128]{1,0:T(8,128)(2,1)}, bf16[3072,128]{1,0:T(8,128)(2,1)}, u32[]{:S(2)}, u32[]{:S(2)}) %collective-permute-start.7) | collective-permute-done | bytes 786464 | tf_op jit(solution)/shard_map/ppermute | solution.py:552
  108.5 1.9 %pass_on.1 = (bf16[1024,128]{1,0:T(8,128)(2,1)}, bf16[1024,128]{1,0:T(8,128)(2,1)}) custom-call(bf16[3072,128]{1,0:T(8,128)(2,1)} %collective-permute-done.6.g1, bf16[3072,128]{1,0:T(8,128)(2,1)} %collective-permute-done.7.g3), custom_call_target="tpu_custom_call" | custom-call | bytes 1000000 | tf_op jit(solution)/shard_map/pass_on/pallas_call | solution.py:541
  110.4 0.1 collective-permute-start.8
  110.5 2.0 %collective-permute-start.9 = (bf16[1024,128]{1,0:T(8,128)(2,1)}, bf16[1024,128]{1,0:T(8,128)(2,1)}, u32[]{:S(2)}, u32[]{:S(2)}) collective-permute-start(bf16[1024,128]{1,0:T(8,128)(2,1)} %get-tuple-element.43), channel_id=1, source_target_pairs={{0,3},{1,0},{2,1},{3,2},{4,7},{5,4},{6,5},{7,6},{8,11},{9,8},{10,9... | collective-permute-start | bytes 786440 | tf_op jit(solution)/shard_map/ppermute | solution.py:552
  112.5 7.6 %scatter_near.1.start = f32[4096,128]{1,0:T(8,128)} custom-call(s32[1]{0:T(128)} %bitcast.5.place.col, s32[4096]{0:T(1024)} %src.8, bf16[2048,128]{1,0:T(8,128)(2,1)} %get-tuple-element.39.g0, bf16[3072,128]{1,0:T(8,128)(2,1)} %collective-permute-done.6.g1, bf16[3072,128]{1,0:T(8,128)(2,1)} %collective-permute-done.7.g3), custom_call_target="tpu_custom_call" | custom-call | flops 10000000000 | bytes 20000000 | tf_op jit(solution)/shard_map/scatter_near/pallas_call | solution.py:394
  120.1 0.3 collective-permute-done.9.wl
  120.4 7.1 %scatter_far.1.start = f32[4096,128]{1,0:T(8,128)} custom-call(s32[1]{0:T(128)} %bitcast.5.place.col, s32[4096]{0:T(1024)} %src.8, s32[1000]{0:T(1024)} %neg.3, f32[4096,128]{1,0:T(8,128)} %scatter_near.1.start, bf16[2048,128]{1,0:T(8,128)(2,1)} %get-tuple-element.39.g0, bf16[3072,128]{1,0:T(8,128)(2,1)} %collective-permute-done.6.g1, ...), custom_call_target="tpu_custom_call" | custom-call | flops 10000000000 | bytes 20000000 | tf_op jit(solution)/shard_map/scatter_far/pallas_call | solution.py:442
  127.6 7.1 %scatter_tails.1 = (f32[4096,128]{1,0:T(8,128)}, f32[32,128]{1,0:T(8,128)}) custom-call(s32[4096]{0:T(1024)} %reshape.40.wanted_in, f32[4096,128]{1,0:T(8,128)} %scatter_far.1.start, f32[4096,128]{1,0:T(8,128)} %get-tuple-element.44.factors, bf16[4096,128]{1,0:T(8,128)(2,1)} %bitcast.10.pulled), custom_call_target="tpu_custom_call" | custom-call | bytes 30000000 | tf_op jit(solution)/shard_map/scatter_tails/pallas_call | solution.py:500
  134.7 1.7 %collective-permute-start.12 = (f32[32,128]{1,0:T(8,128)}, f32[32,128]{1,0:T(8,128)S(1)}, u32[]{:S(2)}, u32[]{:S(2)}) collective-permute-start(f32[32,128]{1,0:T(8,128)} %get-tuple-element.49), channel_id=1, source_target_pairs={{0,3},{1,0},{2,1},{3,2},{4,7},{5,4},{6,5},{7,6},{8,11},{9,8},{10,9... | collective-permute-start | bytes 49160 | tf_op jit(solution)/shard_map/ppermute | solution.py:552
  136.4 0.4 collective-permute-start.11
  136.8 3.7 %collective-permute-start.10 = (f32[32,128]{1,0:T(8,128)}, f32[32,128]{1,0:T(8,128)S(1)}, u32[]{:S(2)}, u32[]{:S(2)}) collective-permute-start(f32[32,128]{1,0:T(8,128)} %get-tuple-element.49), channel_id=1, source_target_pairs={{0,2},{1,3},{2,0},{3,1},{4,6},{5,7},{6,4},{7,5},{8,10},{9,11},{10,... | collective-permute-start | bytes 49160 | tf_op jit(solution)/shard_map/ppermute | solution.py:552
  140.5 1.6 %copy-done = f32[4096,128]{1,0:T(8,128)S(1)} copy-done((f32[4096,128]{1,0:T(8,128)S(1)}, f32[4096,128]{1,0:T(8,128)}, u32[]{:S(2)}) %copy-start) | copy-done | bytes 2097176
  142.1 1.6 %copy-done.1 = f32[4096,128]{1,0:T(8,128)S(1)} copy-done((f32[4096,128]{1,0:T(8,128)S(1)}, f32[4096,128]{1,0:T(8,128)}, u32[]{:S(2)}) %copy-start.1) | copy-done | bytes 2097176
  143.7 0.3 stage.1
  144.0 0.0 collective-permute-done.11
  144.1 0.0 collective-permute-done.10
  144.1 0.4 copy-done.2
  144.4 0.0 copy-done.3
  144.4 0.6 fusion
  145.1 1.7 %divide_subtract_fusion = f32[4096,128]{1,0:T(8,128)} fusion(f32[4096,128]{1,0:T(8,128)S(1)} %get-tuple-element.47, f32[4096,128]{1,0:T(8,128)S(1)} %get-tuple-element.48, f32[4096]{0:T(1024)S(1)} %get-tuple-element.50), kind=kLoop, calls=%fused_computation | loop fusion | flops 1048576 | bytes 6307840 | tf_op jit(solution)/shard_map/sub | solution.py:594
  (9 shorter events, 0.0 us)
Async XLA Ops:
  2.1 21.4 %all-to-all-start = ((s32[64,1,128]{2,1,0:T(1,128)}), s32[64,1,128]{2,1,0:T(1,128)S(1)}, u32[]{:S(2)}, u32[]{:S(2)}) async-start(s32[64,1,128]{2,1,0:T(1,128)} %bitcast.20), calls=%async_computation | async-start | bytes 65536 | tf_op jit(solution)/shard_map/all_to_all | solution.py:568
  18.7 25.3 %collective-permute-start = (bf16[1024,128]{1,0:T(8,128)(2,1)}, bf16[1024,128]{1,0:T(8,128)(2,1)}, u32[]{:S(2)}, u32[]{:S(2)}) collective-permute-start(bf16[1024,128]{1,0:T(8,128)(2,1)} %get-tuple-element.29), channel_id=1, source_target_pairs={{0,1},{1,2},{2,3},{3,0},{4,5},{5,6},{6,7},{7,4},{8,9},{9,10},{10,1... | collective-permute-start | bytes 786440 | tf_op jit(solution)/shard_map/ppermute | solution.py:552
  20.4 23.7 %collective-permute-start.1 = (bf16[1024,128]{1,0:T(8,128)(2,1)}, bf16[1024,128]{1,0:T(8,128)(2,1)}, u32[]{:S(2)}, u32[]{:S(2)}) collective-permute-start(bf16[1024,128]{1,0:T(8,128)(2,1)} %get-tuple-element.30), channel_id=1, source_target_pairs={{0,3},{1,0},{2,1},{3,2},{4,7},{5,4},{6,5},{7,6},{8,11},{9,8},{10,9... | collective-permute-start | bytes 786440 | tf_op jit(solution)/shard_map/ppermute | solution.py:552
  32.6 42.3 %all-to-all-start.1 = ((bf16[256,16,128]{2,1,0:T(8,128)(2,1)}), bf16[256,16,128]{2,1,0:T(8,128)(2,1)}, u32[]{:S(2)}, u32[]{:S(2)}) async-start(bf16[256,16,128]{2,1,0:T(8,128)(2,1)} %bitcast.19), calls=%async_computation.1 | async-start | bytes 2097152 | tf_op jit(solution)/shard_map/all_to_all | solution.py:563
  44.0 10.4 %copy-start.4 = (s32[1,64]{1,0:T(1,128)S(1)}, s32[1,64]{1,0:T(1,128)}, u32[]{:S(2)}) copy-start(s32[1,64]{1,0:T(1,128)} %param.14) | copy-start | bytes 772
  44.1 14.1 %collective-permute-start.2 = (bf16[1024,128]{1,0:T(8,128)(2,1)}, bf16[1024,128]{1,0:T(8,128)(2,1)}, u32[]{:S(2)}, u32[]{:S(2)}) collective-permute-start(bf16[1024,128]{1,0:T(8,128)(2,1)} %collective-permute-done.vr), channel_id=1, source_target_pairs={{0,1},{1,2},{2,3},{3,0},{4,5},{5,6},{6,7},{7,4},{8,9},{9,10},{10,1... | collective-permute-start | bytes 786440 | tf_op jit(solution)/shard_map/ppermute | solution.py:552
  45.6 13.8 %collective-permute-start.3 = (bf16[1024,128]{1,0:T(8,128)(2,1)}, bf16[1024,128]{1,0:T(8,128)(2,1)}, u32[]{:S(2)}, u32[]{:S(2)}) collective-permute-start(bf16[1024,128]{1,0:T(8,128)(2,1)} %collective-permute-done.1.vl), channel_id=1, source_target_pairs={{0,3},{1,0},{2,1},{3,2},{4,7},{5,4},{6,5},{7,6},{8,11},{9,8},{10,9... | collective-permute-start | bytes 786440 | tf_op jit(solution)/shard_map/ppermute | solution.py:552
  51.1 19.8 %collective-permute-start.4 = (bf16[1536,128]{1,0:T(8,128)(2,1)}, bf16[1536,128]{1,0:T(8,128)(2,1)}, u32[]{:S(2)}, u32[]{:S(2)}) collective-permute-start(bf16[1536,128]{1,0:T(8,128)(2,1)} %get-tuple-element.35), channel_id=1, source_target_pairs={{0,1},{1,2},{2,3},{3,0},{4,5},{5,6},{6,7},{7,4},{8,9},{9,10},{10,1... | collective-permute-start | bytes 1179656 | tf_op jit(solution)/shard_map/ppermute | solution.py:552
  52.4 19.6 %collective-permute-start.5 = (bf16[1536,128]{1,0:T(8,128)(2,1)}, bf16[1536,128]{1,0:T(8,128)(2,1)}, u32[]{:S(2)}, u32[]{:S(2)}) collective-permute-start(bf16[1536,128]{1,0:T(8,128)(2,1)} %get-tuple-element.36), channel_id=1, source_target_pairs={{0,3},{1,0},{2,1},{3,2},{4,7},{5,4},{6,5},{7,6},{8,11},{9,8},{10,9... | collective-permute-start | bytes 1179656 | tf_op jit(solution)/shard_map/ppermute | solution.py:552
  82.2 23.7 %collective-permute-start.6 = (bf16[3072,128]{1,0:T(8,128)(2,1)}, bf16[3072,128]{1,0:T(8,128)(2,1)}, u32[]{:S(2)}, u32[]{:S(2)}) collective-permute-start(bf16[3072,128]{1,0:T(8,128)(2,1)} %get-tuple-element.40), channel_id=1, source_target_pairs={{0,3},{1,0},{2,1},{3,2},{4,7},{5,4},{6,5},{7,6},{8,11},{9,8},{10,9... | collective-permute-start | bytes 2359304 | tf_op jit(solution)/shard_map/ppermute | solution.py:552
  83.8 24.7 %collective-permute-start.7 = (bf16[3072,128]{1,0:T(8,128)(2,1)}, bf16[3072,128]{1,0:T(8,128)(2,1)}, u32[]{:S(2)}, u32[]{:S(2)}) collective-permute-start(bf16[3072,128]{1,0:T(8,128)(2,1)} %get-tuple-element.41), channel_id=1, source_target_pairs={{0,1},{1,2},{2,3},{3,0},{4,5},{5,6},{6,7},{7,4},{8,9},{9,10},{10,1... | collective-permute-start | bytes 2359304 | tf_op jit(solution)/shard_map/ppermute | solution.py:552
  84.5 43.1 %all-to-all-start.2 = ((bf16[256,16,128]{2,1,0:T(8,128)(2,1)}), bf16[256,16,128]{2,1,0:T(8,128)(2,1)}, u32[]{:S(2)}, u32[]{:S(2)}) async-start(bf16[256,16,128]{2,1,0:T(8,128)(2,1)} %bitcast.18), calls=%async_computation.2 | async-start | bytes 2097152 | tf_op jit(solution)/shard_map/all_to_all | solution.py:563
  110.4 9.7 %collective-permute-start.8 = (bf16[1024,128]{1,0:T(8,128)(2,1)}, bf16[1024,128]{1,0:T(8,128)(2,1)}, u32[]{:S(2)}, u32[]{:S(2)}) collective-permute-start(bf16[1024,128]{1,0:T(8,128)(2,1)} %get-tuple-element.42), channel_id=1, source_target_pairs={{0,1},{1,2},{2,3},{3,0},{4,5},{5,6},{6,7},{7,4},{8,9},{9,10},{10,1... | collective-permute-start | bytes 786440 | tf_op jit(solution)/shard_map/ppermute | solution.py:552
  110.5 9.9 %collective-permute-start.9 = (bf16[1024,128]{1,0:T(8,128)(2,1)}, bf16[1024,128]{1,0:T(8,128)(2,1)}, u32[]{:S(2)}, u32[]{:S(2)}) collective-permute-start(bf16[1024,128]{1,0:T(8,128)(2,1)} %get-tuple-element.43), channel_id=1, source_target_pairs={{0,3},{1,0},{2,1},{3,2},{4,7},{5,4},{6,5},{7,6},{8,11},{9,8},{10,9... | collective-permute-start | bytes 786440 | tf_op jit(solution)/shard_map/ppermute | solution.py:552
  134.7 9.3 %collective-permute-start.12 = (f32[32,128]{1,0:T(8,128)}, f32[32,128]{1,0:T(8,128)S(1)}, u32[]{:S(2)}, u32[]{:S(2)}) collective-permute-start(f32[32,128]{1,0:T(8,128)} %get-tuple-element.49), channel_id=1, source_target_pairs={{0,3},{1,0},{2,1},{3,2},{4,7},{5,4},{6,5},{7,6},{8,11},{9,8},{10,9... | collective-permute-start | bytes 49160 | tf_op jit(solution)/shard_map/ppermute | solution.py:552
  136.4 7.6 %collective-permute-start.11 = (f32[32,128]{1,0:T(8,128)}, f32[32,128]{1,0:T(8,128)S(1)}, u32[]{:S(2)}, u32[]{:S(2)}) collective-permute-start(f32[32,128]{1,0:T(8,128)} %get-tuple-element.49), channel_id=1, source_target_pairs={{0,1},{1,2},{2,3},{3,0},{4,5},{5,6},{6,7},{7,4},{8,9},{9,10},{10,1... | collective-permute-start | bytes 49160 | tf_op jit(solution)/shard_map/ppermute | solution.py:552
  136.8 7.2 %collective-permute-start.10 = (f32[32,128]{1,0:T(8,128)}, f32[32,128]{1,0:T(8,128)S(1)}, u32[]{:S(2)}, u32[]{:S(2)}) collective-permute-start(f32[32,128]{1,0:T(8,128)} %get-tuple-element.49), channel_id=1, source_target_pairs={{0,2},{1,3},{2,0},{3,1},{4,6},{5,7},{6,4},{7,5},{8,10},{9,11},{10,... | collective-permute-start | bytes 49160 | tf_op jit(solution)/shard_map/ppermute | solution.py:552
  140.5 1.6 %copy-start = (f32[4096,128]{1,0:T(8,128)S(1)}, f32[4096,128]{1,0:T(8,128)}, u32[]{:S(2)}) copy-start(f32[4096,128]{1,0:T(8,128)} %table.7) | copy-start | bytes 6291460
  142.1 1.6 %copy-start.1 = (f32[4096,128]{1,0:T(8,128)S(1)}, f32[4096,128]{1,0:T(8,128)}, u32[]{:S(2)}) copy-start(f32[4096,128]{1,0:T(8,128)} %get-tuple-element.46.gradient) | copy-start | bytes 6291460
  143.7 0.7 copy-start.2
  143.7 0.7 copy-start.3

commit v6 on v5

--- a/solution.py
+++ b/solution.py
@@ -354,12 +354,9 @@
     )(settings, weighted, *pieces)
 
 
-def begin(tables, start=None):
-    for n, table in enumerate(tables):
-        if n > 0 or start is None:
-            table[...] = jnp.zeros((SLOTS, WIDTH), F32)
-        else:
-            table[...] = start[...]
+def begin(tables):
+    for table in tables:
+        table[...] = jnp.zeros((SLOTS, WIDTH), F32)
 
 
 def finish(tables):
@@ -369,13 +366,16 @@
     tables[0][...] = total
 
 
-def scatter_near_body(col, src, g0, g1, g3, out, b0, b1, b3, r0, r1, r3, sems, *tables):
+def scatter_near_body(settings_in, src_in, g0, g1, g3, out, settings, src, b0, b1, b3, r0, r1, r3, sems, *tables):
     tables = (out,) + tables
     copies = Copies(sems)
+    copies.start(settings_in, settings)
+    copies.start(src_in, src)
     for source, target in ((g0, b0), (g1, b1), (g3, b3)):
         copies.start(source.at[pl.ds(0, EDGES)], target)
     begin(tables)
     copies.wait()
+    col = settings[0, BUCKETS_END]
     for source, target in ((b0, r0), (b1, r1), (b3, r3)):
         target[...] = source[...].astype(F32)
 
@@ -383,38 +383,45 @@
     def _(b):
         for i in range(PART):
             for s, rows in ((0, r0), (1, r1), (3, r3)):
-                base = b * BUCKET + ((col[0] + s) & (COLS - 1)) * PART
+                base = b * BUCKET + ((col + s) & (COLS - 1)) * PART
                 into = tables[(i * 3 + s) % CHAINS]
                 into[pl.ds(src[base + i], 1), :] += rows[pl.ds(b * PART + i, 1), :]
 
     finish(tables)
 
 
-def scatter_near(col, src, g0, g1, g3):
+def scatter_near(settings, src, g0, g1, g3):
     return call(
         scatter_near_body,
         "scatter_near",
         [(shape(SLOTS, F32), VMEM)],
-        [SMEM] * 2 + [HBM] * 3,
-        [pltpu.VMEM((EDGES, WIDTH), BF16)] * 3
+        [HBM] * 5,
+        [pltpu.SMEM(settings.shape, I32), pltpu.SMEM(src.shape, I32)]
+        + [pltpu.VMEM((EDGES, WIDTH), BF16)] * 3
         + [pltpu.VMEM((EDGES, WIDTH), F32)] * 3
-        + [pltpu.SemaphoreType.DMA((3,))]
+        + [pltpu.SemaphoreType.DMA((5,))]
         + [TABLE] * (CHAINS - 1),
         WHOLE,
         flops=10_000_000_000,
         moved=20_000_000,
-    )(col, src, g0, g1, g3)[0]
-
-
-def scatter_far_body(col, src, neg, start, g0, g1, g3, wr, wl, out, b0, b1, b3, br, bl, rr, rl, corrupt, sems, *tables):
+    )(settings, src, g0, g1, g3)[0]
+
+
+def scatter_far_body(
+    settings_in, src_in, neg_in, start, g0, g1, g3, wr, wl, out, settings, src, neg, b0, b1, b3, br, bl, rr, rl, corrupt, sems, *tables
+):
     tables = (out,) + tables
     copies = Copies(sems)
+    for source, target in ((settings_in, settings), (src_in, src), (neg_in, neg)):
+        copies.start(source, target)
     copies.start(wr, br)
     copies.start(wl, bl)
     for source, target in ((g0, b0), (g1, b1), (g3, b3)):
         copies.start(source.at[pl.ds(EDGES, NEG_PAD)], target)
-    begin(tables, start)
-    copies.wait()
+    copies.start(start, out)
+    begin(tables[1:])
+    copies.wait()
+    col = settings[0, BUCKETS_END]
     rr[...] = br[0:HALF, :].astype(F32)
     rl[...] = bl[0:HALF, :].astype(F32)
     near = b0[...].astype(F32) + b1[...].astype(F32) + b3[...].astype(F32)
@@ -425,7 +432,7 @@
     def _(b):
         for i in range(PART):
             for n, rows in enumerate((rr, rl)):
-                base = (b + n * OWNERS // 2) * BUCKET + ((col[0] + 2) & (COLS - 1)) * PART
+                base = (b + n * OWNERS // 2) * BUCKET + ((col + 2) & (COLS - 1)) * PART
                 into = tables[(i * 2 + n) % CHAINS]
                 into[pl.ds(src[base + i], 1), :] += rows[pl.ds(b * PART + i, 1), :]
 
@@ -438,20 +445,21 @@
     finish(tables)
 
 
-def scatter_far(col, src, neg, start, g0, g1, g3, wr, wl):
+def scatter_far(settings, src, neg, start, g0, g1, g3, wr, wl):
     return call(
         scatter_far_body,
         "scatter_far",
         [(shape(SLOTS, F32), VMEM)],
-        [SMEM] * 3 + [VMEM] + [HBM] * 5,
-        [pltpu.VMEM((NEG_PAD, WIDTH), BF16)] * 5
+        [HBM] * 9,
+        [pltpu.SMEM(settings.shape, I32), pltpu.SMEM(src.shape, I32), pltpu.SMEM(neg.shape, I32)]
+        + [pltpu.VMEM((NEG_PAD, WIDTH), BF16)] * 5
         + [pltpu.VMEM((HALF, WIDTH), F32)] * 2
-        + [pltpu.VMEM((NEG_PAD, WIDTH), F32), pltpu.SemaphoreType.DMA((5,))]
+        + [pltpu.VMEM((NEG_PAD, WIDTH), F32), pltpu.SemaphoreType.DMA((9,))]
         + [TABLE] * (CHAINS - 1),
         WHOLE,
         flops=10_000_000_000,
         moved=20_000_000,
-    )(col, src, neg, start, g0, g1, g3, wr, wl)[0]
+    )(settings, src, neg, start, g0, g1, g3, wr, wl)[0]
 
 
 def scatter_tails_body(
@@ -582,8 +590,8 @@
     from_left, from_right = shifted(right, 1), shifted(left, -1)
     on_r, on_l = pass_on(from_right, from_left)
     far_a, far_b = shifted(on_r, 1), shifted(on_l, -1)
-    gradient = scatter_near(place, src_rows, own, from_right, from_left)
-    gradient = scatter_far(place, src_rows, neg_rows, gradient, own, from_right, from_left, far_a, far_b)
+    gradient = scatter_near(settings, src_rows, own, from_right, from_left)
+    gradient = scatter_far(settings, src_rows, neg_rows, gradient, own, from_right, from_left, far_a, far_b)
     gradient, squares = scatter_tails(
         wanted[:, :BUCKET].reshape(-1), gradient, factors, pulled
     )

time: 148 us -> 147 us (level)
  Pallas kernels: 54.8 us -> 52.7 us
    pallas_call x2, Pallas kernels: 14.7 us -> 12.6 us  [the longest x1 6.38 us: scatter_near(): call(scatter_near_body, 'scatter_near', [(shape(SLOTS, F32), VMEM)], [HBM...]
  transfers between devices with their start and end apart: 16 -> 16, of which waited for: 9 -> 10; matrix products, arithmetic and copies ran while one was open for 1% -> 1% of each run, Pallas kernels for 27% -> 25%
where the time goes in v6:
time: 147 us; the launch traced here: 146 us
  Pallas kernels  52.7 us (36%)
  starting transfers between devices  52.1 us (35%)
  waiting for transfers between devices  33.1 us (23%)
  local copies, waits for them, and re-layouts  4.81 us (3%)
  other arithmetic  2.28 us (2%)
    ppermute x13, waiting for transfers between devices, shifted(): return lax.ppermute(x, 'col', [(i, (i + s) % COLS) for i in range(COLS)])  27.4 us
    all_to_all x2, starting transfers between devices, sent(): lax.all_to_all(x.reshape(OWNERS * COLS, PART, WIDTH), axes, split_axis=0,...  22.2 us
    ppermute x13, starting transfers between devices, shifted(): return lax.ppermute(x, 'col', [(i, (i + s) % COLS) for i in range(COLS)])  18 us
    all_to_all x1, starting transfers between devices, shards(): lax.all_to_all(words, 'dom', split_axis=0, concat_axis=0, tiled=True)  11.9 us
    pallas_call x1, Pallas kernels, gather_tails(): call(gather_tails_body, 'gather_tails', [(shape(SLOTS, BF16), HBM), (shap...  9.19 us
    pallas_call x1, Pallas kernels, edge_scores(): call(edge_scores_body, 'edge_scores', [(jax.ShapeDtypeStruct(whole, BF16)...  7.21 us
    pallas_call x1, Pallas kernels, scatter_tails(): call(scatter_tails_body, 'scatter_tails', [(shape(SLOTS, F32), VMEM), (sh...  7.13 us
    pallas_call x1, Pallas kernels, scatter_near(): call(scatter_near_body, 'scatter_near', [(shape(SLOTS, F32), VMEM)], [HBM...  6.38 us
  transfers between devices with their start and end apart: 16, of which 10 were waited for; matrix products, arithmetic and copies ran while one was open for 1% of the time, Pallas kernels for 25%

profile of v6, /device:TPU:8, one launch (start us, length us, event | category | flops | bytes accessed | tf_op | source)
XLA Modules:
  0.0 145.8 jit_solution(2756688440840780486)
XLA Ops:
  0.6 1.4 request.1
  2.1 11.9 %all-to-all-start = ((s32[64,1,128]{2,1,0:T(1,128)}), s32[64,1,128]{2,1,0:T(1,128)S(1)}, u32[]{:S(2)}, u32[]{:S(2)}) async-start(s32[64,1,128]{2,1,0:T(1,128)} %bitcast.20), calls=%async_computation | async-start | bytes 65536 | tf_op jit(solution)/shard_map/all_to_all | solution.py:576
  14.0 4.7 %gather_far.1 = (bf16[1024,128]{1,0:T(8,128)(2,1)}, bf16[1024,128]{1,0:T(8,128)(2,1)}, bf16[1024,128]{1,0:T(8,128)(2,1)}) custom-call(s32[1]{0:T(128)} %bitcast.8.place, s32[4096]{0:T(1024)} %src_in.3, s32[1000]{0:T(1024)} %neg_in.1, f32[4096,128]{1,0:T(8,128)} %table.7), custom_call_target="tpu_custom_call" | custom-call | bytes 10000000 | tf_op jit(solution)/shard_map/gather_far/pallas_call | solution.py:98
  18.7 1.7 %collective-permute-start = (bf16[1024,128]{1,0:T(8,128)(2,1)}, bf16[1024,128]{1,0:T(8,128)(2,1)}, u32[]{:S(2)}, u32[]{:S(2)}) collective-permute-start(bf16[1024,128]{1,0:T(8,128)(2,1)} %get-tuple-element.29), channel_id=1, source_target_pairs={{0,1},{1,2},{2,3},{3,0},{4,5},{5,6},{6,7},{7,4},{8,9},{9,10},{10,1... | collective-permute-start | bytes 786440 | tf_op jit(solution)/shard_map/ppermute | solution.py:560
  20.4 0.4 collective-permute-start.1
  20.8 2.6 %all-to-all-done = s32[64,1,128]{2,1,0:T(1,128)S(1)} async-done(((s32[64,1,128]{2,1,0:T(1,128)}), s32[64,1,128]{2,1,0:T(1,128)S(1)}, u32[]{:S(2)}, u32[]{:S(2)}) %all-to-all-start) | async-done | bytes 32800 | tf_op jit(solution)/shard_map/all_to_all | solution.py:576
  23.4 9.2 %gather_tails.1 = (bf16[4096,128]{1,0:T(8,128)(2,1)}, f32[4096,128]{1,0:T(8,128)}) custom-call(s32[8192]{0:T(1024)S(1)} %bitcast.16, f32[4096,128]{1,0:T(8,128)} %table.7, f32[1345,128]{1,0:T(8,128)} %relations_in.1), custom_call_target="tpu_custom_call" | custom-call | flops 10000000000 | bytes 20000000 | tf_op jit(solution)/shard_map/gather_tails/pallas_call | solution.py:202
  32.6 11.4 %all-to-all-start.1 = ((bf16[256,16,128]{2,1,0:T(8,128)(2,1)}), bf16[256,16,128]{2,1,0:T(8,128)(2,1)}, u32[]{:S(2)}, u32[]{:S(2)}) async-start(bf16[256,16,128]{2,1,0:T(8,128)(2,1)} %bitcast.19), calls=%async_computation.1 | async-start | bytes 2097152 | tf_op jit(solution)/shard_map/all_to_all | solution.py:571
  44.0 0.0 collective-permute-done.1.vl
  44.0 0.0 copy-start.4
  44.1 1.5 %collective-permute-start.2 = (bf16[1024,128]{1,0:T(8,128)(2,1)}, bf16[1024,128]{1,0:T(8,128)(2,1)}, u32[]{:S(2)}, u32[]{:S(2)}) collective-permute-start(bf16[1024,128]{1,0:T(8,128)(2,1)} %collective-permute-done.vr), channel_id=1, source_target_pairs={{0,1},{1,2},{2,3},{3,0},{4,5},{5,6},{6,7},{7,4},{8,9},{9,10},{10,1... | collective-permute-start | bytes 786440 | tf_op jit(solution)/shard_map/ppermute | solution.py:560
  45.6 0.8 collective-permute-start.3
  46.4 4.7 %gather_near.1 = (bf16[1536,128]{1,0:T(8,128)(2,1)}, bf16[1536,128]{1,0:T(8,128)(2,1)}) custom-call(s32[1]{0:T(128)} %bitcast.8.place, s32[4096]{0:T(1024)} %src_in.3, f32[4096,128]{1,0:T(8,128)} %table.7, bf16[1024,128]{1,0:T(8,128)(2,1)} %get-tuple-element.34.corrupt.n0), custom_call_target="tpu_custom_call" | custom-call | flops 16999999488 | bytes 20000000 | tf_op jit(solution)/shard_map/gather_near/pallas_call | solution.py:127
  51.1 1.3 collective-permute-start.4
  52.4 2.1 %collective-permute-start.5 = (bf16[1536,128]{1,0:T(8,128)(2,1)}, bf16[1536,128]{1,0:T(8,128)(2,1)}, u32[]{:S(2)}, u32[]{:S(2)}) collective-permute-start(bf16[1536,128]{1,0:T(8,128)(2,1)} %get-tuple-element.36), channel_id=1, source_target_pairs={{0,3},{1,0},{2,1},{3,2},{4,7},{5,4},{6,5},{7,6},{8,11},{9,8},{10,9... | collective-permute-start | bytes 1179656 | tf_op jit(solution)/shard_map/ppermute | solution.py:560
  54.4 0.6 concatenate.3.settings_in
  55.0 3.2 %collective-permute-done.2.wr = bf16[1024,128]{1,0:T(8,128)(2,1)} collective-permute-done((bf16[1024,128]{1,0:T(8,128)(2,1)}, bf16[1024,128]{1,0:T(8,128)(2,1)}, u32[]{:S(2)}, u32[]{:S(2)}) %collective-permute-start.2) | collective-permute-done | bytes 262176 | tf_op jit(solution)/shard_map/ppermute | solution.py:560
  58.1 1.2 collective-permute-done.3.wl
  59.4 3.6 %gather_own.1.h0 = bf16[1024,128]{1,0:T(8,128)(2,1)} custom-call(s32[1]{0:T(128)} %bitcast.8.place, s32[4096]{0:T(1024)} %src_in.3, f32[4096,128]{1,0:T(8,128)} %table.7), custom_call_target="tpu_custom_call" | custom-call | flops 3000000000 | bytes 3000000 | tf_op jit(solution)/shard_map/gather_own/pallas_call | solution.py:227
  63.0 7.9 %collective-permute-done.4.dr = bf16[1536,128]{1,0:T(8,128)(2,1)} collective-permute-done((bf16[1536,128]{1,0:T(8,128)(2,1)}, bf16[1536,128]{1,0:T(8,128)(2,1)}, u32[]{:S(2)}, u32[]{:S(2)}) %collective-permute-start.4) | collective-permute-done | bytes 393248 | tf_op jit(solution)/shard_map/ppermute | solution.py:560
  70.9 1.0 collective-permute-done.5.dl
  71.9 3.1 %all-to-all-done.1 = bf16[256,16,128]{2,1,0:T(8,128)(2,1)} async-done(((bf16[256,16,128]{2,1,0:T(8,128)(2,1)}), bf16[256,16,128]{2,1,0:T(8,128)(2,1)}, u32[]{:S(2)}, u32[]{:S(2)}) %all-to-all-start.1) | async-done | bytes 1048608 | tf_op jit(solution)/shard_map/all_to_all | solution.py:571
  75.0 7.2 %edge_scores.1 = (bf16[64,4,16,128]{3,2,1,0:T(8,128)(2,1)}, bf16[2048,128]{1,0:T(8,128)(2,1)}, bf16[3072,128]{1,0:T(8,128)(2,1)}, bf16[3072,128]{1,0:T(8,128)(2,1)}) custom-call(s32[1,128]{1,0:T(1,128)} %concatenate.3.settings_in, bf16[64,4,16,128]{3,2,1,0:T(8,128)(2,1)} %bitcast.7.weighted_in, bf16[1024,128]{1,0:T(8,128)(2,1)} %gather_own.1.h0, ...), custom_call_target="tpu_custom_call" | custom-call | flops 3200000000 | bytes 8000000 | tf_op jit(solution)/shard_map/edge_scores/pallas_call | solution.py:336
  82.2 1.6 %collective-permute-start.6 = (bf16[3072,128]{1,0:T(8,128)(2,1)}, bf16[3072,128]{1,0:T(8,128)(2,1)}, u32[]{:S(2)}, u32[]{:S(2)}) collective-permute-start(bf16[3072,128]{1,0:T(8,128)(2,1)} %get-tuple-element.40), channel_id=1, source_target_pairs={{0,3},{1,0},{2,1},{3,2},{4,7},{5,4},{6,5},{7,6},{8,11},{9,8},{10,9... | collective-permute-start | bytes 2359304 | tf_op jit(solution)/shard_map/ppermute | solution.py:560
  83.8 0.7 collective-permute-start.7
  84.5 10.8 %all-to-all-start.2 = ((bf16[256,16,128]{2,1,0:T(8,128)(2,1)}), bf16[256,16,128]{2,1,0:T(8,128)(2,1)}, u32[]{:S(2)}, u32[]{:S(2)}) async-start(bf16[256,16,128]{2,1,0:T(8,128)(2,1)} %bitcast.18), calls=%async_computation.2 | async-start | bytes 2097152 | tf_op jit(solution)/shard_map/all_to_all | solution.py:571
  95.2 0.7 reshape.40.wanted_in
  95.9 9.8 %collective-permute-done.6.g1 = bf16[3072,128]{1,0:T(8,128)(2,1)} collective-permute-done((bf16[3072,128]{1,0:T(8,128)(2,1)}, bf16[3072,128]{1,0:T(8,128)(2,1)}, u32[]{:S(2)}, u32[]{:S(2)}) %collective-permute-start.6) | collective-permute-done | bytes 786464 | tf_op jit(solution)/shard_map/ppermute | solution.py:560
  105.8 2.7 %collective-permute-done.7.g3 = bf16[3072,128]{1,0:T(8,128)(2,1)} collective-permute-done((bf16[3072,128]{1,0:T(8,128)(2,1)}, bf16[3072,128]{1,0:T(8,128)(2,1)}, u32[]{:S(2)}, u32[]{:S(2)}) %collective-permute-start.7) | collective-permute-done | bytes 786464 | tf_op jit(solution)/shard_map/ppermute | solution.py:560
  108.5 1.9 %pass_on.1 = (bf16[1024,128]{1,0:T(8,128)(2,1)}, bf16[1024,128]{1,0:T(8,128)(2,1)}) custom-call(bf16[3072,128]{1,0:T(8,128)(2,1)} %collective-permute-done.6.g1, bf16[3072,128]{1,0:T(8,128)(2,1)} %collective-permute-done.7.g3), custom_call_target="tpu_custom_call" | custom-call | bytes 1000000 | tf_op jit(solution)/shard_map/pass_on/pallas_call | solution.py:549
  110.4 0.1 collective-permute-start.8
  110.5 2.0 %collective-permute-start.9 = (bf16[1024,128]{1,0:T(8,128)(2,1)}, bf16[1024,128]{1,0:T(8,128)(2,1)}, u32[]{:S(2)}, u32[]{:S(2)}) collective-permute-start(bf16[1024,128]{1,0:T(8,128)(2,1)} %get-tuple-element.43), channel_id=1, source_target_pairs={{0,3},{1,0},{2,1},{3,2},{4,7},{5,4},{6,5},{7,6},{8,11},{9,8},{10,9... | collective-permute-start | bytes 786440 | tf_op jit(solution)/shard_map/ppermute | solution.py:560
  112.5 6.4 %scatter_near.1.start = f32[4096,128]{1,0:T(8,128)} custom-call(s32[1,128]{1,0:T(1,128)} %concatenate.3.settings_in, s32[4096]{0:T(1024)} %src_in.3, bf16[2048,128]{1,0:T(8,128)(2,1)} %get-tuple-element.39.g0, bf16[3072,128]{1,0:T(8,128)(2,1)} %collective-permute-done.6.g1, bf16[3072,128]{1,0:T(8,128)(2,1)} %collective-permute-done.7.g3), custom_call_target="tpu_custom_call" | custom-call | flops 10000000000 | bytes 20000000 | tf_op jit(solution)/shard_map/scatter_near/pallas_call | solution.py:394
  118.9 1.0 collective-permute-done.8.wr
  119.8 0.6 collective-permute-done.9.wl
  120.4 6.2 %scatter_far.1.start = f32[4096,128]{1,0:T(8,128)} custom-call(s32[1,128]{1,0:T(1,128)} %concatenate.3.settings_in, s32[4096]{0:T(1024)} %src_in.3, s32[1000]{0:T(1024)} %neg_in.1, f32[4096,128]{1,0:T(8,128)} %scatter_near.1.start, bf16[2048,128]{1,0:T(8,128)(2,1)} %get-tuple-element.39.g0, bf16[3072,128]{1,0:T(8,128)(2,1)} %collective-permute-done.6.g1, ...), custom_call_target="tpu_custom_call" | custom-call | flops 10000000000 | bytes 20000000 | tf_op jit(solution)/shard_map/scatter_far/pallas_call | solution.py:449
  126.7 0.0 all-to-all-done.2
  126.7 7.1 %scatter_tails.1 = (f32[4096,128]{1,0:T(8,128)}, f32[32,128]{1,0:T(8,128)}) custom-call(s32[4096]{0:T(1024)} %reshape.40.wanted_in, f32[4096,128]{1,0:T(8,128)} %scatter_far.1.start, f32[4096,128]{1,0:T(8,128)} %get-tuple-element.44.factors, bf16[4096,128]{1,0:T(8,128)(2,1)} %bitcast.10.pulled), custom_call_target="tpu_custom_call" | custom-call | bytes 30000000 | tf_op jit(solution)/shard_map/scatter_tails/pallas_call | solution.py:508
  133.8 1.7 %collective-permute-start.12 = (f32[32,128]{1,0:T(8,128)}, f32[32,128]{1,0:T(8,128)S(1)}, u32[]{:S(2)}, u32[]{:S(2)}) collective-permute-start(f32[32,128]{1,0:T(8,128)} %get-tuple-element.49), channel_id=1, source_target_pairs={{0,3},{1,0},{2,1},{3,2},{4,7},{5,4},{6,5},{7,6},{8,11},{9,8},{10,9... | collective-permute-start | bytes 49160 | tf_op jit(solution)/shard_map/ppermute | solution.py:560
  135.5 0.4 collective-permute-start.11
  135.9 3.7 %collective-permute-start.10 = (f32[32,128]{1,0:T(8,128)}, f32[32,128]{1,0:T(8,128)S(1)}, u32[]{:S(2)}, u32[]{:S(2)}) collective-permute-start(f32[32,128]{1,0:T(8,128)} %get-tuple-element.49), channel_id=1, source_target_pairs={{0,2},{1,3},{2,0},{3,1},{4,6},{5,7},{6,4},{7,5},{8,10},{9,11},{10,... | collective-permute-start | bytes 49160 | tf_op jit(solution)/shard_map/ppermute | solution.py:560
  139.6 1.6 %copy-done = f32[4096,128]{1,0:T(8,128)S(1)} copy-done((f32[4096,128]{1,0:T(8,128)S(1)}, f32[4096,128]{1,0:T(8,128)}, u32[]{:S(2)}) %copy-start) | copy-done | bytes 2097176
  141.2 1.6 %copy-done.1 = f32[4096,128]{1,0:T(8,128)S(1)} copy-done((f32[4096,128]{1,0:T(8,128)S(1)}, f32[4096,128]{1,0:T(8,128)}, u32[]{:S(2)}) %copy-start.1) | copy-done | bytes 2097176
  142.8 0.3 stage.1
  143.2 0.4 copy-done.2
  143.5 0.0 copy-done.3
  143.5 0.6 fusion
  144.2 1.7 %divide_subtract_fusion = f32[4096,128]{1,0:T(8,128)} fusion(f32[4096,128]{1,0:T(8,128)S(1)} %get-tuple-element.47, f32[4096,128]{1,0:T(8,128)S(1)} %get-tuple-element.48, f32[4096]{0:T(1024)S(1)} %get-tuple-element.50), kind=kLoop, calls=%fused_computation | loop fusion | flops 1048576 | bytes 6307840 | tf_op jit(solution)/shard_map/sub | solution.py:602
  (9 shorter events, 0.0 us)
Async XLA Ops:
  2.1 21.4 %all-to-all-start = ((s32[64,1,128]{2,1,0:T(1,128)}), s32[64,1,128]{2,1,0:T(1,128)S(1)}, u32[]{:S(2)}, u32[]{:S(2)}) async-start(s32[64,1,128]{2,1,0:T(1,128)} %bitcast.20), calls=%async_computation | async-start | bytes 65536 | tf_op jit(solution)/shard_map/all_to_all | solution.py:576
  18.7 25.3 %collective-permute-start = (bf16[1024,128]{1,0:T(8,128)(2,1)}, bf16[1024,128]{1,0:T(8,128)(2,1)}, u32[]{:S(2)}, u32[]{:S(2)}) collective-permute-start(bf16[1024,128]{1,0:T(8,128)(2,1)} %get-tuple-element.29), channel_id=1, source_target_pairs={{0,1},{1,2},{2,3},{3,0},{4,5},{5,6},{6,7},{7,4},{8,9},{9,10},{10,1... | collective-permute-start | bytes 786440 | tf_op jit(solution)/shard_map/ppermute | solution.py:560
  20.4 23.7 %collective-permute-start.1 = (bf16[1024,128]{1,0:T(8,128)(2,1)}, bf16[1024,128]{1,0:T(8,128)(2,1)}, u32[]{:S(2)}, u32[]{:S(2)}) collective-permute-start(bf16[1024,128]{1,0:T(8,128)(2,1)} %get-tuple-element.30), channel_id=1, source_target_pairs={{0,3},{1,0},{2,1},{3,2},{4,7},{5,4},{6,5},{7,6},{8,11},{9,8},{10,9... | collective-permute-start | bytes 786440 | tf_op jit(solution)/shard_map/ppermute | solution.py:560
  32.6 42.3 %all-to-all-start.1 = ((bf16[256,16,128]{2,1,0:T(8,128)(2,1)}), bf16[256,16,128]{2,1,0:T(8,128)(2,1)}, u32[]{:S(2)}, u32[]{:S(2)}) async-start(bf16[256,16,128]{2,1,0:T(8,128)(2,1)} %bitcast.19), calls=%async_computation.1 | async-start | bytes 2097152 | tf_op jit(solution)/shard_map/all_to_all | solution.py:571
  44.0 10.4 %copy-start.4 = (s32[1,64]{1,0:T(1,128)S(1)}, s32[1,64]{1,0:T(1,128)}, u32[]{:S(2)}) copy-start(s32[1,64]{1,0:T(1,128)} %param.14) | copy-start | bytes 772
  44.1 14.1 %collective-permute-start.2 = (bf16[1024,128]{1,0:T(8,128)(2,1)}, bf16[1024,128]{1,0:T(8,128)(2,1)}, u32[]{:S(2)}, u32[]{:S(2)}) collective-permute-start(bf16[1024,128]{1,0:T(8,128)(2,1)} %collective-permute-done.vr), channel_id=1, source_target_pairs={{0,1},{1,2},{2,3},{3,0},{4,5},{5,6},{6,7},{7,4},{8,9},{9,10},{10,1... | collective-permute-start | bytes 786440 | tf_op jit(solution)/shard_map/ppermute | solution.py:560
  45.6 13.8 %collective-permute-start.3 = (bf16[1024,128]{1,0:T(8,128)(2,1)}, bf16[1024,128]{1,0:T(8,128)(2,1)}, u32[]{:S(2)}, u32[]{:S(2)}) collective-permute-start(bf16[1024,128]{1,0:T(8,128)(2,1)} %collective-permute-done.1.vl), channel_id=1, source_target_pairs={{0,3},{1,0},{2,1},{3,2},{4,7},{5,4},{6,5},{7,6},{8,11},{9,8},{10,9... | collective-permute-start | bytes 786440 | tf_op jit(solution)/shard_map/ppermute | solution.py:560
  51.1 19.8 %collective-permute-start.4 = (bf16[1536,128]{1,0:T(8,128)(2,1)}, bf16[1536,128]{1,0:T(8,128)(2,1)}, u32[]{:S(2)}, u32[]{:S(2)}) collective-permute-start(bf16[1536,128]{1,0:T(8,128)(2,1)} %get-tuple-element.35), channel_id=1, source_target_pairs={{0,1},{1,2},{2,3},{3,0},{4,5},{5,6},{6,7},{7,4},{8,9},{9,10},{10,1... | collective-permute-start | bytes 1179656 | tf_op jit(solution)/shard_map/ppermute | solution.py:560
  52.4 19.6 %collective-permute-start.5 = (bf16[1536,128]{1,0:T(8,128)(2,1)}, bf16[1536,128]{1,0:T(8,128)(2,1)}, u32[]{:S(2)}, u32[]{:S(2)}) collective-permute-start(bf16[1536,128]{1,0:T(8,128)(2,1)} %get-tuple-element.36), channel_id=1, source_target_pairs={{0,3},{1,0},{2,1},{3,2},{4,7},{5,4},{6,5},{7,6},{8,11},{9,8},{10,9... | collective-permute-start | bytes 1179656 | tf_op jit(solution)/shard_map/ppermute | solution.py:560
  82.2 23.6 %collective-permute-start.6 = (bf16[3072,128]{1,0:T(8,128)(2,1)}, bf16[3072,128]{1,0:T(8,128)(2,1)}, u32[]{:S(2)}, u32[]{:S(2)}) collective-permute-start(bf16[3072,128]{1,0:T(8,128)(2,1)} %get-tuple-element.40), channel_id=1, source_target_pairs={{0,3},{1,0},{2,1},{3,2},{4,7},{5,4},{6,5},{7,6},{8,11},{9,8},{10,9... | collective-permute-start | bytes 2359304 | tf_op jit(solution)/shard_map/ppermute | solution.py:560
  83.8 24.7 %collective-permute-start.7 = (bf16[3072,128]{1,0:T(8,128)(2,1)}, bf16[3072,128]{1,0:T(8,128)(2,1)}, u32[]{:S(2)}, u32[]{:S(2)}) collective-permute-start(bf16[3072,128]{1,0:T(8,128)(2,1)} %get-tuple-element.41), channel_id=1, source_target_pairs={{0,1},{1,2},{2,3},{3,0},{4,5},{5,6},{6,7},{7,4},{8,9},{9,10},{10,1... | collective-permute-start | bytes 2359304 | tf_op jit(solution)/shard_map/ppermute | solution.py:560
  84.5 42.2 %all-to-all-start.2 = ((bf16[256,16,128]{2,1,0:T(8,128)(2,1)}), bf16[256,16,128]{2,1,0:T(8,128)(2,1)}, u32[]{:S(2)}, u32[]{:S(2)}) async-start(bf16[256,16,128]{2,1,0:T(8,128)(2,1)} %bitcast.18), calls=%async_computation.2 | async-start | bytes 2097152 | tf_op jit(solution)/shard_map/all_to_all | solution.py:571
  110.4 9.5 %collective-permute-start.8 = (bf16[1024,128]{1,0:T(8,128)(2,1)}, bf16[1024,128]{1,0:T(8,128)(2,1)}, u32[]{:S(2)}, u32[]{:S(2)}) collective-permute-start(bf16[1024,128]{1,0:T(8,128)(2,1)} %get-tuple-element.42), channel_id=1, source_target_pairs={{0,1},{1,2},{2,3},{3,0},{4,5},{5,6},{6,7},{7,4},{8,9},{9,10},{10,1... | collective-permute-start | bytes 786440 | tf_op jit(solution)/shard_map/ppermute | solution.py:560
  110.5 10.0 %collective-permute-start.9 = (bf16[1024,128]{1,0:T(8,128)(2,1)}, bf16[1024,128]{1,0:T(8,128)(2,1)}, u32[]{:S(2)}, u32[]{:S(2)}) collective-permute-start(bf16[1024,128]{1,0:T(8,128)(2,1)} %get-tuple-element.43), channel_id=1, source_target_pairs={{0,3},{1,0},{2,1},{3,2},{4,7},{5,4},{6,5},{7,6},{8,11},{9,8},{10,9... | collective-permute-start | bytes 786440 | tf_op jit(solution)/shard_map/ppermute | solution.py:560
  133.8 9.3 %collective-permute-start.12 = (f32[32,128]{1,0:T(8,128)}, f32[32,128]{1,0:T(8,128)S(1)}, u32[]{:S(2)}, u32[]{:S(2)}) collective-permute-start(f32[32,128]{1,0:T(8,128)} %get-tuple-element.49), channel_id=1, source_target_pairs={{0,3},{1,0},{2,1},{3,2},{4,7},{5,4},{6,5},{7,6},{8,11},{9,8},{10,9... | collective-permute-start | bytes 49160 | tf_op jit(solution)/shard_map/ppermute | solution.py:560
  135.5 7.6 %collective-permute-start.11 = (f32[32,128]{1,0:T(8,128)}, f32[32,128]{1,0:T(8,128)S(1)}, u32[]{:S(2)}, u32[]{:S(2)}) collective-permute-start(f32[32,128]{1,0:T(8,128)} %get-tuple-element.49), channel_id=1, source_target_pairs={{0,1},{1,2},{2,3},{3,0},{4,5},{5,6},{6,7},{7,4},{8,9},{9,10},{10,1... | collective-permute-start | bytes 49160 | tf_op jit(solution)/shard_map/ppermute | solution.py:560
  135.9 7.2 %collective-permute-start.10 = (f32[32,128]{1,0:T(8,128)}, f32[32,128]{1,0:T(8,128)S(1)}, u32[]{:S(2)}, u32[]{:S(2)}) collective-permute-start(f32[32,128]{1,0:T(8,128)} %get-tuple-element.49), channel_id=1, source_target_pairs={{0,2},{1,3},{2,0},{3,1},{4,6},{5,7},{6,4},{7,5},{8,10},{9,11},{10,... | collective-permute-start | bytes 49160 | tf_op jit(solution)/shard_map/ppermute | solution.py:560
  139.6 1.6 %copy-start = (f32[4096,128]{1,0:T(8,128)S(1)}, f32[4096,128]{1,0:T(8,128)}, u32[]{:S(2)}) copy-start(f32[4096,128]{1,0:T(8,128)} %table.7) | copy-start | bytes 6291460
  141.2 1.6 %copy-start.1 = (f32[4096,128]{1,0:T(8,128)S(1)}, f32[4096,128]{1,0:T(8,128)}, u32[]{:S(2)}) copy-start(f32[4096,128]{1,0:T(8,128)} %get-tuple-element.46.gradient) | copy-start | bytes 6291460
  142.8 0.7 copy-start.2
  142.8 0.7 copy-start.3

commit v7 on v6

--- a/solution.py
+++ b/solution.py
@@ -75,7 +75,7 @@
                 rows[pl.ds(n * EDGES + b * PART + i, 1), :] = table[pl.ds(src[base + i], 1), :]
 
 
-def gather_far_body(place, src, neg, table, via_r, via_l, corrupt_out, rows, corrupt, rounded, vr, vl, sems):
+def gather_far_body(place, src, neg, table, via_r, via_l, corrupt_out, first_out, second_out, rows, corrupt, rounded, vr, vl, sems):
     copies = Copies(sems)
 
     @pl.loop(0, NEG // 40)
@@ -86,6 +86,8 @@
     corrupt[NEG:NEG_PAD, :] = jnp.zeros((NEG_PAD - NEG, WIDTH), F32)
     rounded[...] = corrupt[...].astype(BF16)
     copies.start(rounded, corrupt_out)
+    copies.start(rounded.at[pl.ds(0, HALF)], first_out)
+    copies.start(rounded.at[pl.ds(HALF, HALF)], second_out)
     head_rows(place, src, table, rows, (2,))
     for held, out, part in ((vr, via_r, slice(0, HALF)), (vl, via_l, slice(HALF, 2 * HALF))):
         held[0:HALF, :] = rows[part, :].astype(BF16)
@@ -98,44 +100,39 @@
     return call(
         gather_far_body,
         "gather_far",
-        [(shape(2 * HALF, BF16), HBM)] * 3,
+        [(shape(2 * HALF, BF16), HBM)] * 3 + [(shape(HALF, BF16), HBM)] * 2,
         [SMEM, SMEM, SMEM, VMEM],
         [pltpu.VMEM((EDGES, WIDTH), F32), pltpu.VMEM((NEG_PAD, WIDTH), F32)]
         + [pltpu.VMEM((2 * HALF, WIDTH), BF16)] * 3
-        + [pltpu.SemaphoreType.DMA((3,))],
+        + [pltpu.SemaphoreType.DMA((5,))],
         WHOLE,
         moved=10_000_000,
     )(place, src, neg, table)
 
 
-def gather_near_body(place, src, table, corrupt, right, left, rows, halves, r, l, in_sems, sems):
-    arrivals, copies = Copies(in_sems), Copies(sems)
-    arrivals.start(corrupt, halves)
+def gather_near_body(place, src, table, right, left, rows, r, l, sems):
+    copies = Copies(sems)
     head_rows(place, src, table, rows, (1, 3))
-    arrivals.wait()
-    r[0:EDGES, :] = rows[0:EDGES, :].astype(BF16)
-    r[EDGES:, :] = halves[HALF:, :]
+    r[...] = rows[0:EDGES, :].astype(BF16)
     copies.start(r, right)
-    l[0:EDGES, :] = rows[EDGES : 2 * EDGES, :].astype(BF16)
-    l[EDGES:, :] = halves[0:HALF, :]
+    l[...] = rows[EDGES : 2 * EDGES, :].astype(BF16)
     copies.start(l, left)
     copies.wait()
 
 
-def gather_near(place, src, table, corrupt):
-    sizes = (EDGES + HALF, EDGES + HALF)
+def gather_near(place, src, table):
     return call(
         gather_near_body,
         "gather_near",
-        [(shape(n, BF16), HBM) for n in sizes],
-        [SMEM, SMEM, VMEM, HBM],
-        [pltpu.VMEM((2 * EDGES, WIDTH), F32), pltpu.VMEM((NEG_PAD, WIDTH), BF16)]
-        + [pltpu.VMEM((n, WIDTH), BF16) for n in sizes]
-        + [pltpu.SemaphoreType.DMA((1,)), pltpu.SemaphoreType.DMA((2,))],
+        [(shape(EDGES, BF16), HBM)] * 2,
+        [SMEM, SMEM, VMEM],
+        [pltpu.VMEM((2 * EDGES, WIDTH), F32)]
+        + [pltpu.VMEM((EDGES, WIDTH), BF16)] * 2
+        + [pltpu.SemaphoreType.DMA((2,))],
         WHOLE,
         flops=17_000_000_000,
         moved=20_000_000,
-    )(place, src, table, corrupt)
+    )(place, src, table)
 
 
 LINE = 2 * BUCKET
@@ -241,7 +238,7 @@
 
 
 def edge_scores_body(
-    settings_in, weighted_in, h0, n0, dr, vr, dl, vl, wr, wl, pulled_out, own, right, left, *rest
+    settings_in, weighted_in, h0, n0, dr, nr, vr, dl, nl, vl, wr, wl, pulled_out, own, right, left, *rest
 ):
     settings, weighted, heads, corrupt, grad_scores, pulled, o, r, l, in_sems, sems = rest
     span = [slice(s * WIDTH, (s + 1) * WIDTH) for s in range(COLS)]
@@ -256,10 +253,10 @@
     for_scores = [
         fetch(n0, 0, corrupt, 0, 0, NEG_PAD),
         fetch(vr, HALF, corrupt, 0, 1, HALF),
-        fetch(dr, EDGES, corrupt, HALF, 1, HALF),
+        fetch(nr, 0, corrupt, HALF, 1, HALF),
         fetch(wr, HALF, corrupt, 0, 2, HALF),
         fetch(wl, HALF, corrupt, HALF, 2, HALF),
-        fetch(dl, EDGES, corrupt, 0, 3, HALF),
+        fetch(nl, 0, corrupt, 0, 3, HALF),
         fetch(vl, HALF, corrupt, HALF, 3, HALF),
     ]
     for_weights = [arrivals.start(weighted_in.at[at], weighted.at[at]) for at in blocks]
@@ -337,7 +334,7 @@
         edge_scores_body,
         "edge_scores",
         [(jax.ShapeDtypeStruct(whole, BF16), HBM)] + [(shape(n, BF16), HBM) for n in sizes],
-        [HBM] * 10,
+        [HBM] * 12,
         [
             pltpu.SMEM(settings.shape, I32),
             pltpu.VMEM(whole, BF16),
@@ -574,17 +571,20 @@
 
     words = request(dst_rows, rel_ids)
     wanted = lax.all_to_all(words, "dom", split_axis=0, concat_axis=0, tiled=True)
-    via_r, via_l, negatives = gather_far(place, src_rows, neg_rows, embeddings)
+    via_r, via_l, negatives, first, second = gather_far(place, src_rows, neg_rows, embeddings)
     vr, vl = shifted(via_r, 1), shifted(via_l, -1)
     weighted, factors = gather_tails(wanted.reshape(-1), embeddings, relations)
     weighted = sent(weighted).reshape(OWNERS, COLS, PART, WIDTH)
-    after, factors, vr, vl = lax.optimization_barrier((negatives, factors, vr, vl))
-    right, left = gather_near(place, src_rows, embeddings, after)
+    after, first, second, near_rows, factors, vr, vl = lax.optimization_barrier(
+        (negatives, first, second, src_rows, factors, vr, vl)
+    )
+    nr, nl = shifted(second, 1), shifted(first, -1)
+    wr, wl = shifted(vr, 1), shifted(vl, -1)
+    right, left = gather_near(place, near_rows, embeddings)
     near_r, near_l = shifted(right, 1), shifted(left, -1)
-    wr, wl = shifted(vr, 1), shifted(vl, -1)
-    own_rows, wr, wl = lax.optimization_barrier((src_rows, wr, wl))
+    own_rows, nr, nl, wr, wl = lax.optimization_barrier((src_rows, nr, nl, wr, wl))
     heads = gather_own(place, own_rows, embeddings)
-    pieces = [heads, after, near_r, vr, near_l, vl, wr, wl]
+    pieces = [heads, after, near_r, nr, vr, near_l, nl, vl, wr, wl]
     pulled, own, right, left = edge_scores(settings, weighted, pieces)
     pulled = sent(pulled).reshape(SLOTS, WIDTH)
     from_left, from_right = shifted(right, 1), shifted(left, -1)

time: 147 us -> 147 us (level)
  waiting for transfers between devices: 33.1 us -> 29.9 us
  starting transfers between devices: 52.1 us -> 55.2 us
    ppermute x13 -> x15, waiting for transfers between devices: 27.4 us -> 24.4 us  [shifted(): return lax.ppermute(x, 'col', [(i, (i + s) % COLS) for i in range(COLS)])]
    ppermute x13 -> x15, starting transfers between devices: 18 us -> 21 us  [shifted(): return lax.ppermute(x, 'col', [(i, (i + s) % COLS) for i in range(COLS)])]
    unnamed x10 -> x12, local copies, waits for them, and re-layouts: 3.57 us -> 3.57 us
  transfers between devices with their start and end apart: 16 -> 18, of which waited for: 10 -> 10; matrix products, arithmetic and copies ran while one was open for 1% -> 1% of each run, Pallas kernels for 25% -> 25%
where the time goes in v7:
time: 147 us; the launch traced here: 146 us
  starting transfers between devices  55.2 us (38%)
  Pallas kernels  52.7 us (36%)
  waiting for transfers between devices  29.9 us (20%)
  local copies, waits for them, and re-layouts  4.84 us (3%)
  other arithmetic  2.28 us (2%)
    ppermute x15, waiting for transfers between devices, shifted(): return lax.ppermute(x, 'col', [(i, (i + s) % COLS) for i in range(COLS)])  24.4 us
    all_to_all x2, starting transfers between devices, sent(): lax.all_to_all(x.reshape(OWNERS * COLS, PART, WIDTH), axes, split_axis=0,...  22.3 us
    ppermute x15, starting transfers between devices, shifted(): return lax.ppermute(x, 'col', [(i, (i + s) % COLS) for i in range(COLS)])  21 us
    all_to_all x1, starting transfers between devices, shards(): lax.all_to_all(words, 'dom', split_axis=0, concat_axis=0, tiled=True)  11.9 us
    pallas_call x1, Pallas kernels, gather_tails(): call(gather_tails_body, 'gather_tails', [(shape(SLOTS, BF16), HBM), (shap...  9.19 us
    pallas_call x1, Pallas kernels, edge_scores(): call(edge_scores_body, 'edge_scores', [(jax.ShapeDtypeStruct(whole, BF16)...  7.21 us
    pallas_call x1, Pallas kernels, scatter_tails(): call(scatter_tails_body, 'scatter_tails', [(shape(SLOTS, F32), VMEM), (sh...  7.14 us
    pallas_call x1, Pallas kernels, scatter_near(): call(scatter_near_body, 'scatter_near', [(shape(SLOTS, F32), VMEM)], [HBM...  6.4 us
  transfers between devices with their start and end apart: 18, of which 10 were waited for; matrix products, arithmetic and copies ran while one was open for 1% of the time, Pallas kernels for 25%

profile of v7, /device:TPU:8, one launch (start us, length us, event | category | flops | bytes accessed | tf_op | source)
XLA Modules:
  0.0 145.7 jit_solution(15784727136834060665)
XLA Ops:
  0.6 1.4 request.1
  2.1 11.9 %all-to-all-start = ((s32[64,1,128]{2,1,0:T(1,128)}), s32[64,1,128]{2,1,0:T(1,128)S(1)}, u32[]{:S(2)}, u32[]{:S(2)}) async-start(s32[64,1,128]{2,1,0:T(1,128)} %bitcast.20), calls=%async_computation | async-start | bytes 65536 | tf_op jit(solution)/shard_map/all_to_all | solution.py:573
  14.0 4.7 %gather_far.1 = (bf16[1024,128]{1,0:T(8,128)(2,1)}, bf16[1024,128]{1,0:T(8,128)(2,1)}, bf16[1024,128]{1,0:T(8,128)(2,1)}, bf16[512,128]{1,0:T(8,128)(2,1)}, bf16[512,128]{1,0:T(8,128)(2,1)}) custom-call(s32[1]{0:T(128)} %bitcast.8.place, s32[4096]{0:T(1024)} %src_in.3, s32[1000]{0:T(1024)} %neg_in.1, f32[4096,128]{1,0:T(8,128)} %table.7), custom_call_target="tpu_custom_call" | custom-call | bytes 10000000 | tf_op jit(solution)/shard_map/gather_far/pallas_call | solution.py:100
  18.7 1.7 %collective-permute-start = (bf16[1024,128]{1,0:T(8,128)(2,1)}, bf16[1024,128]{1,0:T(8,128)(2,1)}, u32[]{:S(2)}, u32[]{:S(2)}) collective-permute-start(bf16[1024,128]{1,0:T(8,128)(2,1)} %get-tuple-element.38), channel_id=1, source_target_pairs={{0,1},{1,2},{2,3},{3,0},{4,5},{5,6},{6,7},{7,4},{8,9},{9,10},{10,1... | collective-permute-start | bytes 786440 | tf_op jit(solution)/shard_map/ppermute | solution.py:557
  20.4 0.4 collective-permute-start.1
  20.8 2.6 %all-to-all-done = s32[64,1,128]{2,1,0:T(1,128)S(1)} async-done(((s32[64,1,128]{2,1,0:T(1,128)}), s32[64,1,128]{2,1,0:T(1,128)S(1)}, u32[]{:S(2)}, u32[]{:S(2)}) %all-to-all-start) | async-done | bytes 32800 | tf_op jit(solution)/shard_map/all_to_all | solution.py:573
  23.4 9.2 %gather_tails.1 = (bf16[4096,128]{1,0:T(8,128)(2,1)}, f32[4096,128]{1,0:T(8,128)}) custom-call(s32[8192]{0:T(1024)S(1)} %bitcast.16, f32[4096,128]{1,0:T(8,128)} %table.7, f32[1345,128]{1,0:T(8,128)} %relations_in.1), custom_call_target="tpu_custom_call" | custom-call | flops 10000000000 | bytes 20000000 | tf_op jit(solution)/shard_map/gather_tails/pallas_call | solution.py:199
  32.6 0.0 copy-start.5
  32.6 11.4 %all-to-all-start.1 = ((bf16[256,16,128]{2,1,0:T(8,128)(2,1)}), bf16[256,16,128]{2,1,0:T(8,128)(2,1)}, u32[]{:S(2)}, u32[]{:S(2)}) async-start(bf16[256,16,128]{2,1,0:T(8,128)(2,1)} %bitcast.18), calls=%async_computation.1 | async-start | bytes 2097152 | tf_op jit(solution)/shard_map/all_to_all | solution.py:568
  44.1 0.6 concatenate.3.settings_in
  44.7 1.5 %collective-permute-start.2 = (bf16[512,128]{1,0:T(8,128)(2,1)}, bf16[512,128]{1,0:T(8,128)(2,1)}, u32[]{:S(2)}, u32[]{:S(2)}) collective-permute-start(bf16[512,128]{1,0:T(8,128)(2,1)} %get-tuple-element.40), channel_id=1, source_target_pairs={{0,1},{1,2},{2,3},{3,0},{4,5},{5,6},{6,7},{7,4},{8,9},{9,10},{10,1... | collective-permute-start | bytes 393224 | tf_op jit(solution)/shard_map/ppermute | solution.py:557
  46.1 0.8 collective-permute-start.3
  47.0 1.2 collective-permute-start.4
  48.2 2.0 %collective-permute-start.5 = (bf16[1024,128]{1,0:T(8,128)(2,1)}, bf16[1024,128]{1,0:T(8,128)(2,1)}, u32[]{:S(2)}, u32[]{:S(2)}) collective-permute-start(bf16[1024,128]{1,0:T(8,128)(2,1)} %collective-permute-done.1.vl), channel_id=1, source_target_pairs={{0,3},{1,0},{2,1},{3,2},{4,7},{5,4},{6,5},{7,6},{8,11},{9,8},{10,9... | collective-permute-start | bytes 786440 | tf_op jit(solution)/shard_map/ppermute | solution.py:557
  50.1 4.6 %gather_near.1 = (bf16[1024,128]{1,0:T(8,128)(2,1)}, bf16[1024,128]{1,0:T(8,128)(2,1)}) custom-call(s32[1]{0:T(128)} %bitcast.8.place, s32[4096]{0:T(1024)} %src_in.3, f32[4096,128]{1,0:T(8,128)} %table.7), custom_call_target="tpu_custom_call" | custom-call | flops 16999999488 | bytes 20000000 | tf_op jit(solution)/shard_map/gather_near/pallas_call | solution.py:124
  54.7 0.1 collective-permute-start.6
  54.8 3.4 %collective-permute-start.7 = (bf16[1024,128]{1,0:T(8,128)(2,1)}, bf16[1024,128]{1,0:T(8,128)(2,1)}, u32[]{:S(2)}, u32[]{:S(2)}) collective-permute-start(bf16[1024,128]{1,0:T(8,128)(2,1)} %get-tuple-element.49), channel_id=1, source_target_pairs={{0,3},{1,0},{2,1},{3,2},{4,7},{5,4},{6,5},{7,6},{8,11},{9,8},{10,9... | collective-permute-start | bytes 786440 | tf_op jit(solution)/shard_map/ppermute | solution.py:557
  58.3 5.1 %collective-permute-done.4.wr = bf16[1024,128]{1,0:T(8,128)(2,1)} collective-permute-done((bf16[1024,128]{1,0:T(8,128)(2,1)}, bf16[1024,128]{1,0:T(8,128)(2,1)}, u32[]{:S(2)}, u32[]{:S(2)}) %collective-permute-start.4) | collective-permute-done | bytes 262176 | tf_op jit(solution)/shard_map/ppermute | solution.py:557
  63.4 1.2 collective-permute-done.5.wl
  64.6 3.6 %gather_own.1.h0 = bf16[1024,128]{1,0:T(8,128)(2,1)} custom-call(s32[1]{0:T(128)} %bitcast.8.place, s32[4096]{0:T(1024)} %src_in.3, f32[4096,128]{1,0:T(8,128)} %table.7), custom_call_target="tpu_custom_call" | custom-call | flops 3000000000 | bytes 3000000 | tf_op jit(solution)/shard_map/gather_own/pallas_call | solution.py:224
  68.2 3.0 %collective-permute-done.6.dr = bf16[1024,128]{1,0:T(8,128)(2,1)} collective-permute-done((bf16[1024,128]{1,0:T(8,128)(2,1)}, bf16[1024,128]{1,0:T(8,128)(2,1)}, u32[]{:S(2)}, u32[]{:S(2)}) %collective-permute-start.6) | collective-permute-done | bytes 262176 | tf_op jit(solution)/shard_map/ppermute | solution.py:557
  71.2 0.9 collective-permute-done.7.dl
  72.1 2.9 %all-to-all-done.1 = bf16[256,16,128]{2,1,0:T(8,128)(2,1)} async-done(((bf16[256,16,128]{2,1,0:T(8,128)(2,1)}), bf16[256,16,128]{2,1,0:T(8,128)(2,1)}, u32[]{:S(2)}, u32[]{:S(2)}) %all-to-all-start.1) | async-done | bytes 1048608 | tf_op jit(solution)/shard_map/all_to_all | solution.py:568
  75.0 7.2 %edge_scores.1 = (bf16[64,4,16,128]{3,2,1,0:T(8,128)(2,1)}, bf16[2048,128]{1,0:T(8,128)(2,1)}, bf16[3072,128]{1,0:T(8,128)(2,1)}, bf16[3072,128]{1,0:T(8,128)(2,1)}) custom-call(s32[1,128]{1,0:T(1,128)} %concatenate.3.settings_in, bf16[64,4,16,128]{3,2,1,0:T(8,128)(2,1)} %bitcast.7.weighted_in, bf16[1024,128]{1,0:T(8,128)(2,1)} %gather_own.1.h0, ...), custom_call_target="tpu_custom_call" | custom-call | flops 3200000000 | bytes 8000000 | tf_op jit(solution)/shard_map/edge_scores/pallas_call | solution.py:333
  82.2 1.5 %collective-permute-start.8 = (bf16[3072,128]{1,0:T(8,128)(2,1)}, bf16[3072,128]{1,0:T(8,128)(2,1)}, u32[]{:S(2)}, u32[]{:S(2)}) collective-permute-start(bf16[3072,128]{1,0:T(8,128)(2,1)} %get-tuple-element.54), channel_id=1, source_target_pairs={{0,3},{1,0},{2,1},{3,2},{4,7},{5,4},{6,5},{7,6},{8,11},{9,8},{10,9... | collective-permute-start | bytes 2359304 | tf_op jit(solution)/shard_map/ppermute | solution.py:557
  83.7 0.6 collective-permute-start.9
  84.3 10.9 %all-to-all-start.2 = ((bf16[256,16,128]{2,1,0:T(8,128)(2,1)}), bf16[256,16,128]{2,1,0:T(8,128)(2,1)}, u32[]{:S(2)}, u32[]{:S(2)}) async-start(bf16[256,16,128]{2,1,0:T(8,128)(2,1)} %bitcast.19), calls=%async_computation.2 | async-start | bytes 2097152 | tf_op jit(solution)/shard_map/all_to_all | solution.py:568
  95.2 0.7 reshape.40.wanted_in
  95.9 9.7 %collective-permute-done.8.g1 = bf16[3072,128]{1,0:T(8,128)(2,1)} collective-permute-done((bf16[3072,128]{1,0:T(8,128)(2,1)}, bf16[3072,128]{1,0:T(8,128)(2,1)}, u32[]{:S(2)}, u32[]{:S(2)}) %collective-permute-start.8) | collective-permute-done | bytes 786464 | tf_op jit(solution)/shard_map/ppermute | solution.py:557
  105.6 2.8 %collective-permute-done.9.g3 = bf16[3072,128]{1,0:T(8,128)(2,1)} collective-permute-done((bf16[3072,128]{1,0:T(8,128)(2,1)}, bf16[3072,128]{1,0:T(8,128)(2,1)}, u32[]{:S(2)}, u32[]{:S(2)}) %collective-permute-start.9) | collective-permute-done | bytes 786464 | tf_op jit(solution)/shard_map/ppermute | solution.py:557
  108.4 1.9 %pass_on.1 = (bf16[1024,128]{1,0:T(8,128)(2,1)}, bf16[1024,128]{1,0:T(8,128)(2,1)}) custom-call(bf16[3072,128]{1,0:T(8,128)(2,1)} %collective-permute-done.8.g1, bf16[3072,128]{1,0:T(8,128)(2,1)} %collective-permute-done.9.g3), custom_call_target="tpu_custom_call" | custom-call | bytes 1000000 | tf_op jit(solution)/shard_map/pass_on/pallas_call | solution.py:546
  110.3 0.1 collective-permute-start.10
  110.4 2.0 %collective-permute-start.11 = (bf16[1024,128]{1,0:T(8,128)(2,1)}, bf16[1024,128]{1,0:T(8,128)(2,1)}, u32[]{:S(2)}, u32[]{:S(2)}) collective-permute-start(bf16[1024,128]{1,0:T(8,128)(2,1)} %get-tuple-element.57), channel_id=1, source_target_pairs={{0,3},{1,0},{2,1},{3,2},{4,7},{5,4},{6,5},{7,6},{8,11},{9,8},{10,9... | collective-permute-start | bytes 786440 | tf_op jit(solution)/shard_map/ppermute | solution.py:557
  112.4 6.4 %scatter_near.1.start = f32[4096,128]{1,0:T(8,128)} custom-call(s32[1,128]{1,0:T(1,128)} %concatenate.3.settings_in, s32[4096]{0:T(1024)} %src_in.3, bf16[2048,128]{1,0:T(8,128)(2,1)} %get-tuple-element.53.g0, bf16[3072,128]{1,0:T(8,128)(2,1)} %collective-permute-done.8.g1, bf16[3072,128]{1,0:T(8,128)(2,1)} %collective-permute-done.9.g3), custom_call_target="tpu_custom_call" | custom-call | flops 10000000000 | bytes 20000000 | tf_op jit(solution)/shard_map/scatter_near/pallas_call | solution.py:391
  118.8 1.0 collective-permute-done.10.wr
  119.8 0.7 collective-permute-done.11.wl
  120.4 6.3 %scatter_far.1.start = f32[4096,128]{1,0:T(8,128)} custom-call(s32[1,128]{1,0:T(1,128)} %concatenate.3.settings_in, s32[4096]{0:T(1024)} %src_in.3, s32[1000]{0:T(1024)} %neg_in.1, f32[4096,128]{1,0:T(8,128)} %scatter_near.1.start, bf16[2048,128]{1,0:T(8,128)(2,1)} %get-tuple-element.53.g0, bf16[3072,128]{1,0:T(8,128)(2,1)} %collective-permute-done.8.g1, ...), custom_call_target="tpu_custom_call" | custom-call | flops 10000000000 | bytes 20000000 | tf_op jit(solution)/shard_map/scatter_far/pallas_call | solution.py:446
  126.7 7.1 %scatter_tails.1 = (f32[4096,128]{1,0:T(8,128)}, f32[32,128]{1,0:T(8,128)}) custom-call(s32[4096]{0:T(1024)} %reshape.40.wanted_in, f32[4096,128]{1,0:T(8,128)} %scatter_far.1.start, f32[4096,128]{1,0:T(8,128)} %get-tuple-element.58.factors, bf16[4096,128]{1,0:T(8,128)(2,1)} %bitcast.10.pulled), custom_call_target="tpu_custom_call" | custom-call | bytes 30000000 | tf_op jit(solution)/shard_map/scatter_tails/pallas_call | solution.py:505
  133.9 1.6 %collective-permute-start.14 = (f32[32,128]{1,0:T(8,128)}, f32[32,128]{1,0:T(8,128)S(1)}, u32[]{:S(2)}, u32[]{:S(2)}) collective-permute-start(f32[32,128]{1,0:T(8,128)} %get-tuple-element.63), channel_id=1, source_target_pairs={{0,3},{1,0},{2,1},{3,2},{4,7},{5,4},{6,5},{7,6},{8,11},{9,8},{10,9... | collective-permute-start | bytes 49160 | tf_op jit(solution)/shard_map/ppermute | solution.py:557
  135.4 0.5 collective-permute-start.13
  136.0 3.5 %collective-permute-start.12 = (f32[32,128]{1,0:T(8,128)}, f32[32,128]{1,0:T(8,128)S(1)}, u32[]{:S(2)}, u32[]{:S(2)}) collective-permute-start(f32[32,128]{1,0:T(8,128)} %get-tuple-element.63), channel_id=1, source_target_pairs={{0,2},{1,3},{2,0},{3,1},{4,6},{5,7},{6,4},{7,5},{8,10},{9,11},{10,... | collective-permute-start | bytes 49160 | tf_op jit(solution)/shard_map/ppermute | solution.py:557
  139.5 1.6 %copy-done = f32[4096,128]{1,0:T(8,128)S(1)} copy-done((f32[4096,128]{1,0:T(8,128)S(1)}, f32[4096,128]{1,0:T(8,128)}, u32[]{:S(2)}) %copy-start) | copy-done | bytes 2097176
  141.1 1.6 %copy-done.1 = f32[4096,128]{1,0:T(8,128)S(1)} copy-done((f32[4096,128]{1,0:T(8,128)S(1)}, f32[4096,128]{1,0:T(8,128)}, u32[]{:S(2)}) %copy-start.1) | copy-done | bytes 2097176
  142.7 0.3 stage.1
  143.0 0.4 copy-done.2
  143.4 0.0 copy-done.3
  143.4 0.6 fusion
  144.0 1.7 %divide_subtract_fusion = f32[4096,128]{1,0:T(8,128)} fusion(f32[4096,128]{1,0:T(8,128)S(1)} %get-tuple-element.61, f32[4096,128]{1,0:T(8,128)S(1)} %get-tuple-element.62, f32[4096]{0:T(1024)S(1)} %get-tuple-element.64), kind=kLoop, calls=%fused_computation | loop fusion | flops 1048576 | bytes 6307840 | tf_op jit(solution)/shard_map/sub | solution.py:602
  (15 shorter events, 0.0 us)
Async XLA Ops:
  2.1 21.4 %all-to-all-start = ((s32[64,1,128]{2,1,0:T(1,128)}), s32[64,1,128]{2,1,0:T(1,128)S(1)}, u32[]{:S(2)}, u32[]{:S(2)}) async-start(s32[64,1,128]{2,1,0:T(1,128)} %bitcast.20), calls=%async_computation | async-start | bytes 65536 | tf_op jit(solution)/shard_map/all_to_all | solution.py:573
  18.7 25.9 %collective-permute-start = (bf16[1024,128]{1,0:T(8,128)(2,1)}, bf16[1024,128]{1,0:T(8,128)(2,1)}, u32[]{:S(2)}, u32[]{:S(2)}) collective-permute-start(bf16[1024,128]{1,0:T(8,128)(2,1)} %get-tuple-element.38), channel_id=1, source_target_pairs={{0,1},{1,2},{2,3},{3,0},{4,5},{5,6},{6,7},{7,4},{8,9},{9,10},{10,1... | collective-permute-start | bytes 786440 | tf_op jit(solution)/shard_map/ppermute | solution.py:557
  20.4 24.3 %collective-permute-start.1 = (bf16[1024,128]{1,0:T(8,128)(2,1)}, bf16[1024,128]{1,0:T(8,128)(2,1)}, u32[]{:S(2)}, u32[]{:S(2)}) collective-permute-start(bf16[1024,128]{1,0:T(8,128)(2,1)} %get-tuple-element.39), channel_id=1, source_target_pairs={{0,3},{1,0},{2,1},{3,2},{4,7},{5,4},{6,5},{7,6},{8,11},{9,8},{10,9... | collective-permute-start | bytes 786440 | tf_op jit(solution)/shard_map/ppermute | solution.py:557
  32.6 11.4 %copy-start.5 = (s32[1,64]{1,0:T(1,128)S(1)}, s32[1,64]{1,0:T(1,128)}, u32[]{:S(2)}) copy-start(s32[1,64]{1,0:T(1,128)} %param.14) | copy-start | bytes 772
  32.6 13.5 %copy-start.4 = (bf16[512,128]{1,0:T(8,128)(2,1)S(1)}, bf16[512,128]{1,0:T(8,128)(2,1)}, u32[]{:S(2)}) copy-start(bf16[512,128]{1,0:T(8,128)(2,1)} %get-tuple-element.41) | copy-start | bytes 393220
  32.6 42.4 %all-to-all-start.1 = ((bf16[256,16,128]{2,1,0:T(8,128)(2,1)}), bf16[256,16,128]{2,1,0:T(8,128)(2,1)}, u32[]{:S(2)}, u32[]{:S(2)}) async-start(bf16[256,16,128]{2,1,0:T(8,128)(2,1)} %bitcast.18), calls=%async_computation.1 | async-start | bytes 2097152 | tf_op jit(solution)/shard_map/all_to_all | solution.py:568
  44.7 10.2 %collective-permute-start.2 = (bf16[512,128]{1,0:T(8,128)(2,1)}, bf16[512,128]{1,0:T(8,128)(2,1)}, u32[]{:S(2)}, u32[]{:S(2)}) collective-permute-start(bf16[512,128]{1,0:T(8,128)(2,1)} %get-tuple-element.40), channel_id=1, source_target_pairs={{0,1},{1,2},{2,3},{3,0},{4,5},{5,6},{6,7},{7,4},{8,9},{9,10},{10,1... | collective-permute-start | bytes 393224 | tf_op jit(solution)/shard_map/ppermute | solution.py:557
  46.1 12.2 %collective-permute-start.3 = (bf16[512,128]{1,0:T(8,128)(2,1)S(1)}, bf16[512,128]{1,0:T(8,128)(2,1)}, u32[]{:S(2)}, u32[]{:S(2)}) collective-permute-start(bf16[512,128]{1,0:T(8,128)(2,1)S(1)} %copy-done.4), channel_id=1, source_target_pairs={{0,3},{1,0},{2,1},{3,2},{4,7},{5,4},{6,5},{7,6},{8,11},{9,8},{10,9... | collective-permute-start | bytes 393224 | tf_op jit(solution)/shard_map/ppermute | solution.py:557
  47.0 16.4 %collective-permute-start.4 = (bf16[1024,128]{1,0:T(8,128)(2,1)}, bf16[1024,128]{1,0:T(8,128)(2,1)}, u32[]{:S(2)}, u32[]{:S(2)}) collective-permute-start(bf16[1024,128]{1,0:T(8,128)(2,1)} %collective-permute-done.vr), channel_id=1, source_target_pairs={{0,1},{1,2},{2,3},{3,0},{4,5},{5,6},{6,7},{7,4},{8,9},{9,10},{10,1... | collective-permute-start | bytes 786440 | tf_op jit(solution)/shard_map/ppermute | solution.py:557
  48.2 16.4 %collective-permute-start.5 = (bf16[1024,128]{1,0:T(8,128)(2,1)}, bf16[1024,128]{1,0:T(8,128)(2,1)}, u32[]{:S(2)}, u32[]{:S(2)}) collective-permute-start(bf16[1024,128]{1,0:T(8,128)(2,1)} %collective-permute-done.1.vl), channel_id=1, source_target_pairs={{0,3},{1,0},{2,1},{3,2},{4,7},{5,4},{6,5},{7,6},{8,11},{9,8},{10,9... | collective-permute-start | bytes 786440 | tf_op jit(solution)/shard_map/ppermute | solution.py:557
  54.7 16.5 %collective-permute-start.6 = (bf16[1024,128]{1,0:T(8,128)(2,1)}, bf16[1024,128]{1,0:T(8,128)(2,1)}, u32[]{:S(2)}, u32[]{:S(2)}) collective-permute-start(bf16[1024,128]{1,0:T(8,128)(2,1)} %get-tuple-element.47), channel_id=1, source_target_pairs={{0,1},{1,2},{2,3},{3,0},{4,5},{5,6},{6,7},{7,4},{8,9},{9,10},{10,1... | collective-permute-start | bytes 786440 | tf_op jit(solution)/shard_map/ppermute | solution.py:557
  54.8 17.3 %collective-permute-start.7 = (bf16[1024,128]{1,0:T(8,128)(2,1)}, bf16[1024,128]{1,0:T(8,128)(2,1)}, u32[]{:S(2)}, u32[]{:S(2)}) collective-permute-start(bf16[1024,128]{1,0:T(8,128)(2,1)} %get-tuple-element.49), channel_id=1, source_target_pairs={{0,3},{1,0},{2,1},{3,2},{4,7},{5,4},{6,5},{7,6},{8,11},{9,8},{10,9... | collective-permute-start | bytes 786440 | tf_op jit(solution)/shard_map/ppermute | solution.py:557
  82.2 23.4 %collective-permute-start.8 = (bf16[3072,128]{1,0:T(8,128)(2,1)}, bf16[3072,128]{1,0:T(8,128)(2,1)}, u32[]{:S(2)}, u32[]{:S(2)}) collective-permute-start(bf16[3072,128]{1,0:T(8,128)(2,1)} %get-tuple-element.54), channel_id=1, source_target_pairs={{0,3},{1,0},{2,1},{3,2},{4,7},{5,4},{6,5},{7,6},{8,11},{9,8},{10,9... | collective-permute-start | bytes 2359304 | tf_op jit(solution)/shard_map/ppermute | solution.py:557
  83.7 24.7 %collective-permute-start.9 = (bf16[3072,128]{1,0:T(8,128)(2,1)}, bf16[3072,128]{1,0:T(8,128)(2,1)}, u32[]{:S(2)}, u32[]{:S(2)}) collective-permute-start(bf16[3072,128]{1,0:T(8,128)(2,1)} %get-tuple-element.55), channel_id=1, source_target_pairs={{0,1},{1,2},{2,3},{3,0},{4,5},{5,6},{6,7},{7,4},{8,9},{9,10},{10,1... | collective-permute-start | bytes 2359304 | tf_op jit(solution)/shard_map/ppermute | solution.py:557
  84.3 42.4 %all-to-all-start.2 = ((bf16[256,16,128]{2,1,0:T(8,128)(2,1)}), bf16[256,16,128]{2,1,0:T(8,128)(2,1)}, u32[]{:S(2)}, u32[]{:S(2)}) async-start(bf16[256,16,128]{2,1,0:T(8,128)(2,1)} %bitcast.19), calls=%async_computation.2 | async-start | bytes 2097152 | tf_op jit(solution)/shard_map/all_to_all | solution.py:568
  110.3 9.5 %collective-permute-start.10 = (bf16[1024,128]{1,0:T(8,128)(2,1)}, bf16[1024,128]{1,0:T(8,128)(2,1)}, u32[]{:S(2)}, u32[]{:S(2)}) collective-permute-start(bf16[1024,128]{1,0:T(8,128)(2,1)} %get-tuple-element.56), channel_id=1, source_target_pairs={{0,1},{1,2},{2,3},{3,0},{4,5},{5,6},{6,7},{7,4},{8,9},{9,10},{10,1... | collective-permute-start | bytes 786440 | tf_op jit(solution)/shard_map/ppermute | solution.py:557
  110.4 10.1 %collective-permute-start.11 = (bf16[1024,128]{1,0:T(8,128)(2,1)}, bf16[1024,128]{1,0:T(8,128)(2,1)}, u32[]{:S(2)}, u32[]{:S(2)}) collective-permute-start(bf16[1024,128]{1,0:T(8,128)(2,1)} %get-tuple-element.57), channel_id=1, source_target_pairs={{0,3},{1,0},{2,1},{3,2},{4,7},{5,4},{6,5},{7,6},{8,11},{9,8},{10,9... | collective-permute-start | bytes 786440 | tf_op jit(solution)/shard_map/ppermute | solution.py:557
  133.9 9.1 %collective-permute-start.14 = (f32[32,128]{1,0:T(8,128)}, f32[32,128]{1,0:T(8,128)S(1)}, u32[]{:S(2)}, u32[]{:S(2)}) collective-permute-start(f32[32,128]{1,0:T(8,128)} %get-tuple-element.63), channel_id=1, source_target_pairs={{0,3},{1,0},{2,1},{3,2},{4,7},{5,4},{6,5},{7,6},{8,11},{9,8},{10,9... | collective-permute-start | bytes 49160 | tf_op jit(solution)/shard_map/ppermute | solution.py:557
  135.4 7.6 %collective-permute-start.13 = (f32[32,128]{1,0:T(8,128)}, f32[32,128]{1,0:T(8,128)S(1)}, u32[]{:S(2)}, u32[]{:S(2)}) collective-permute-start(f32[32,128]{1,0:T(8,128)} %get-tuple-element.63), channel_id=1, source_target_pairs={{0,1},{1,2},{2,3},{3,0},{4,5},{5,6},{6,7},{7,4},{8,9},{9,10},{10,1... | collective-permute-start | bytes 49160 | tf_op jit(solution)/shard_map/ppermute | solution.py:557
  136.0 7.1 %collective-permute-start.12 = (f32[32,128]{1,0:T(8,128)}, f32[32,128]{1,0:T(8,128)S(1)}, u32[]{:S(2)}, u32[]{:S(2)}) collective-permute-start(f32[32,128]{1,0:T(8,128)} %get-tuple-element.63), channel_id=1, source_target_pairs={{0,2},{1,3},{2,0},{3,1},{4,6},{5,7},{6,4},{7,5},{8,10},{9,11},{10,... | collective-permute-start | bytes 49160 | tf_op jit(solution)/shard_map/ppermute | solution.py:557
  139.5 1.6 %copy-start = (f32[4096,128]{1,0:T(8,128)S(1)}, f32[4096,128]{1,0:T(8,128)}, u32[]{:S(2)}) copy-start(f32[4096,128]{1,0:T(8,128)} %table.7) | copy-start | bytes 6291460
  141.1 1.6 %copy-start.1 = (f32[4096,128]{1,0:T(8,128)S(1)}, f32[4096,128]{1,0:T(8,128)}, u32[]{:S(2)}) copy-start(f32[4096,128]{1,0:T(8,128)} %get-tuple-element.60.gradient) | copy-start | bytes 6291460
  142.7 0.7 copy-start.2
  142.7 0.7 copy-start.3
